TPU v7x, 32 devices: a whole 2x2x4 slice. The times are simulated.
32 devices in a mesh: chan: 4 (over x, core), sym: 4 (over z), sub: 2 (over y).
Axes of the slice: x: 2, y: 2, z: 4, core: 2. Of those that a mesh axis runs over, the one named last changes fastest.
Arguments:
- samples: float32 [2, 64, 24, 9216], P(None, ('chan', 'sub'), 'sym'), parts along dimension 1, may hold values from -16 to 16
- constellation_index: int32 [96, 4096], P(('chan', 'sym'), 'sub'), parts along dimension 0, may hold values from 0 to 63, as said below
- pilot_offsets: int32 [24], P('sym'), may hold values from 0 to 11
- cp_offset: int32 [96], P(('chan', 'sym')), parts along dimension 0, may hold values from 0 to 1024, as said below
Outputs:
- caf: float32 [2, 64, 24, 1024], P(None, 'chan', 'sym', 'sub'), parts along dimension 1
There are 4 independent parts, one for each index of `chan`. A program takes and returns all parts, laid end to end along the dimension named above; an argument that names none is the same for every part. Nothing has to cross between parts.
Inputs may be any that keep to these rules, and one draw needn't show every extreme that they name: Symbol m's scattered pilots sit on the active subcarriers k with k mod 12 == pilot_offsets[m]. The transform window of symbol m is samples cp_offset[m] to cp_offset[m] + 64 * 128 - 1 of its record. `constellation_index`: the index's low three bits give the in-phase level, the high three the quadrature level.
All inputs are finite; a program needn't handle non-finite values.
Results may differ from a plain program's by a relative error of at most 0.0003.
Values may be sent and summed in bfloat16 or wider, within the bound.
No kernel may reach another device: no remote copies, remote signals or barrier semaphores. Data moves between devices by JAX's collectives and lax.ppermute only.
A program may use at most 64 MiB of HBM per device.

v0:
```python
import math

import jax
import jax.numpy as jnp
from jax import lax
from jax.sharding import PartitionSpec as P

OUTER_FACTOR = 64
INNER_FACTOR = 128
ACTIVE_TONES = 4096
GUARD_SAMPLES = 1024
SMOOTH_HALFSPAN = 48
PSP = 12


TWO_PI = 2.0 * math.pi
ROOT_FORTYTWO = math.sqrt(42.0)
HIGHEST = lax.Precision.HIGHEST


def lookup_tables(numerator, period):
    angle = TWO_PI / period * (numerator % period).astype(jnp.float32)
    return (jnp.cos(angle), jnp.sin(angle))


def cut_windows(samples, cp_offset, length):

    def one_symbol(record, offset):
        return lax.dynamic_slice_in_dim(record, offset, length, axis=2)

    return jax.vmap(one_symbol, in_axes=(2, 0), out_axes=2)(samples, cp_offset)


def slice_spectrum(symbol_windows, first_len, second_len, band_slice):
    lead = symbol_windows.shape[1:3]
    whole = first_len * second_len
    real_part = symbol_windows[0].reshape(-1, first_len, second_len)
    imag_part = symbol_windows[1].reshape(-1, first_len, second_len)
    index_a = jnp.arange(first_len, dtype=jnp.int32)
    index_b = jnp.arange(second_len, dtype=jnp.int32)
    cos_one, sin_one = lookup_tables(index_a[:, None] * index_a[None, :], first_len)
    section_re = jnp.einsum("ka,nab->nkb", cos_one, real_part, precision=HIGHEST) + jnp.einsum(
        "ka,nab->nkb", sin_one, imag_part, precision=HIGHEST
    )
    section_im = jnp.einsum("ka,nab->nkb", cos_one, imag_part, precision=HIGHEST) - jnp.einsum(
        "ka,nab->nkb", sin_one, real_part, precision=HIGHEST
    )
    cos_two, sin_two = lookup_tables(index_a[:, None] * index_b[None, :], whole)
    twist_re = section_re * cos_two + section_im * sin_two
    twist_im = section_im * cos_two - section_re * sin_two
    lowest = (whole - band_slice) // 2 // first_len
    index_j = lowest + jnp.arange(band_slice // first_len, dtype=jnp.int32)
    cos_three, sin_three = lookup_tables(index_j[:, None] * index_b[None, :], second_len)
    out_re = jnp.einsum("nkb,jb->njk", twist_re, cos_three, precision=HIGHEST) + jnp.einsum(
        "nkb,jb->njk", twist_im, sin_three, precision=HIGHEST
    )
    out_im = jnp.einsum("nkb,jb->njk", twist_im, cos_three, precision=HIGHEST) - jnp.einsum(
        "nkb,jb->njk", twist_re, sin_three, precision=HIGHEST
    )
    stacked = jnp.stack([out_re, out_im]) * (1.0 / math.sqrt(whole))
    return stacked.reshape((2,) + lead + (band_slice,))


def smooth(zero_padded, window_width, radius):
    block_piece = 512
    blocks = window_width // block_piece
    pieces = jnp.stack(
        [
            zero_padded[
                ..., step_body * block_piece : step_body * block_piece + block_piece + 2 * radius
            ]
            for step_body in range(blocks)
        ],
        axis=-2,
    )
    taps = (
        jnp.arange(block_piece + 2 * radius, dtype=jnp.int32)[:, None]
        - radius
        - jnp.arange(block_piece, dtype=jnp.int32)[None, :]
    )
    weights = jnp.maximum(radius + 1 - jnp.abs(taps), 0).astype(jnp.float32)
    smoothed = jnp.einsum("...nj,jo->...no", pieces, weights, precision=HIGHEST)
    return smoothed.reshape(zero_padded.shape[:-1] + (window_width,))


def purify_tones(
    spectrum_rows,
    level_real,
    level_imaginary,
    pilot_offsets,
    first_factor,
    window_width,
    extend_edges,
):
    factor = ROOT_FORTYTWO / (level_real * level_real + level_imaginary * level_imaginary)
    ratio_re = (spectrum_rows[0] * level_real + spectrum_rows[1] * level_imaginary) * factor
    ratio_im = (spectrum_rows[1] * level_real - spectrum_rows[0] * level_imaginary) * factor
    ratio = jnp.stack([ratio_re, ratio_im])
    positions = (
        first_factor
        - SMOOTH_HALFSPAN
        + jnp.arange(window_width + 2 * SMOOTH_HALFSPAN, dtype=jnp.int32)
    )
    inside_mask = (positions >= 0) & (positions < ACTIVE_TONES)
    pilot = (inside_mask[None, :] & (positions[None, :] % PSP == pilot_offsets[:, None])).astype(
        jnp.float32
    )
    picked = ratio * pilot[:, SMOOTH_HALFSPAN : SMOOTH_HALFSPAN + window_width]
    numerator = smooth(extend_edges(picked), window_width, SMOOTH_HALFSPAN)
    denominator = smooth(pilot, window_width, SMOOTH_HALFSPAN)
    return ratio - numerator / denominator


def local(samples, constellation_index, pilot_offsets, cp_offset):
    symbol_windows = cut_windows(samples, cp_offset, OUTER_FACTOR * INNER_FACTOR)
    spectrum_rows = slice_spectrum(symbol_windows, OUTER_FACTOR, INNER_FACTOR, ACTIVE_TONES)
    sym_count = lax.axis_size("sym")
    symbol_local = samples.shape[2]
    range_normalizer = 1.0 / math.sqrt(ACTIVE_TONES)
    level_real = (2 * (constellation_index % 8) - 7).astype(jnp.float32)
    level_imaginary = (2 * (constellation_index // 8) - 7).astype(jnp.float32)
    turned = None
    gathered_re, gathered_im = (
        lax.all_gather(level_real.astype(jnp.bfloat16), "sub", axis=1, tiled=True),
        lax.all_gather(level_imaginary.astype(jnp.bfloat16), "sub", axis=1, tiled=True),
    )

    def pad_zero(values):
        return jnp.pad(values, ((0, 0), (0, 0), (0, 0), (SMOOTH_HALFSPAN, SMOOTH_HALFSPAN)))

    purified = purify_tones(
        spectrum_rows,
        gathered_re.astype(jnp.float32),
        gathered_im.astype(jnp.float32),
        pilot_offsets,
        0,
        ACTIVE_TONES,
        pad_zero,
    )
    local_channel_estimates = spectrum_rows.shape[1]
    flattened = purified.reshape(2, local_channel_estimates * symbol_local, ACTIVE_TONES)
    block_piece = 512
    delay_lags = jnp.arange(GUARD_SAMPLES, dtype=jnp.int32)

    def accumulate_block(step_body, running):
        part = lax.dynamic_slice_in_dim(flattened, step_body * block_piece, block_piece, 2)
        tone_indices = step_body * block_piece + jnp.arange(block_piece, dtype=jnp.int32)
        cosine_factor, sine_factor = lookup_tables(
            tone_indices[:, None] * delay_lags[None, :], ACTIVE_TONES
        )
        real_out = jnp.einsum("bk,kt->bt", part[0], cosine_factor, precision=HIGHEST) - jnp.einsum(
            "bk,kt->bt", part[1], sine_factor, precision=HIGHEST
        )
        imag_out = jnp.einsum("bk,kt->bt", part[0], sine_factor, precision=HIGHEST) + jnp.einsum(
            "bk,kt->bt", part[1], cosine_factor, precision=HIGHEST
        )
        return running + jnp.stack([real_out, imag_out])

    initial_value = jnp.zeros(
        (2, local_channel_estimates * symbol_local, GUARD_SAMPLES), jnp.float32
    )
    summed_total = (
        lax.fori_loop(0, ACTIVE_TONES // block_piece, accumulate_block, initial_value)
        * range_normalizer
    )
    own_profiles = summed_total.reshape(2, local_channel_estimates, symbol_local, GUARD_SAMPLES)
    profiles = None
    profiles = lax.all_to_all(own_profiles, "sub", split_axis=3, concat_axis=1, tiled=True)
    symbols = sym_count * symbol_local
    doppler_norm = 1.0 / math.sqrt(symbols)
    turned = lax.all_to_all(profiles, "sym", split_axis=3, concat_axis=2, tiled=True)
    symbol_ids = jnp.arange(symbols, dtype=jnp.int32)
    cosine_factor, sine_factor = lookup_tables(symbol_ids[:, None] * symbol_ids[None, :], symbols)
    real_out = jnp.einsum("fm,cmq->cfq", cosine_factor, turned[0], precision=HIGHEST) + jnp.einsum(
        "fm,cmq->cfq", sine_factor, turned[1], precision=HIGHEST
    )
    imag_out = jnp.einsum("fm,cmq->cfq", cosine_factor, turned[1], precision=HIGHEST) - jnp.einsum(
        "fm,cmq->cfq", sine_factor, turned[0], precision=HIGHEST
    )
    spread = jnp.stack([real_out, imag_out]) * doppler_norm
    caf = lax.all_to_all(spread, "sym", split_axis=2, concat_axis=3, tiled=True)
    return caf


def solution(mesh):
    return jax.shard_map(
        local,
        mesh=mesh,
        in_specs=(
            P(None, ("chan", "sub"), "sym", None),
            P(("chan", "sym"), "sub"),
            P("sym"),
            P(("chan", "sym")),
        ),
        out_specs=P(None, "chan", "sym", "sub"),
        check_vma=False,
    )
```

profile of v0, /device:TPU:0, one launch (start us, length us, event | category | flops | bytes accessed | tf_op | source)
XLA Modules:
  0.0 508.3 jit_solution(3174878857204853326)
XLA Ops:
  3.1 16.8 %while.17 = (s32[]{:T(128)}, f32[6,2,8,9216]{3,2,1,0:T(8,128)S(1)}, s32[6,4]{0,1:T(4,128)S(1)}, f32[6,2,8,8192]{3,2,1,0:T(8,128)}, s32[]{:T(128)}) while((s32[]{:T(128)}, f32[6,2,8,9216]{3,2,1,0:T(8,128)S(1)}, s32[6,4]{0,1:T(4,128)S(1)}, f32[6,2,8,8192]{3,2,1,0:T(8,128)}, s32[]{:T(128)}) %tuple.81), condition=%wide.while_cond, body=%wide.while_body.sunk | while | flops 2 | bytes 1050225 | solution.py:29
  111.9 302.9 %while.18 = (s32[]{:T(128)}, f32[2,48,1024]{2,1,0:T(8,128)S(1)}, f32[2,48,4096]{2,1,0:T(8,128)S(1)}, s32[]{:T(128)}, s32[]{:T(128)}, /*index=5*/s32[]{:T(128)}, s32[]{:T(128)}, s32[]{}) while((s32[]{:T(128)}, f32[2,48,1024]{2,1,0:T(8,128)S(1)}, f32[2,48,4096]{2,1,0:T(8,128)S(1)}, s32[]{:T(128)}, s32[]{:T(128)}, ...), condition=%wide.region_1.2_spmd.clone, body=%wide.region_0.1_spmd.clone.sunk | while | flops 1237713408 | bytes 2762933 | solution.py:163
  112.3 9.0 %fusion.229 = f32[48,1024]{1,0:T(8,128)S(1)} fusion(s32[512]{0:T(512)S(1)} %iota_add_fusion.5, f32[2,48,4096]{2,1,0:T(8,128)S(1)} %get-tuple-element.266, s32[]{:T(128)S(6)} %select_n.234), kind=kOutput, calls=%fused_computation.19.clone.1 | convolution fusion | flops 309329920 | bytes 296964 | tf_op jit(solution)/shard_map/while/body/eval_jaxpr/bk,kt->bt/dot_general | solution.py:151
  121.3 9.3 %fusion.230 = f32[1,48,1024]{2,1,0:T(8,128)S(1)} fusion(f32[48,1024]{1,0:T(8,128)S(1)} %fusion.229, s32[512]{0:T(512)S(1)} %iota_add_fusion.5, f32[2,48,4096]{2,1,0:T(8,128)S(1)} %get-tuple-element.266, s32[]{:T(128)S(6)} %add.439, s32[]{:T(128)S(6)} %select_n.234), kind=kOutput, calls=%fused_computation.16.clone.1 | convolution fusion | flops 309379072 | bytes 493576 | tf_op jit(solution)/shard_map/while/body/eval_jaxpr/bk,kt->bt/dot_general | solution.py:151
  130.6 9.5 %fusion.227 = f32[48,1024]{1,0:T(8,128)S(1)} fusion(s32[512]{0:T(512)S(1)} %iota_add_fusion.5, f32[2,48,4096]{2,1,0:T(8,128)S(1)} %get-tuple-element.266, s32[]{:T(128)S(6)} %select_n.234), kind=kOutput, calls=%fused_computation.20.clone.1 | convolution fusion | flops 309329920 | bytes 296964 | tf_op jit(solution)/shard_map/while/body/eval_jaxpr/bk,kt->bt/dot_general | solution.py:154
  158.6 9.5 %fusion.230 = f32[1,48,1024]{2,1,0:T(8,128)S(1)} fusion(f32[48,1024]{1,0:T(8,128)S(1)} %fusion.229, s32[512]{0:T(512)S(1)} %iota_add_fusion.5, f32[2,48,4096]{2,1,0:T(8,128)S(1)} %get-tuple-element.266, s32[]{:T(128)S(6)} %add.439, s32[]{:T(128)S(6)} %select_n.234), kind=kOutput, calls=%fused_computation.16.clone.1 | convolution fusion | flops 309379072 | bytes 493576 | tf_op jit(solution)/shard_map/while/body/eval_jaxpr/bk,kt->bt/dot_general | solution.py:151
  168.1 9.3 %fusion.227 = f32[48,1024]{1,0:T(8,128)S(1)} fusion(s32[512]{0:T(512)S(1)} %iota_add_fusion.5, f32[2,48,4096]{2,1,0:T(8,128)S(1)} %get-tuple-element.266, s32[]{:T(128)S(6)} %select_n.234), kind=kOutput, calls=%fused_computation.20.clone.1 | convolution fusion | flops 309329920 | bytes 296964 | tf_op jit(solution)/shard_map/while/body/eval_jaxpr/bk,kt->bt/dot_general | solution.py:154
  196.1 9.3 %fusion.230 = f32[1,48,1024]{2,1,0:T(8,128)S(1)} fusion(f32[48,1024]{1,0:T(8,128)S(1)} %fusion.229, s32[512]{0:T(512)S(1)} %iota_add_fusion.5, f32[2,48,4096]{2,1,0:T(8,128)S(1)} %get-tuple-element.266, s32[]{:T(128)S(6)} %add.439, s32[]{:T(128)S(6)} %select_n.234), kind=kOutput, calls=%fused_computation.16.clone.1 | convolution fusion | flops 309379072 | bytes 493576 | tf_op jit(solution)/shard_map/while/body/eval_jaxpr/bk,kt->bt/dot_general | solution.py:151
  205.4 9.5 %fusion.227 = f32[48,1024]{1,0:T(8,128)S(1)} fusion(s32[512]{0:T(512)S(1)} %iota_add_fusion.5, f32[2,48,4096]{2,1,0:T(8,128)S(1)} %get-tuple-element.266, s32[]{:T(128)S(6)} %select_n.234), kind=kOutput, calls=%fused_computation.20.clone.1 | convolution fusion | flops 309329920 | bytes 296964 | tf_op jit(solution)/shard_map/while/body/eval_jaxpr/bk,kt->bt/dot_general | solution.py:154
  233.4 9.5 %fusion.230 = f32[1,48,1024]{2,1,0:T(8,128)S(1)} fusion(f32[48,1024]{1,0:T(8,128)S(1)} %fusion.229, s32[512]{0:T(512)S(1)} %iota_add_fusion.5, f32[2,48,4096]{2,1,0:T(8,128)S(1)} %get-tuple-element.266, s32[]{:T(128)S(6)} %add.439, s32[]{:T(128)S(6)} %select_n.234), kind=kOutput, calls=%fused_computation.16.clone.1 | convolution fusion | flops 309379072 | bytes 493576 | tf_op jit(solution)/shard_map/while/body/eval_jaxpr/bk,kt->bt/dot_general | solution.py:151
  242.9 9.3 %fusion.227 = f32[48,1024]{1,0:T(8,128)S(1)} fusion(s32[512]{0:T(512)S(1)} %iota_add_fusion.5, f32[2,48,4096]{2,1,0:T(8,128)S(1)} %get-tuple-element.266, s32[]{:T(128)S(6)} %select_n.234), kind=kOutput, calls=%fused_computation.20.clone.1 | convolution fusion | flops 309329920 | bytes 296964 | tf_op jit(solution)/shard_map/while/body/eval_jaxpr/bk,kt->bt/dot_general | solution.py:154
  270.9 9.3 %fusion.230 = f32[1,48,1024]{2,1,0:T(8,128)S(1)} fusion(f32[48,1024]{1,0:T(8,128)S(1)} %fusion.229, s32[512]{0:T(512)S(1)} %iota_add_fusion.5, f32[2,48,4096]{2,1,0:T(8,128)S(1)} %get-tuple-element.266, s32[]{:T(128)S(6)} %add.439, s32[]{:T(128)S(6)} %select_n.234), kind=kOutput, calls=%fused_computation.16.clone.1 | convolution fusion | flops 309379072 | bytes 493576 | tf_op jit(solution)/shard_map/while/body/eval_jaxpr/bk,kt->bt/dot_general | solution.py:151
  280.2 9.5 %fusion.227 = f32[48,1024]{1,0:T(8,128)S(1)} fusion(s32[512]{0:T(512)S(1)} %iota_add_fusion.5, f32[2,48,4096]{2,1,0:T(8,128)S(1)} %get-tuple-element.266, s32[]{:T(128)S(6)} %select_n.234), kind=kOutput, calls=%fused_computation.20.clone.1 | convolution fusion | flops 309329920 | bytes 296964 | tf_op jit(solution)/shard_map/while/body/eval_jaxpr/bk,kt->bt/dot_general | solution.py:154
  308.1 9.5 %fusion.230 = f32[1,48,1024]{2,1,0:T(8,128)S(1)} fusion(f32[48,1024]{1,0:T(8,128)S(1)} %fusion.229, s32[512]{0:T(512)S(1)} %iota_add_fusion.5, f32[2,48,4096]{2,1,0:T(8,128)S(1)} %get-tuple-element.266, s32[]{:T(128)S(6)} %add.439, s32[]{:T(128)S(6)} %select_n.234), kind=kOutput, calls=%fused_computation.16.clone.1 | convolution fusion | flops 309379072 | bytes 493576 | tf_op jit(solution)/shard_map/while/body/eval_jaxpr/bk,kt->bt/dot_general | solution.py:151
  317.6 9.3 %fusion.227 = f32[48,1024]{1,0:T(8,128)S(1)} fusion(s32[512]{0:T(512)S(1)} %iota_add_fusion.5, f32[2,48,4096]{2,1,0:T(8,128)S(1)} %get-tuple-element.266, s32[]{:T(128)S(6)} %select_n.234), kind=kOutput, calls=%fused_computation.20.clone.1 | convolution fusion | flops 309329920 | bytes 296964 | tf_op jit(solution)/shard_map/while/body/eval_jaxpr/bk,kt->bt/dot_general | solution.py:154
  345.6 9.3 %fusion.230 = f32[1,48,1024]{2,1,0:T(8,128)S(1)} fusion(f32[48,1024]{1,0:T(8,128)S(1)} %fusion.229, s32[512]{0:T(512)S(1)} %iota_add_fusion.5, f32[2,48,4096]{2,1,0:T(8,128)S(1)} %get-tuple-element.266, s32[]{:T(128)S(6)} %add.439, s32[]{:T(128)S(6)} %select_n.234), kind=kOutput, calls=%fused_computation.16.clone.1 | convolution fusion | flops 309379072 | bytes 493576 | tf_op jit(solution)/shard_map/while/body/eval_jaxpr/bk,kt->bt/dot_general | solution.py:151
  354.9 9.5 %fusion.227 = f32[48,1024]{1,0:T(8,128)S(1)} fusion(s32[512]{0:T(512)S(1)} %iota_add_fusion.5, f32[2,48,4096]{2,1,0:T(8,128)S(1)} %get-tuple-element.266, s32[]{:T(128)S(6)} %select_n.234), kind=kOutput, calls=%fused_computation.20.clone.1 | convolution fusion | flops 309329920 | bytes 296964 | tf_op jit(solution)/shard_map/while/body/eval_jaxpr/bk,kt->bt/dot_general | solution.py:154
  382.9 9.5 %fusion.230 = f32[1,48,1024]{2,1,0:T(8,128)S(1)} fusion(f32[48,1024]{1,0:T(8,128)S(1)} %fusion.229, s32[512]{0:T(512)S(1)} %iota_add_fusion.5, f32[2,48,4096]{2,1,0:T(8,128)S(1)} %get-tuple-element.266, s32[]{:T(128)S(6)} %add.439, s32[]{:T(128)S(6)} %select_n.234), kind=kOutput, calls=%fused_computation.16.clone.1 | convolution fusion | flops 309379072 | bytes 493576 | tf_op jit(solution)/shard_map/while/body/eval_jaxpr/bk,kt->bt/dot_general | solution.py:151
  392.4 9.3 %fusion.227 = f32[48,1024]{1,0:T(8,128)S(1)} fusion(s32[512]{0:T(512)S(1)} %iota_add_fusion.5, f32[2,48,4096]{2,1,0:T(8,128)S(1)} %get-tuple-element.266, s32[]{:T(128)S(6)} %select_n.234), kind=kOutput, calls=%fused_computation.20.clone.1 | convolution fusion | flops 309329920 | bytes 296964 | tf_op jit(solution)/shard_map/while/body/eval_jaxpr/bk,kt->bt/dot_general | solution.py:154
  421.8 12.0 %reshape.264 = f32[2,1,49152]{2,1,0:T(1,128)S(1)} reshape(f32[1024,6,2,8]{3,2,1,0:T(2,128)} %bitcast.182) | data formatting | bytes 786432
  433.8 9.2 %all_to_all.51 = f32[2,1,49152]{2,1,0:T(1,128)S(1)} all-to-all(f32[2,1,49152]{2,1,0:T(1,128)S(1)} %reshape.264), channel_id=1, replica_groups=mesh['chan'=4,'sym'=4,'sub'=2] {'sub'}, dimensions={0} | all-to-all | bytes 786432 | tf_op jit(solution)/shard_map/all_to_all | solution.py:168
  445.4 12.5 %reshape.265 = f32[1024,6,2,8]{3,2,1,0:T(2,128)} reshape(f32[2,49152]{1,0:T(2,128)S(1)} %reduce) | data formatting | bytes 786432
  471.8 13.8 %all_to_all.52 = f32[4,1,24576]{2,1,0:T(1,128)S(1)} all-to-all(f32[4,1,24576]{2,1,0:T(1,128)S(1)} %reshape.266), channel_id=1, replica_groups=mesh['chan'=4,'sym'=4,'sub'=2] {'sym'}, dimensions={0} | all-to-all | bytes 786432 | tf_op jit(solution)/shard_map/all_to_all | solution.py:171
  495.6 11.3 %all_to_all.53 = f32[2,16,24,128]{3,1,0,2:T(8,128)S(1)} all-to-all(f32[2,16,24,128]{3,1,0,2:T(8,128)S(1)} %copy.420), channel_id=1, replica_groups=mesh['chan'=4,'sym'=4,'sub'=2] {'sym'}, dimensions={2} | all-to-all | bytes 786432 | tf_op jit(solution)/shard_map/all_to_all | solution.py:181
  (177 shorter events, 282.4 us)
Async XLA Ops:
  0.8 2.2 copy-start.15
  33.9 1.7 copy-start
  37.3 1.8 copy-start.3
  37.3 1.8 copy-start.4
  43.9 4.9 copy-start.13
  75.6 1.4 copy-start.14
  75.6 3.0 copy-start.1
  105.2 1.2 copy-start.12
  105.2 1.2 copy-start.11
  105.2 1.2 copy-start.10
  105.2 1.2 copy-start.9
  105.2 1.3 copy-start.8
  105.2 1.3 copy-start.7
  105.2 1.3 copy-start.6
  105.2 1.3 copy-start.5
  109.2 2.4 copy-start.2
where the time goes:
time: 514 us; the launch traced here: 508 us
  matrix products  331 us (64%)
  local copies, waits for them, and re-layouts  109 us (21%)
  blocking collectives  44.8 us (9%)
  other arithmetic  15.8 us (3%)
  loops' own time  6.85 us (1%)
    dot_general x8, matrix products, accumulate_block(): jnp.einsum('bk,kt->bt', part[1], sine_factor, precision=HIGHEST)  75.2 us
    dot_general x8, matrix products, accumulate_block(): jnp.einsum('bk,kt->bt', part[0], sine_factor, precision=HIGHEST)  75.2 us
    dot_general x8, matrix products, accumulate_block(): jnp.einsum('bk,kt->bt', part[0], cosine_factor, precision=HIGHEST)  72.3 us
    dot_general x8, matrix products, accumulate_block(): jnp.einsum('bk,kt->bt', part[1], cosine_factor, precision=HIGHEST)  72.3 us
    unnamed x39, local copies, waits for them, and re-layouts  35.3 us
    gather x18, local copies, waits for them, and re-layouts  16.8 us
    all_to_all x1, blocking collectives, local(): lax.all_to_all(profiles, 'sym', split_axis=3, concat_axis=2, tiled=True)  13.8 us
    another operation x19, local copies, waits for them, and re-layouts, smooth(): jnp.stack([zero_padded[..., step_body * block_piece:step_body * block_pie...  13 us

commit v1 on v0

v1 whole, which is shorter than its diff:
```python
import functools
import math

import jax
import jax.numpy as jnp
import ml_dtypes
import numpy as np
from jax import lax
from jax.experimental import pallas as pl
from jax.experimental.pallas import tpu as pltpu
from jax.sharding import PartitionSpec as P

OUTER_FACTOR = 64
INNER_FACTOR = 128
ACTIVE_TONES = 4096
GUARD_SAMPLES = 1024
SMOOTH_HALFSPAN = 48
PSP = 12

TWO_PI = 2.0 * math.pi
ROOT_FORTYTWO = math.sqrt(42.0)
HIGHEST = lax.Precision.HIGHEST

WHOLE = OUTER_FACTOR * INNER_FACTOR
FOLD = 32
WIDE = WHOLE // FOLD
LANES = 128
ROWS = 8
LOWEST = (WHOLE - ACTIVE_TONES) // 2
RANGE_ROWS = GUARD_SAMPLES // LANES
VMEM_LIMIT = 48 * 1024 * 1024


def split_table(table):
    high = table.astype(np.float32).astype(ml_dtypes.bfloat16)
    low = (table - high.astype(np.float64)).astype(np.float32).astype(ml_dtypes.bfloat16)
    return high, low


def turning(sign, product, period):
    angle = sign * TWO_PI / period * (product % period)
    cosine, sine = np.cos(angle), np.sin(angle)
    return np.block([[cosine, sine], [-sine, cosine]])


def residue_order():
    row = np.arange(FOLD)
    return row // 8 + 4 * (row % 8)


def spectrum_tables():
    b = np.arange(WIDE)
    j = LOWEST // FOLD + np.arange(ACTIVE_TONES // FOLD)
    high, low = split_table(turning(-1, b[:, None] * j[None, :], WIDE))
    angle = -TWO_PI / WHOLE * (residue_order()[:, None] * b[None, :])
    return high, low, np.stack([np.cos(angle), np.sin(angle)]).astype(np.float32)


def range_tables():
    j = np.arange(ACTIVE_TONES // FOLD)
    l = np.arange(LANES)
    high, low = split_table(turning(1, j[:, None] * l[None, :], ACTIVE_TONES // FOLD))
    angle = TWO_PI / ACTIVE_TONES * (residue_order()[:, None] * l[None, :])
    return high, low, np.stack([np.cos(angle), np.sin(angle)]).astype(np.float32)


def times(x, turn):
    re, im = x
    turn = turn % 1.0
    eighth = round(turn * 8)
    if abs(turn * 8 - eighth) < 1e-9:
        eighth %= 8
        if eighth % 2 == 0:
            return [(re, im), (-im, re), (-re, -im), (im, -re)][eighth // 2]
        half = math.sqrt(0.5)
        add, sub = (re + im) * half, (re - im) * half
        return [(sub, add), (-add, sub), (-sub, -add), (add, -sub)][eighth // 2]
    c, s = math.cos(TWO_PI * turn), math.sin(TWO_PI * turn)
    return re * c - im * s, re * s + im * c


def plus(x, y):
    return x[0] + y[0], x[1] + y[1]


def minus(x, y):
    return x[0] - y[0], x[1] - y[1]


def turn_quarter(x, sign):
    return (-x[1], x[0]) if sign > 0 else (x[1], -x[0])


def dft4(x, sign):
    a, b = plus(x[0], x[2]), minus(x[0], x[2])
    c, d = plus(x[1], x[3]), turn_quarter(minus(x[1], x[3]), sign)
    return [plus(a, c), plus(b, d), minus(a, c), minus(b, d)]


def dft8(x, sign):
    even, odd = dft4(x[0::2], sign), dft4(x[1::2], sign)
    odd = [times(o, sign * k / 8) for k, o in enumerate(odd)]
    return [plus(e, o) for e, o in zip(even, odd)] + [minus(e, o) for e, o in zip(even, odd)]


def dft3(x, sign):
    total, diff = plus(x[1], x[2]), minus(x[1], x[2])
    mid = (x[0][0] - 0.5 * total[0], x[0][1] - 0.5 * total[1])
    root = sign * math.sqrt(0.75)
    side = (-root * diff[1], root * diff[0])
    return [plus(x[0], total), plus(mid, side), minus(mid, side)]


def dft6(x, sign):
    even, odd = dft3(x[0::2], sign), dft3(x[1::2], sign)
    odd = [times(o, sign * k / 6) for k, o in enumerate(odd)]
    return [plus(e, o) for e, o in zip(even, odd)] + [minus(e, o) for e, o in zip(even, odd)]


def split_rows(x):
    high = x.astype(jnp.bfloat16)
    return high, (x - high.astype(jnp.float32)).astype(jnp.bfloat16)


def dot(x, w):
    return lax.dot_general(x, w, (((1,), (0,)), ((), ())), preferred_element_type=jnp.float32)


def spectrum_kernel(off_ref, x_ref, high_ref, low_ref, twist_ref, out_ref, mid_ref, rows_ref):
    off = off_ref[pl.program_id(0)]
    lane = lax.broadcasted_iota(jnp.int32, (ROWS, LANES), 1)

    def sample(part, chunk):
        value = x_ref[part, 0, :, chunk * LANES : (chunk + 1) * LANES]
        if chunk * LANES < GUARD_SAMPLES:
            wrapped = x_ref[part, 0, :, WHOLE + chunk * LANES : WHOLE + (chunk + 1) * LANES]
            value = jnp.where(lane < off - chunk * LANES, wrapped, value)
        return value

    halves = WIDE // LANES
    for h in range(halves):
        for v in range(8):
            chunks = [halves * (8 * u + v) + h for u in range(4)]
            y = dft4([(sample(0, c), sample(1, c)) for c in chunks], -1)
            for p in range(4):
                mid_ref[h, p, v, 0], mid_ref[h, p, v, 1] = times(y[p], -v * p / FOLD)
    for h in range(halves):
        for p in range(4):
            x = [(mid_ref[h, p, v, 0], mid_ref[h, p, v, 1]) for v in range(8)]
            y = dft8(x, -1)
            for q in range(0, 8, 2):
                pair = []
                for row in (p * 8 + q, p * 8 + q + 1):
                    re, im = y[row - p * 8]
                    c = twist_ref[0, row : row + 1, h * LANES : (h + 1) * LANES]
                    s = twist_ref[1, row : row + 1, h * LANES : (h + 1) * LANES]
                    pair.append((re * c - im * s, re * s + im * c))
                at = slice((p * 8 + q) * ROWS, (p * 8 + q + 2) * ROWS)
                for part in range(2):
                    high, low = split_rows(jnp.concatenate([pair[0][part], pair[1][part]], axis=0))
                    column = part * WIDE + h * LANES
                    rows_ref[at, column : column + LANES] = high
                    rows_ref[at, 2 * WIDE + column : 2 * WIDE + column + LANES] = low
    high = rows_ref[:, : 2 * WIDE]
    low = rows_ref[:, 2 * WIDE :]
    out_ref[0, 0] = dot(high, high_ref[...]) + dot(low, high_ref[...]) + dot(high, low_ref[...])


def profile_kernel(
    blocks, scale, off_ref, pilot_ref, place_ref, s_ref, index_ref, high_ref, low_ref, twist_ref, *refs
):
    outs = refs[:blocks]
    gain_ref, ratio_ref, num_ref, rows_ref, range_ref, prof_ref = refs[blocks:]
    m = pl.program_id(0)
    off, offset = off_ref[m], pilot_ref[m]
    tones = ACTIVE_TONES // FOLD

    row = lax.broadcasted_iota(jnp.int32, (FOLD, tones), 0)
    lane = lax.broadcasted_iota(jnp.int32, (FOLD, tones), 1)
    k = (row >> 3) + 4 * (row & 7) + FOLD * lane
    angle = ((off * (k + LOWEST)) & (WHOLE - 1)).astype(jnp.float32) * (TWO_PI / WHOLE)
    index = index_ref[0].astype(jnp.float32)
    high_bits = jnp.floor(index * 0.125)
    level_re = 2.0 * (index - 8.0 * high_bits) - 7.0
    level_im = 2.0 * high_bits - 7.0
    factor = scale / (level_re * level_re + level_im * level_im)
    c, s = jnp.cos(angle), jnp.sin(angle)
    gain_ref[0] = (c * level_re + s * level_im) * factor
    gain_ref[1] = (s * level_re - c * level_im) * factor
    span = SMOOTH_HALFSPAN + 1
    is_pilot = lax.rem(k + (PSP - offset), PSP) == 0
    total = jnp.where(is_pilot, 201.0, 200.0)
    first_after = ACTIVE_TONES + lax.rem(offset + PSP * ACTIVE_TONES - ACTIVE_TONES, PSP)
    for i in range(4):
        before = span - (k - offset + PSP * (i + 1))
        after = span - (first_after + PSP * i - k)
        total = total - jnp.maximum(before, 0).astype(jnp.float32) - jnp.maximum(after, 0).astype(jnp.float32)
    gain_ref[2] = 1.0 / total
    gain_ref[3] = jnp.where(is_pilot, 1.0, 0.0)

    for i in range(FOLD):
        re = s_ref[0, 0, i * ROWS : (i + 1) * ROWS, :tones]
        im = s_ref[0, 0, i * ROWS : (i + 1) * ROWS, tones:]
        c = gain_ref[0, i : i + 1, :]
        s = gain_ref[1, i : i + 1, :]
        ratio_ref[0, i] = re * c - im * s
        ratio_ref[1, i] = re * s + im * c

    r = offset & 3
    lane = lax.broadcasted_iota(jnp.int32, (ROWS, tones), 1)
    for part in range(2):
        picked = [ratio_ref[part, r * 8 + a] * gain_ref[3, pl.ds(r * 8 + a, 1), :] for a in range(8)]

        def pilot(i):
            b, a = i // 8, i % 8
            if b == 0:
                return picked[a]
            rolled = pltpu.roll(picked[a], (-b) % tones, 1)
            return jnp.where((lane + b >= 0) & (lane + b < tones), rolled, 0.0)

        q = {i: pilot(i) for i in range(-13, 21)}
        slope = sum(q[i] for i in range(0, 12)) - sum(q[i] for i in range(-12, 0))
        value = sum((49 - 4 * abs(i + 1)) * q[i] for i in range(-13, 12))
        for a in range(-1, 8):
            for s in range(4):
                place = r + s
                here = value if s == 0 else value + s * slope - q[a - 12]
                num_ref[part, (place & 3) * 10 + a + 1 + (place >> 2)] = here
            value = value + 4.0 * slope - q[a - 12] + q[a + 13]
            if a < 7:
                slope = slope + q[a + 13] - 2.0 * q[a + 1] + q[a - 11]

    for i in range(0, FOLD, 2):
        for part in range(2):
            pair = []
            for row in (i, i + 1):
                smooth = num_ref[part, (row // 8) * 10 + row % 8 + 1] * gain_ref[2, row : row + 1, :]
                pair.append(ratio_ref[part, row] - smooth)
            high, low = split_rows(jnp.concatenate(pair, axis=0))
            at = slice(i * ROWS, (i + 2) * ROWS)
            rows_ref[at, part * tones : (part + 1) * tones] = high
            rows_ref[at, (2 + part) * tones : (3 + part) * tones] = low
    high = rows_ref[:, : 2 * tones]
    low = rows_ref[:, 2 * tones :]
    range_ref[...] = dot(high, high_ref[...]) + dot(low, high_ref[...]) + dot(high, low_ref[...])

    sums = None
    for p in range(4):
        x = []
        for q in range(8):
            i = p * 8 + q
            re = range_ref[i * ROWS : (i + 1) * ROWS, :LANES]
            im = range_ref[i * ROWS : (i + 1) * ROWS, LANES:]
            c = twist_ref[0, i : i + 1, :]
            s = twist_ref[1, i : i + 1, :]
            x.append((re * c - im * s, re * s + im * c))
        y = [times(v, p * h / FOLD) for h, v in enumerate(dft8(x, 1))]
        sums = y if sums is None else [plus(a, b) for a, b in zip(sums, y)]
    if blocks == 1:
        for h in range(RANGE_ROWS):
            outs[0][0, 0, 0, h], outs[0][0, 0, 1, h] = sums[h]
        return
    for h in range(RANGE_ROWS):
        prof_ref[0, h], prof_ref[1, h] = sums[h]
    each = RANGE_ROWS // blocks
    for d in range(blocks):
        block = place_ref[0] ^ d
        for part in range(2):
            for h in range(each):
                outs[d][0, 0, part, h] = prof_ref[part, block * each + h]


def doppler_kernel(place_ref, *refs):
    pieces, outs, (turned_ref, spread_ref) = refs[:4], refs[4:8], refs[8:]
    own, rank = place_ref[0], place_ref[1]
    local_symbols, _, _, each = pieces[0].shape[:4]
    for d in range(4):
        for m in range(local_symbols):
            turned_ref[own ^ d, m] = pieces[d][m, 0]
    for h in range(each):
        grid = {}
        for m in range(local_symbols):
            x = [(turned_ref[s, m, 0, h], turned_ref[s, m, 1, h]) for s in range(4)]
            for p, y in enumerate(dft4(x, -1)):
                grid[p, m] = times(y, -m * p / (4 * local_symbols))
        for p in range(4):
            for q, y in enumerate(dft6([grid[p, m] for m in range(local_symbols)], -1)):
                f = p + 4 * q
                at = slice(h * LANES, (h + 1) * LANES)
                spread_ref[f // local_symbols, 0, f % local_symbols, :, at] = y[0]
                spread_ref[f // local_symbols, 1, f % local_symbols, :, at] = y[1]
    for d in range(4):
        outs[d][...] = spread_ref[rank ^ d]


def join_kernel(place_ref, *refs):
    pieces, out_ref = refs[:4], refs[4]
    own = place_ref[0]
    wide = pieces[0].shape[-1]
    for d in range(4):
        h = own ^ d
        rows = pl.ds(pl.multiple_of((h & 1) * ROWS, ROWS), ROWS)
        columns = pl.ds(pl.multiple_of((h >> 1) * wide, LANES), wide)
        out_ref[:, :, rows, columns] = pieces[d][...]


def spectra(windows, cp_offset):
    _, symbols, channels, record = windows.shape
    high, low, twist = spectrum_tables()
    tones = ACTIVE_TONES // FOLD
    whole = lambda a: pl.BlockSpec(a.shape, lambda m, g, *_: (0,) * a.ndim)
    return pl.pallas_call(
        spectrum_kernel,
        grid_spec=pltpu.PrefetchScalarGridSpec(
            num_scalar_prefetch=1,
            grid=(symbols, channels // ROWS),
            in_specs=[
                pl.BlockSpec((2, 1, ROWS, record), lambda m, g, *_: (0, m, g, 0)),
                whole(high),
                whole(low),
                whole(twist),
            ],
            out_specs=pl.BlockSpec((1, 1, FOLD * ROWS, 2 * tones), lambda m, g, *_: (m, g, 0, 0)),
            scratch_shapes=[
                pltpu.VMEM((WIDE // LANES, 4, 8, 2, ROWS, LANES), jnp.float32),
                pltpu.VMEM((FOLD * ROWS, 4 * WIDE), jnp.bfloat16),
            ],
        ),
        out_shape=jax.ShapeDtypeStruct((symbols, channels // ROWS, FOLD * ROWS, 2 * tones), jnp.float32),
        compiler_params=pltpu.CompilerParams(vmem_limit_bytes=VMEM_LIMIT),
        name="spectra",
    )(cp_offset, windows, high, low, twist)


def profiles(spectrum, index, pilot_offsets, cp_offset, place, blocks, scale):
    symbols, groups = spectrum.shape[:2]
    high, low, twist = range_tables()
    tones = ACTIVE_TONES // FOLD
    each = RANGE_ROWS // blocks
    whole = lambda a: pl.BlockSpec(a.shape, lambda m, g, *_: (0,) * a.ndim)
    block = (1, 1, 2, each, ROWS, LANES)
    return pl.pallas_call(
        functools.partial(profile_kernel, blocks, scale),
        grid_spec=pltpu.PrefetchScalarGridSpec(
            num_scalar_prefetch=3,
            grid=(symbols, groups),
            in_specs=[
                pl.BlockSpec((1, 1, FOLD * ROWS, 2 * tones), lambda m, g, *_: (m, g, 0, 0)),
                pl.BlockSpec((1, FOLD, tones), lambda m, g, *_: (m, 0, 0)),
                whole(high),
                whole(low),
                whole(twist),
            ],
            out_specs=[pl.BlockSpec(block, lambda m, g, *_: (m, g, 0, 0, 0, 0))] * blocks,
            scratch_shapes=[
                pltpu.VMEM((4, FOLD, tones), jnp.float32),
                pltpu.VMEM((2, FOLD, ROWS, tones), jnp.float32),
                pltpu.VMEM((2, 40, ROWS, tones), jnp.float32),
                pltpu.VMEM((FOLD * ROWS, 4 * tones), jnp.bfloat16),
                pltpu.VMEM((FOLD * ROWS, 2 * LANES), jnp.float32),
                pltpu.VMEM((2, RANGE_ROWS, ROWS, LANES), jnp.float32),
            ],
        ),
        out_shape=[jax.ShapeDtypeStruct((symbols, groups) + block[2:], jnp.float32)] * blocks,
        compiler_params=pltpu.CompilerParams(vmem_limit_bytes=VMEM_LIMIT),
        name="profiles",
    )(cp_offset, pilot_offsets, place, spectrum, index, high, low, twist)


def doppler_plain(own_profiles, symbols):
    turned = lax.all_to_all(own_profiles, "sub", split_axis=3, concat_axis=1, tiled=True)
    turned = lax.all_to_all(turned, "sym", split_axis=3, concat_axis=2, tiled=True)
    ids = np.arange(symbols)
    angle = TWO_PI / symbols * (ids[:, None] * ids[None, :] % symbols)
    c, s = np.cos(angle).astype(np.float32), np.sin(angle).astype(np.float32)
    product = lambda t, x: jnp.einsum("fm,cmq->cfq", t, x, precision=HIGHEST)
    re = product(c, turned[0]) + product(s, turned[1])
    im = product(c, turned[1]) - product(s, turned[0])
    return lax.all_to_all(jnp.stack([re, im]), "sym", split_axis=2, concat_axis=3, tiled=True)


def doppler_paired(pieces, place, rank, syms, subs):
    share = syms // subs
    got = [pieces[0]] + [
        lax.ppermute(pieces[d], "sym", [(i, i ^ d) for i in range(syms)]) for d in range(1, syms)
    ]
    symbols, _, _, each = got[0].shape[:4]
    piece = jax.ShapeDtypeStruct((2, symbols, ROWS, each * LANES), jnp.float32)
    in_vmem = pl.BlockSpec(memory_space=pltpu.VMEM)
    in_smem = pl.BlockSpec(memory_space=pltpu.SMEM)
    spread = pl.pallas_call(
        doppler_kernel,
        in_specs=[in_smem] + [in_vmem] * syms,
        out_specs=[in_vmem] * syms,
        out_shape=[piece] * syms,
        scratch_shapes=[
            pltpu.VMEM((syms, symbols, 2, each, ROWS, LANES), jnp.float32),
            pltpu.VMEM((syms,) + piece.shape, jnp.float32),
        ],
        compiler_params=pltpu.CompilerParams(vmem_limit_bytes=VMEM_LIMIT),
        name="doppler",
    )(jnp.stack([place, rank]), *got)
    joined = []
    for d in range(syms):
        route = [
            (s * subs + u, (((s % share) * subs + u) ^ d) * subs + s // share)
            for s in range(syms)
            for u in range(subs)
        ]
        joined.append(lax.ppermute(spread[d], ("sym", "sub"), route))
    out = pl.pallas_call(
        join_kernel,
        in_specs=[in_smem] + [in_vmem] * syms,
        out_specs=in_vmem,
        out_shape=jax.ShapeDtypeStruct((2, symbols, subs * ROWS, share * each * LANES), jnp.float32),
        compiler_params=pltpu.CompilerParams(vmem_limit_bytes=VMEM_LIMIT),
        name="join",
    )(place[None], *joined)
    return jnp.transpose(out, (0, 2, 1, 3))


def local(samples, constellation_index, pilot_offsets, cp_offset):
    syms, subs = lax.axis_size("sym"), lax.axis_size("sub")
    place, sub = lax.axis_index("sym"), lax.axis_index("sub")
    channels, symbols = samples.shape[1:3]
    index = constellation_index.reshape(symbols, -1, 8, 4).transpose(0, 3, 2, 1)
    index = index.reshape(symbols, FOLD, -1).astype(jnp.bfloat16)
    index = lax.all_gather(index, "sub", axis=2, tiled=True)
    windows = jnp.transpose(samples, (0, 2, 1, 3))
    short = -channels % ROWS
    if short:
        windows = jnp.pad(windows, ((0, 0), (0, 0), (0, short), (0, 0)))
    spectrum = spectra(windows, cp_offset)
    scale = ROOT_FORTYTWO / math.sqrt(WHOLE * ACTIVE_TONES * symbols * syms)
    paired = syms == 4 and subs == 2 and channels == ROWS and symbols == 6
    got = profiles(
        spectrum, index, pilot_offsets, cp_offset, place[None], syms if paired else 1, scale
    )
    if paired:
        rank = (place % (syms // subs)) * subs + sub
        return doppler_paired(got, place, rank, syms, subs)
    own = jnp.transpose(got[0], (2, 1, 4, 0, 3, 5))
    own = own.reshape(2, channels + short, symbols, GUARD_SAMPLES)[:, :channels]
    return doppler_plain(own, symbols * syms)


def solution(mesh):
    return jax.shard_map(
        local,
        mesh=mesh,
        in_specs=(
            P(None, ("chan", "sub"), "sym", None),
            P(("chan", "sym"), "sub"),
            P("sym"),
            P(("chan", "sym")),
        ),
        out_specs=P(None, "chan", "sym", "sub"),
        check_vma=False,
    )
```

time: 514 us -> 53 us (0.10); the launches traced: 508 us -> 52.6 us
  matrix products: 331 us -> 0 us
  local copies, waits for them, and re-layouts: 109 us -> 7.97 us
  blocking collectives: 44.8 us -> 7.12 us
  other arithmetic: 15.8 us -> 0.92 us
  starting transfers between devices: 0 us -> 14.7 us
  waiting for transfers between devices: 0 us -> 11.4 us
  Pallas kernels: 0 us -> 10.4 us
  loops' own time: 6.85 us -> 0 us
    dot_general x46 -> x0, matrix products: 331 us -> none  [the longest x8 75.2 us: accumulate_block(): jnp.einsum('bk,kt->bt', part[1], sine_factor, precision=HIGHEST)]
    all_to_all x3 -> x0, blocking collectives: 34.3 us -> none  [the longest x1 13.8 us: local(): lax.all_to_all(profiles, 'sym', split_axis=3, concat_axis=2, tiled=True)]
    unnamed x39 -> x18, local copies, waits for them, and re-layouts: 35.3 us -> 5.42 us
    another operation x21 -> x0, local copies, waits for them, and re-layouts: 17.6 us -> none  [the longest x19 13 us: smooth(): jnp.stack([zero_padded[..., step_body * block_piece:step_body * block_pie...]
    gather x18 -> x0, local copies, waits for them, and re-layouts: 16.8 us -> none
    ppermute x0 -> x7, starting transfers between devices: none -> 14.7 us  [the longest x4 10.3 us: doppler_paired(): joined.append(lax.ppermute(spread[d], ('sym', 'sub'), route))]
    all_to_all x6 -> x0, local copies, waits for them, and re-layouts: 13.5 us -> none  [the longest x3 10.1 us: local(): lax.all_to_all(own_profiles, 'sub', split_axis=3, concat_axis=1, tiled=True)]
    ppermute x0 -> x7, waiting for transfers between devices: none -> 11.4 us  [the longest x3 6.88 us: doppler_paired(): lax.ppermute(pieces[d], 'sym', [(i, i ^ d) for i in range(syms)])]
  transfers between devices with their start and end apart: 0 -> 7, of which waited for: 0 -> 4; matrix products, arithmetic and copies ran while one was open for 0% -> 0% of each run, Pallas kernels for 0% -> 0%
where the time goes in v1:
time: 53 us; the launch traced here: 52.6 us
  starting transfers between devices  14.7 us (28%)
  waiting for transfers between devices  11.4 us (22%)
  Pallas kernels  10.4 us (20%)
  local copies, waits for them, and re-layouts  7.97 us (15%)
  blocking collectives  7.12 us (13%)
  other arithmetic  0.92 us (2%)
    ppermute x4, starting transfers between devices, doppler_paired(): joined.append(lax.ppermute(spread[d], ('sym', 'sub'), route))  10.3 us
    all_gather x1, blocking collectives, local(): index = lax.all_gather(index, 'sub', axis=2, tiled=True)  7.12 us
    ppermute x3, waiting for transfers between devices, doppler_paired(): lax.ppermute(pieces[d], 'sym', [(i, i ^ d) for i in range(syms)])  6.88 us
    unnamed x18, local copies, waits for them, and re-layouts  5.42 us
    pallas_call x1, Pallas kernels, spectra(): pl.pallas_call(spectrum_kernel, grid_spec=pltpu.PrefetchScalarGridSpec(nu...  4.5 us
    ppermute x4, waiting for transfers between devices, doppler_paired(): joined.append(lax.ppermute(spread[d], ('sym', 'sub'), route))  4.48 us
    ppermute x3, starting transfers between devices, doppler_paired(): lax.ppermute(pieces[d], 'sym', [(i, i ^ d) for i in range(syms)])  4.48 us
    pallas_call x1, Pallas kernels, profiles(): pl.pallas_call(functools.partial(profile_kernel, blocks, scale), grid_spe...  4.4 us
  transfers between devices with their start and end apart: 7, of which 4 were waited for; matrix products, arithmetic and copies ran while one was open for 0% of the time, Pallas kernels for 0%

profile of v1, /device:TPU:0, one launch (start us, length us, event | category | flops | bytes accessed | tf_op | source)
XLA Modules:
  0.0 52.6 jit_solution(13973282299955656916)
XLA Ops:
  0.0 0.8 %convert_element_type.12 = bf16[6,2048]{1,0:T(8,128)(2,1)S(1)} convert(s32[6,2048]{1,0:T(8,128)} %param.11) | non-fusion elementwise | flops 12288 | bytes 73728 | tf_op jit(solution)/shard_map/convert_element_type | solution.py:427
  0.8 1.7 %convert_element_type.13 = bf16[6,64,8,4]{3,2,1,0:T(8,128)(2,1)S(1)} reshape(bf16[6,2048]{1,0:T(8,128)(2,1)S(1)} %convert_element_type.12) | data formatting | bytes 49152 | tf_op jit(solution)/shard_map/convert_element_type | solution.py:427
  2.6 0.5 %copy.14 = bf16[6,4,8,64]{3,2,1,0:T(8,128)(2,1)S(1)} copy(bf16[6,4,8,64]{1,2,3,0:T(8,128)(2,1)S(1)} %bitcast.7) | data formatting | bytes 49152 | tf_op jit(solution)/shard_map/convert_element_type | solution.py:427
  3.3 7.1 %all_gather.3 = bf16[6,32,128]{1,0,2:T(8,128)(2,1)S(1)} all-gather(bf16[6,32,64]{1,0,2:T(8,128)(2,1)S(1)} %copy.15), channel_id=1, replica_groups=mesh['chan'=4,'sym'=4,'sub'=2] {'sub'}, dimensions={2}, use_global_device_ids=true | all-gather | bytes 73728 | tf_op jit(solution)/shard_map/all_gather | solution.py:428
  10.4 0.2 copy.16.index_ref
  10.6 2.0 %copy-done = f32[2,8,6,9216]{3,1,2,0:T(8,128)S(1)} copy-done((f32[2,8,6,9216]{3,1,2,0:T(8,128)S(1)}, f32[2,8,6,9216]{3,1,2,0:T(8,128)}, u32[]{:S(2)}) %copy-start) | copy-done | bytes 3538968
  12.6 0.9 %copy-done.1 = bf16[512,256]{1,0:T(8,128)(2,1)S(1)} copy-done((bf16[512,256]{1,0:T(8,128)(2,1)S(1)}, bf16[512,256]{1,0:T(8,128)(2,1)}, u32[]{:S(2)}) %copy-start.1) | copy-done | bytes 262168
  13.5 0.9 %copy-done.2 = bf16[512,256]{1,0:T(8,128)(2,1)S(1)} copy-done((bf16[512,256]{1,0:T(8,128)(2,1)S(1)}, bf16[512,256]{1,0:T(8,128)(2,1)}, u32[]{:S(2)}) %copy-start.2) | copy-done | bytes 262168
  14.5 0.8 %copy-done.5 = f32[2,32,256]{2,1,0:T(8,128)S(1)} copy-done((f32[2,32,256]{2,1,0:T(8,128)S(1)}, f32[2,32,256]{2,1,0:T(8,128)}, u32[]{:S(2)}) %copy-start.5) | copy-done | bytes 65560
  15.3 0.7 %copy-done.7 = s32[6]{0:T(128)S(1)} copy-done((s32[6]{0:T(128)S(1)}, s32[6]{0:T(128)}, u32[]{:S(2)}) %copy-start.7) | copy-done | bytes 48
  16.0 4.5 %spectra.1.s_ref = f32[6,1,256,256]{3,2,1,0:T(8,128)S(1)} custom-call(s32[6]{0:T(128)S(1)} %copy-done.7, f32[2,6,8,9216]{3,2,1,0:T(8,128)S(1)} %bitcast.6, bf16[512,256]{1,0:T(8,128)(2,1)S(1)} %copy-done.2, bf16[512,256]{1,0:T(8,128)(2,1)S(1)} %copy-done.1, f32[2,32,256]{2,1,0:T(8,128)S(1)} %copy-done.5), custom_call_target="tpu_custom_call" | custom-call | tf_op jit(solution)/shard_map/spectra/pallas_call | solution.py:312
  20.5 4.4 %profiles.1 = (f32[6,1,2,2,8,128]{5,4,3,2,1,0:T(8,128)S(1)}, f32[6,1,2,2,8,128]{5,4,3,2,1,0:T(8,128)S(1)}, f32[6,1,2,2,8,128]{5,4,3,2,1,0:T(8,128)S(1)}, f32[6,1,2,2,8,128]{5,4,3,2,1,0:T(8,128)S(1)}) custom-call(s32[6]{0:T(128)S(1)} %copy-done.7, s32[6]{0:T(128)S(1)} %copy-done.8, s32[1]{0:T(128)} %bitcast.place_ref, f32[6,1,256,256]{3,2,1,0:T(8,128)S(1)} %spectra.1.s_ref, ...), custom_call_target="tpu_custom_call" | custom-call | tf_op jit(solution)/shard_map/profiles/pallas_call | solution.py:342
  24.9 1.9 %collective-permute-start = (f32[6,1,2,2,8,128]{5,4,3,2,1,0:T(8,128)S(1)}, f32[6,1,2,2,8,128]{5,4,3,2,1,0:T(8,128)S(1)}, u32[]{:S(2)}, u32[]{:S(2)}) collective-permute-start(f32[6,1,2,2,8,128]{5,4,3,2,1,0:T(8,128)S(1)} %get-tuple-element.14), channel_id=1, source_target_pairs={{0,2},{2,0},{4,6},{6,4},{1,3},{3,1},{5,7},{7,5},{8,10},{10,8},{12,... | collective-permute-start | bytes 294920 | tf_op jit(solution)/shard_map/ppermute | solution.py:385
  26.8 2.6 %collective-permute-start.1 = (f32[6,1,2,2,8,128]{5,4,3,2,1,0:T(8,128)S(1)}, f32[6,1,2,2,8,128]{5,4,3,2,1,0:T(8,128)S(1)}, u32[]{:S(2)}, u32[]{:S(2)}) collective-permute-start(f32[6,1,2,2,8,128]{5,4,3,2,1,0:T(8,128)S(1)} %get-tuple-element.15), channel_id=1, source_target_pairs={{0,4},{2,6},{4,0},{6,2},{1,5},{3,7},{5,1},{7,3},{8,12},{10,14},{12... | collective-permute-start | bytes 294920 | tf_op jit(solution)/shard_map/ppermute | solution.py:385
  29.5 1.1 %collective-permute-done.refs_1_ = f32[6,1,2,2,8,128]{5,4,3,2,1,0:T(8,128)S(1)} collective-permute-done((f32[6,1,2,2,8,128]{5,4,3,2,1,0:T(8,128)S(1)}, f32[6,1,2,2,8,128]{5,4,3,2,1,0:T(8,128)S(1)}, u32[]{:S(2)}, u32[]{:S(2)}) %collective-permute-start) | collective-permute-done | bytes 98336 | tf_op jit(solution)/shard_map/ppermute | solution.py:385
  30.6 5.8 %collective-permute-done.1.refs_2_ = f32[6,1,2,2,8,128]{5,4,3,2,1,0:T(8,128)S(1)} collective-permute-done((f32[6,1,2,2,8,128]{5,4,3,2,1,0:T(8,128)S(1)}, f32[6,1,2,2,8,128]{5,4,3,2,1,0:T(8,128)S(1)}, u32[]{:S(2)}, u32[]{:S(2)}) %collective-permute-start.1) | collective-permute-done | bytes 98336 | tf_op jit(solution)/shard_map/ppermute | solution.py:385
  36.4 0.7 %doppler.1 = (f32[2,6,8,256]{3,2,1,0:T(8,128)S(1)}, f32[2,6,8,256]{3,2,1,0:T(8,128)S(1)}, f32[2,6,8,256]{3,2,1,0:T(8,128)S(1)}, f32[2,6,8,256]{3,2,1,0:T(8,128)S(1)}) custom-call(s32[2]{0:T(128)S(1)} %pad_add_fusion.place_ref, f32[6,1,2,2,8,128]{5,4,3,2,1,0:T(8,128)S(1)} %get-tuple-element.13.refs_0_, ...), custom_call_target="tpu_custom_call" | custom-call | tf_op jit(solution)/shard_map/doppler/pallas_call | solution.py:391
  37.1 0.7 %collective-permute-start.3 = (f32[2,6,8,256]{3,2,1,0:T(8,128)S(1)}, f32[2,6,8,256]{3,2,1,0:T(8,128)S(1)}, u32[]{:S(2)}, u32[]{:S(2)}) collective-permute-start(f32[2,6,8,256]{3,2,1,0:T(8,128)S(1)} %get-tuple-element.17), channel_id=1, source_target_pairs={{0,0},{1,2},{2,4},{3,6},{4,1},{5,3},{6,5},{7,7},{8,8},{9,10},{10,1... | collective-permute-start | bytes 294920 | tf_op jit(solution)/shard_map/ppermute | solution.py:410
  37.8 4.5 %collective-permute-start.4 = (f32[2,6,8,256]{3,2,1,0:T(8,128)S(1)}, f32[2,6,8,256]{3,2,1,0:T(8,128)S(1)}, u32[]{:S(2)}, u32[]{:S(2)}) collective-permute-start(f32[2,6,8,256]{3,2,1,0:T(8,128)S(1)} %get-tuple-element.18), channel_id=1, source_target_pairs={{0,2},{1,0},{2,6},{3,4},{4,3},{5,1},{6,7},{7,5},{8,10},{9,8},{10,1... | collective-permute-start | bytes 294920 | tf_op jit(solution)/shard_map/ppermute | solution.py:410
  42.3 2.2 %collective-permute-start.5 = (f32[2,6,8,256]{3,2,1,0:T(8,128)S(1)}, f32[2,6,8,256]{3,2,1,0:T(8,128)S(1)}, u32[]{:S(2)}, u32[]{:S(2)}) collective-permute-start(f32[2,6,8,256]{3,2,1,0:T(8,128)S(1)} %get-tuple-element.19), channel_id=1, source_target_pairs={{0,4},{1,6},{2,0},{3,2},{4,5},{5,7},{6,1},{7,3},{8,12},{9,14},{10,... | collective-permute-start | bytes 294920 | tf_op jit(solution)/shard_map/ppermute | solution.py:410
  44.5 2.9 %collective-permute-start.6 = (f32[2,6,8,256]{3,2,1,0:T(8,128)S(1)}, f32[2,6,8,256]{3,2,1,0:T(8,128)S(1)}, u32[]{:S(2)}, u32[]{:S(2)}) collective-permute-start(f32[2,6,8,256]{3,2,1,0:T(8,128)S(1)} %get-tuple-element.20), channel_id=1, source_target_pairs={{0,6},{1,4},{2,2},{3,0},{4,7},{5,5},{6,3},{7,1},{8,14},{9,12},{10,... | collective-permute-start | bytes 294920 | tf_op jit(solution)/shard_map/ppermute | solution.py:410
  47.4 1.1 %collective-permute-done.5.refs_2_ = f32[2,6,8,256]{3,2,1,0:T(8,128)S(1)} collective-permute-done((f32[2,6,8,256]{3,2,1,0:T(8,128)S(1)}, f32[2,6,8,256]{3,2,1,0:T(8,128)S(1)}, u32[]{:S(2)}, u32[]{:S(2)}) %collective-permute-start.5) | collective-permute-done | bytes 98336 | tf_op jit(solution)/shard_map/ppermute | solution.py:410
  48.5 3.4 %collective-permute-done.6.refs_3_ = f32[2,6,8,256]{3,2,1,0:T(8,128)S(1)} collective-permute-done((f32[2,6,8,256]{3,2,1,0:T(8,128)S(1)}, f32[2,6,8,256]{3,2,1,0:T(8,128)S(1)}, u32[]{:S(2)}, u32[]{:S(2)}) %collective-permute-start.6) | collective-permute-done | bytes 98336 | tf_op jit(solution)/shard_map/ppermute | solution.py:410
  51.9 0.8 %join.1 = f32[2,6,16,512]{3,2,1,0:T(8,128)} custom-call(s32[1]{0:T(128)} %bitcast.place_ref, f32[2,6,8,256]{3,2,1,0:T(8,128)S(1)} %collective-permute-done.3.refs_0_, f32[2,6,8,256]{3,2,1,0:T(8,128)S(1)} %collective-permute-done.4.refs_1_, f32[2,6,8,256]{3,2,1,0:T(8,128)S(1)} %collective-permute-done.5.refs_2_, ...), custom_call_target="tpu_custom_call" | custom-call | tf_op jit(solution)/shard_map/join/pallas_call | solution.py:411
  (19 shorter events, 0.3 us)
Async XLA Ops:
  2.5 17.9 %copy-start.3 = (bf16[256,256]{1,0:T(8,128)(2,1)S(1)}, bf16[256,256]{1,0:T(8,128)(2,1)}, u32[]{:S(2)}) copy-start(bf16[256,256]{1,0:T(8,128)(2,1)} %constant.37.clone.low_ref) | copy-start | bytes 393220
  2.6 17.9 %copy-start.4 = (bf16[256,256]{1,0:T(8,128)(2,1)S(1)}, bf16[256,256]{1,0:T(8,128)(2,1)}, u32[]{:S(2)}) copy-start(bf16[256,256]{1,0:T(8,128)(2,1)} %constant.36.clone.high_ref) | copy-start | bytes 393220
  2.6 17.9 %copy-start.6 = (f32[2,32,128]{2,1,0:T(8,128)S(1)}, f32[2,32,128]{2,1,0:T(8,128)}, u32[]{:S(2)}) copy-start(f32[2,32,128]{2,1,0:T(8,128)} %constant.38.clone.twist_ref) | copy-start | bytes 98308
  2.6 17.9 %copy-start.8 = (s32[6]{0:T(128)S(1)}, s32[6]{0:T(128)}, u32[]{:S(2)}) copy-start(s32[6]{0:T(128)} %pilot_ref.1) | copy-start | bytes 76
  10.6 2.0 %copy-start = (f32[2,8,6,9216]{3,1,2,0:T(8,128)S(1)}, f32[2,8,6,9216]{3,1,2,0:T(8,128)}, u32[]{:S(2)}) copy-start(f32[2,8,6,9216]{3,1,2,0:T(8,128)} %param.10) | copy-start | bytes 10616836
  12.6 0.9 %copy-start.1 = (bf16[512,256]{1,0:T(8,128)(2,1)S(1)}, bf16[512,256]{1,0:T(8,128)(2,1)}, u32[]{:S(2)}) copy-start(bf16[512,256]{1,0:T(8,128)(2,1)} %constant.34.clone.low_ref) | copy-start | bytes 786436
  13.5 0.9 %copy-start.2 = (bf16[512,256]{1,0:T(8,128)(2,1)S(1)}, bf16[512,256]{1,0:T(8,128)(2,1)}, u32[]{:S(2)}) copy-start(bf16[512,256]{1,0:T(8,128)(2,1)} %constant.33.clone.high_ref) | copy-start | bytes 786436
  14.5 0.8 %copy-start.5 = (f32[2,32,256]{2,1,0:T(8,128)S(1)}, f32[2,32,256]{2,1,0:T(8,128)}, u32[]{:S(2)}) copy-start(f32[2,32,256]{2,1,0:T(8,128)} %constant.35.clone.twist_ref) | copy-start | bytes 196612
  15.3 0.7 %copy-start.7 = (s32[6]{0:T(128)S(1)}, s32[6]{0:T(128)}, u32[]{:S(2)}) copy-start(s32[6]{0:T(128)} %off_ref.3) | copy-start | bytes 76
  24.9 5.7 %collective-permute-start = (f32[6,1,2,2,8,128]{5,4,3,2,1,0:T(8,128)S(1)}, f32[6,1,2,2,8,128]{5,4,3,2,1,0:T(8,128)S(1)}, u32[]{:S(2)}, u32[]{:S(2)}) collective-permute-start(f32[6,1,2,2,8,128]{5,4,3,2,1,0:T(8,128)S(1)} %get-tuple-element.14), channel_id=1, source_target_pairs={{0,2},{2,0},{4,6},{6,4},{1,3},{3,1},{5,7},{7,5},{8,10},{10,8},{12,... | collective-permute-start | bytes 294920 | tf_op jit(solution)/shard_map/ppermute | solution.py:385
  26.8 9.5 %collective-permute-start.1 = (f32[6,1,2,2,8,128]{5,4,3,2,1,0:T(8,128)S(1)}, f32[6,1,2,2,8,128]{5,4,3,2,1,0:T(8,128)S(1)}, u32[]{:S(2)}, u32[]{:S(2)}) collective-permute-start(f32[6,1,2,2,8,128]{5,4,3,2,1,0:T(8,128)S(1)} %get-tuple-element.15), channel_id=1, source_target_pairs={{0,4},{2,6},{4,0},{6,2},{1,5},{3,7},{5,1},{7,3},{8,12},{10,14},{12... | collective-permute-start | bytes 294920 | tf_op jit(solution)/shard_map/ppermute | solution.py:385
  29.4 7.0 %collective-permute-start.2 = (f32[6,1,2,2,8,128]{5,4,3,2,1,0:T(8,128)S(1)}, f32[6,1,2,2,8,128]{5,4,3,2,1,0:T(8,128)S(1)}, u32[]{:S(2)}, u32[]{:S(2)}) collective-permute-start(f32[6,1,2,2,8,128]{5,4,3,2,1,0:T(8,128)S(1)} %get-tuple-element.16), channel_id=1, source_target_pairs={{0,6},{2,4},{4,2},{6,0},{1,7},{3,5},{5,3},{7,1},{8,14},{10,12},{12... | collective-permute-start | bytes 294920 | tf_op jit(solution)/shard_map/ppermute | solution.py:385
  37.1 10.3 %collective-permute-start.3 = (f32[2,6,8,256]{3,2,1,0:T(8,128)S(1)}, f32[2,6,8,256]{3,2,1,0:T(8,128)S(1)}, u32[]{:S(2)}, u32[]{:S(2)}) collective-permute-start(f32[2,6,8,256]{3,2,1,0:T(8,128)S(1)} %get-tuple-element.17), channel_id=1, source_target_pairs={{0,0},{1,2},{2,4},{3,6},{4,1},{5,3},{6,5},{7,7},{8,8},{9,10},{10,1... | collective-permute-start | bytes 294920 | tf_op jit(solution)/shard_map/ppermute | solution.py:410
  37.8 9.6 %collective-permute-start.4 = (f32[2,6,8,256]{3,2,1,0:T(8,128)S(1)}, f32[2,6,8,256]{3,2,1,0:T(8,128)S(1)}, u32[]{:S(2)}, u32[]{:S(2)}) collective-permute-start(f32[2,6,8,256]{3,2,1,0:T(8,128)S(1)} %get-tuple-element.18), channel_id=1, source_target_pairs={{0,2},{1,0},{2,6},{3,4},{4,3},{5,1},{6,7},{7,5},{8,10},{9,8},{10,1... | collective-permute-start | bytes 294920 | tf_op jit(solution)/shard_map/ppermute | solution.py:410
  42.3 6.2 %collective-permute-start.5 = (f32[2,6,8,256]{3,2,1,0:T(8,128)S(1)}, f32[2,6,8,256]{3,2,1,0:T(8,128)S(1)}, u32[]{:S(2)}, u32[]{:S(2)}) collective-permute-start(f32[2,6,8,256]{3,2,1,0:T(8,128)S(1)} %get-tuple-element.19), channel_id=1, source_target_pairs={{0,4},{1,6},{2,0},{3,2},{4,5},{5,7},{6,1},{7,3},{8,12},{9,14},{10,... | collective-permute-start | bytes 294920 | tf_op jit(solution)/shard_map/ppermute | solution.py:410
  44.5 7.4 %collective-permute-start.6 = (f32[2,6,8,256]{3,2,1,0:T(8,128)S(1)}, f32[2,6,8,256]{3,2,1,0:T(8,128)S(1)}, u32[]{:S(2)}, u32[]{:S(2)}) collective-permute-start(f32[2,6,8,256]{3,2,1,0:T(8,128)S(1)} %get-tuple-element.20), channel_id=1, source_target_pairs={{0,6},{1,4},{2,2},{3,0},{4,7},{5,5},{6,3},{7,1},{8,14},{9,12},{10,... | collective-permute-start | bytes 294920 | tf_op jit(solution)/shard_map/ppermute | solution.py:410

commit v2 on v1

v2 whole, which is shorter than its diff:
```python
import functools
import math

import jax
import jax.numpy as jnp
import ml_dtypes
import numpy as np
from jax import lax
from jax.experimental import pallas as pl
from jax.experimental.pallas import tpu as pltpu
from jax.sharding import PartitionSpec as P

OUTER_FACTOR = 64
INNER_FACTOR = 128
ACTIVE_TONES = 4096
GUARD_SAMPLES = 1024
SMOOTH_HALFSPAN = 48
PSP = 12

TWO_PI = 2.0 * math.pi
ROOT_FORTYTWO = math.sqrt(42.0)
HIGHEST = lax.Precision.HIGHEST

WHOLE = OUTER_FACTOR * INNER_FACTOR
FOLD = 32
WIDE = WHOLE // FOLD
LANES = 128
ROWS = 8
LOWEST = (WHOLE - ACTIVE_TONES) // 2
RANGE_ROWS = GUARD_SAMPLES // LANES
VMEM_LIMIT = 48 * 1024 * 1024
SPECTRA_VMEM_LIMIT = 62 * 1024 * 1024


def split_table(table):
    high = table.astype(np.float32).astype(ml_dtypes.bfloat16)
    low = (table - high.astype(np.float64)).astype(np.float32).astype(ml_dtypes.bfloat16)
    return high, low


def turning(sign, product, period):
    angle = sign * TWO_PI / period * (product % period)
    cosine, sine = np.cos(angle), np.sin(angle)
    return np.block([[cosine, sine], [-sine, cosine]])


def residue_order():
    row = np.arange(FOLD)
    return row // 8 + 4 * (row % 8)


def spectrum_tables():
    b = np.arange(WIDE)
    j = LOWEST // FOLD + np.arange(ACTIVE_TONES // FOLD)
    high, low = split_table(turning(-1, b[:, None] * j[None, :], WIDE))
    angle = -TWO_PI / WHOLE * (residue_order()[:, None] * b[None, :])
    return high, low, np.stack([np.cos(angle), np.sin(angle)]).astype(np.float32)


def range_tables():
    j = np.arange(ACTIVE_TONES // FOLD)
    l = np.arange(LANES)
    high, low = split_table(turning(1, j[:, None] * l[None, :], ACTIVE_TONES // FOLD))
    angle = TWO_PI / ACTIVE_TONES * (residue_order()[:, None] * l[None, :])
    return high, low, np.stack([np.cos(angle), np.sin(angle)]).astype(np.float32)


def times(x, turn):
    re, im = x
    turn = turn % 1.0
    eighth = round(turn * 8)
    if abs(turn * 8 - eighth) < 1e-9:
        eighth %= 8
        if eighth % 2 == 0:
            return [(re, im), (-im, re), (-re, -im), (im, -re)][eighth // 2]
        half = math.sqrt(0.5)
        add, sub = (re + im) * half, (re - im) * half
        return [(sub, add), (-add, sub), (-sub, -add), (add, -sub)][eighth // 2]
    c, s = math.cos(TWO_PI * turn), math.sin(TWO_PI * turn)
    return re * c - im * s, re * s + im * c


def plus(x, y):
    return x[0] + y[0], x[1] + y[1]


def minus(x, y):
    return x[0] - y[0], x[1] - y[1]


def turn_quarter(x, sign):
    return (-x[1], x[0]) if sign > 0 else (x[1], -x[0])


def dft4(x, sign):
    a, b = plus(x[0], x[2]), minus(x[0], x[2])
    c, d = plus(x[1], x[3]), turn_quarter(minus(x[1], x[3]), sign)
    return [plus(a, c), plus(b, d), minus(a, c), minus(b, d)]


def dft8(x, sign):
    even, odd = dft4(x[0::2], sign), dft4(x[1::2], sign)
    odd = [times(o, sign * k / 8) for k, o in enumerate(odd)]
    return [plus(e, o) for e, o in zip(even, odd)] + [minus(e, o) for e, o in zip(even, odd)]


def dft3(x, sign):
    total, diff = plus(x[1], x[2]), minus(x[1], x[2])
    mid = (x[0][0] - 0.5 * total[0], x[0][1] - 0.5 * total[1])
    root = sign * math.sqrt(0.75)
    side = (-root * diff[1], root * diff[0])
    return [plus(x[0], total), plus(mid, side), minus(mid, side)]


def dft6(x, sign):
    even, odd = dft3(x[0::2], sign), dft3(x[1::2], sign)
    odd = [times(o, sign * k / 6) for k, o in enumerate(odd)]
    return [plus(e, o) for e, o in zip(even, odd)] + [minus(e, o) for e, o in zip(even, odd)]


def split_rows(x):
    high = x.astype(jnp.bfloat16)
    return high, (x - high.astype(jnp.float32)).astype(jnp.bfloat16)


def dot(x, w):
    return lax.dot_general(x, w, (((1,), (0,)), ((), ())), preferred_element_type=jnp.float32)


def spectrum_kernel(off_ref, x_hbm, high_hbm, low_hbm, twist_hbm, out_ref, x_ref, high_ref, low_ref, twist_ref, mid_ref, rows_ref, sems):
    symbols, groups = out_ref.shape[:2]
    tasks = [(m, g) for m in range(symbols) for g in range(groups)]
    fetches = []
    for n, (m, g) in enumerate(tasks):
        source = x_hbm.at[:, m, g * ROWS : (g + 1) * ROWS, :]
        fetches.append(pltpu.make_async_copy(source, x_ref.at[n], sems.at[3 + n]))
    tables = [
        pltpu.make_async_copy(source, target, sems.at[n])
        for n, (source, target) in enumerate([(twist_hbm, twist_ref), (high_hbm, high_ref), (low_hbm, low_ref)])
    ]
    fetches[0].start()
    for table in tables:
        table.start()
    for fetch in fetches[1:]:
        fetch.start()
    lane = lax.broadcasted_iota(jnp.int32, (ROWS, LANES), 1)
    halves = WIDE // LANES
    for n, (m, g) in enumerate(tasks):
        fetches[n].wait()
        off, slot = off_ref[m], n % 2

        def sample(part, chunk):
            value = x_ref[n, part, :, chunk * LANES : (chunk + 1) * LANES]
            if chunk * LANES < GUARD_SAMPLES:
                wrapped = x_ref[n, part, :, WHOLE + chunk * LANES : WHOLE + (chunk + 1) * LANES]
                value = jnp.where(lane < off - chunk * LANES, wrapped, value)
            return value

        for h in range(halves):
            for v in range(8):
                chunks = [halves * (8 * u + v) + h for u in range(4)]
                y = dft4([(sample(0, c), sample(1, c)) for c in chunks], -1)
                for p in range(4):
                    at = (slot, h, p, v)
                    mid_ref[at + (0,)], mid_ref[at + (1,)] = times(y[p], -v * p / FOLD)
        if n == 0:
            tables[0].wait()
        for p in range(4):
            for h in range(halves):
                at = (slot, h, p)
                y = dft8([(mid_ref[at + (v, 0)], mid_ref[at + (v, 1)]) for v in range(8)], -1)
                for q in range(0, 8, 2):
                    pair = []
                    for row in (p * 8 + q, p * 8 + q + 1):
                        re, im = y[row - p * 8]
                        c = twist_ref[0, row : row + 1, h * LANES : (h + 1) * LANES]
                        s = twist_ref[1, row : row + 1, h * LANES : (h + 1) * LANES]
                        pair.append((re * c - im * s, re * s + im * c))
                    at_rows = slice((p * 8 + q) * ROWS, (p * 8 + q + 2) * ROWS)
                    for part in range(2):
                        high, low = split_rows(jnp.concatenate([pair[0][part], pair[1][part]], axis=0))
                        column = part * WIDE + h * LANES
                        rows_ref[slot, at_rows, column : column + LANES] = high
                        rows_ref[slot, at_rows, 2 * WIDE + column : 2 * WIDE + column + LANES] = low
        if n == 0:
            tables[1].wait()
            tables[2].wait()
        high = rows_ref[slot, :, : 2 * WIDE]
        low = rows_ref[slot, :, 2 * WIDE :]
        out_ref[m, g] = dot(high, high_ref[...]) + dot(low, high_ref[...]) + dot(high, low_ref[...])


def symbol_phases(off_ref, symbols):
    tones = ACTIVE_TONES // FOLD
    row = lax.broadcasted_iota(jnp.int32, (ROWS, tones), 0)
    lane = lax.broadcasted_iota(jnp.int32, (ROWS, tones), 1)
    by_row = by_lane = jnp.zeros((ROWS, tones), jnp.int32)
    for m in range(symbols):
        by_row = jnp.where(row == m, off_ref[m], by_row)
        by_lane = jnp.where(lane == m, off_ref[m], by_lane)

    def phase(product):
        angle = (product & (WHOLE - 1)).astype(jnp.float32) * (TWO_PI / WHOLE)
        return jnp.cos(angle), jnp.sin(angle)

    return phase(by_row * (LOWEST + FOLD * lane)), [phase(by_lane * (p + 4 * row)) for p in range(4)]


def profile_kernel(
    blocks, scale, off_ref, pilot_ref, place_ref, s_ref, own_ref, other_ref, spot_ref, high_ref, low_ref, twist_ref, *refs
):
    outs = refs[:blocks]
    flat_ref, turned_ref, gain_ref, ratio_ref, num_ref, rows_ref, range_ref, prof_ref = refs[blocks:]
    symbols, groups = s_ref.shape[:2]
    tones = ACTIVE_TONES // FOLD
    own_place, swapped = place_ref[0], place_ref[1] > 0
    for j in range(FOLD // 2):
        at = slice(j * LANES, (j + 1) * LANES)
        own, other = own_ref[:, at], other_ref[:, at]
        flat_ref[j, :symbols] = jnp.where(swapped, other, own).astype(jnp.float32)
        flat_ref[FOLD // 2 + j, :symbols] = jnp.where(swapped, own, other).astype(jnp.float32)
    (lane_re, lane_im), row_phases = symbol_phases(off_ref, symbols)

    for m in range(symbols):
        slot = m % 2
        offset = pilot_ref[m]
        stood = flat_ref[:, m, :].T.astype(jnp.bfloat16)
        spread = dot(stood, spot_ref[...])
        turned_ref[slot] = sum(
            spread[FOLD * l : FOLD * (l + 1), tones * l : tones * (l + 1)] for l in range(LANES // FOLD)
        )
        row = lax.broadcasted_iota(jnp.int32, (ROWS, tones), 0)
        lane = lax.broadcasted_iota(jnp.int32, (ROWS, tones), 1)
        first_after = ACTIVE_TONES + lax.rem(offset + PSP * ACTIVE_TONES - ACTIVE_TONES, PSP)
        span = SMOOTH_HALFSPAN + 1
        for p in range(4):
            at = slice(p * 8, p * 8 + 8)
            index = turned_ref[slot, pl.ds(p, 8, stride=4), :]
            high_bits = jnp.floor(index * 0.125)
            level_re = 2.0 * (index - 8.0 * high_bits) - 7.0
            level_im = 2.0 * high_bits - 7.0
            factor = scale / (level_re * level_re + level_im * level_im)
            a, b = lane_re[m : m + 1, :], lane_im[m : m + 1, :]
            c, s = row_phases[p][0][:, m : m + 1], row_phases[p][1][:, m : m + 1]
            c, s = a * c - b * s, a * s + b * c
            gain_ref[slot, 0, at] = (c * level_re + s * level_im) * factor
            gain_ref[slot, 1, at] = (s * level_re - c * level_im) * factor
            k = p + 4 * row + FOLD * lane
            is_pilot = lax.rem(k + (PSP - offset), PSP) == 0
            total = jnp.where(is_pilot, 201.0, 200.0)
            for i in range(4):
                before = span - (k - offset + PSP * (i + 1))
                after = span - (first_after + PSP * i - k)
                total -= (jnp.maximum(before, 0) + jnp.maximum(after, 0)).astype(jnp.float32)
            gain_ref[slot, 2, at] = 1.0 / total
            gain_ref[slot, 3, at] = jnp.where(is_pilot, 1.0, 0.0)

        for g in range(groups):
            for i in range(FOLD):
                re = s_ref[m, g, i * ROWS : (i + 1) * ROWS, :tones]
                im = s_ref[m, g, i * ROWS : (i + 1) * ROWS, tones:]
                c = gain_ref[slot, 0, i : i + 1, :]
                s = gain_ref[slot, 1, i : i + 1, :]
                ratio_ref[slot, 0, i] = re * c - im * s
                ratio_ref[slot, 1, i] = re * s + im * c

            r = offset & 3
            for part in range(2):
                picked = [
                    ratio_ref[slot, part, r * 8 + a] * gain_ref[slot, 3, pl.ds(r * 8 + a, 1), :] for a in range(8)
                ]

                def pilot(i):
                    b, a = i // 8, i % 8
                    if b == 0:
                        return picked[a]
                    rolled = pltpu.roll(picked[a], (-b) % tones, 1)
                    return jnp.where((lane < tones - b) if b > 0 else (lane >= -b), rolled, 0.0)

                q = {i: pilot(i) for i in range(-13, 21)}
                slope = sum(q[i] for i in range(0, 12)) - sum(q[i] for i in range(-12, 0))
                value = sum((49 - 4 * abs(i + 1)) * q[i] for i in range(-13, 12))
                for a in range(-1, 8):
                    for s in range(4):
                        to = r + s
                        here = value if s == 0 else value + s * slope - q[a - 12]
                        num_ref[slot, part, (to & 3) * 10 + a + 1 + (to >> 2)] = here
                    value = value + 4.0 * slope - q[a - 12] + q[a + 13]
                    if a < 7:
                        slope = slope + q[a + 13] - 2.0 * q[a + 1] + q[a - 11]

            for i in range(0, FOLD, 2):
                for part in range(2):
                    pair = []
                    for n in (i, i + 1):
                        smooth = num_ref[slot, part, (n // 8) * 10 + n % 8 + 1] * gain_ref[slot, 2, n : n + 1, :]
                        pair.append(ratio_ref[slot, part, n] - smooth)
                    high, low = split_rows(jnp.concatenate(pair, axis=0))
                    at = slice(i * ROWS, (i + 2) * ROWS)
                    rows_ref[slot, at, part * tones : (part + 1) * tones] = high
                    rows_ref[slot, at, (2 + part) * tones : (3 + part) * tones] = low
            high = rows_ref[slot, :, : 2 * tones]
            low = rows_ref[slot, :, 2 * tones :]
            range_ref[slot] = dot(high, high_ref[...]) + dot(low, high_ref[...]) + dot(high, low_ref[...])

            sums = None
            for p in range(4):
                x = []
                for i in range(p * 8, p * 8 + 8):
                    re = range_ref[slot, i * ROWS : (i + 1) * ROWS, :LANES]
                    im = range_ref[slot, i * ROWS : (i + 1) * ROWS, LANES:]
                    c = twist_ref[0, i : i + 1, :]
                    s = twist_ref[1, i : i + 1, :]
                    x.append((re * c - im * s, re * s + im * c))
                y = [times(v, p * h / FOLD) for h, v in enumerate(dft8(x, 1))]
                sums = y if sums is None else [plus(a, b) for a, b in zip(sums, y)]
            if blocks == 1:
                for h in range(RANGE_ROWS):
                    outs[0][m, g, 0, h], outs[0][m, g, 1, h] = sums[h]
                continue
            for h in range(RANGE_ROWS):
                prof_ref[slot, 0, h], prof_ref[slot, 1, h] = sums[h]
            each = RANGE_ROWS // blocks
            for d in range(blocks):
                block = own_place ^ d
                for part in range(2):
                    for h in range(each):
                        outs[d][m, g, part, h] = prof_ref[slot, part, block * each + h]


def doppler_kernel(place_ref, *refs):
    pieces, outs, (turned_ref, spread_ref) = refs[:4], refs[4:8], refs[8:]
    own, rank = place_ref[0], place_ref[1]
    local_symbols, _, _, each = pieces[0].shape[:4]
    for d in range(4):
        for m in range(local_symbols):
            turned_ref[own ^ d, m] = pieces[d][m, 0]
    for h in range(each):
        grid = {}
        for m in range(local_symbols):
            x = [(turned_ref[s, m, 0, h], turned_ref[s, m, 1, h]) for s in range(4)]
            for p, y in enumerate(dft4(x, -1)):
                grid[p, m] = times(y, -m * p / (4 * local_symbols))
        for p in range(4):
            for q, y in enumerate(dft6([grid[p, m] for m in range(local_symbols)], -1)):
                f = p + 4 * q
                at = slice(h * LANES, (h + 1) * LANES)
                spread_ref[f // local_symbols, 0, f % local_symbols, :, at] = y[0]
                spread_ref[f // local_symbols, 1, f % local_symbols, :, at] = y[1]
    for d in range(4):
        outs[d][...] = spread_ref[rank ^ d]


def join_kernel(place_ref, *refs):
    pieces, out_ref = refs[:4], refs[4]
    own = place_ref[0]
    wide = pieces[0].shape[-1]
    for d in range(4):
        h = own ^ d
        rows = pl.ds(pl.multiple_of((h & 1) * ROWS, ROWS), ROWS)
        columns = pl.ds(pl.multiple_of((h >> 1) * wide, LANES), wide)
        out_ref[:, :, rows, columns] = pieces[d][...]


IN_VMEM = pl.BlockSpec(memory_space=pltpu.VMEM)
IN_SMEM = pl.BlockSpec(memory_space=pltpu.SMEM)
IN_HBM = pl.BlockSpec(memory_space=pltpu.HBM)


def spectra(windows, cp_offset):
    _, symbols, channels, record = windows.shape
    groups = channels // ROWS
    high, low, twist = spectrum_tables()
    tones = ACTIVE_TONES // FOLD
    return pl.pallas_call(
        spectrum_kernel,
        in_specs=[IN_SMEM] + [IN_HBM] * 4,
        out_specs=IN_VMEM,
        scratch_shapes=[
            pltpu.VMEM((symbols * groups, 2, ROWS, record), jnp.float32),
            pltpu.VMEM(high.shape, jnp.bfloat16),
            pltpu.VMEM(low.shape, jnp.bfloat16),
            pltpu.VMEM(twist.shape, jnp.float32),
            pltpu.VMEM((2, WIDE // LANES, 4, 8, 2, ROWS, LANES), jnp.float32),
            pltpu.VMEM((2, FOLD * ROWS, 4 * WIDE), jnp.bfloat16),
            pltpu.SemaphoreType.DMA((3 + symbols * groups,)),
        ],
        out_shape=jax.ShapeDtypeStruct((symbols, groups, FOLD * ROWS, 2 * tones), jnp.float32),
        compiler_params=pltpu.CompilerParams(vmem_limit_bytes=SPECTRA_VMEM_LIMIT),
        cost_estimate=pl.CostEstimate(flops=2 * 10**9, bytes_accessed=8 * 10**6, transcendentals=0),
        name="spectra",
    )(cp_offset, windows, high, low, twist)


def profiles(spectrum, own, other, pilot_offsets, cp_offset, places, blocks, scale):
    symbols, groups = spectrum.shape[:2]
    high, low, twist = range_tables()
    tones = ACTIVE_TONES // FOLD
    each = RANGE_ROWS // blocks
    n, column = np.arange(FOLD)[:, None], np.arange(LANES // FOLD * tones)[None, :]
    spot = (column % tones == LANES // FOLD * n + column // tones).astype(ml_dtypes.bfloat16)
    out = jax.ShapeDtypeStruct((symbols, groups, 2, each, ROWS, LANES), jnp.float32)
    return pl.pallas_call(
        functools.partial(profile_kernel, blocks, scale),
        in_specs=[IN_SMEM] * 3 + [IN_VMEM] * 7,
        out_specs=[IN_VMEM] * blocks,
        scratch_shapes=[
            pltpu.VMEM((FOLD, ROWS, LANES), jnp.float32),
            pltpu.VMEM((2, FOLD, tones), jnp.float32),
            pltpu.VMEM((2, 4, FOLD, tones), jnp.float32),
            pltpu.VMEM((2, 2, FOLD, ROWS, tones), jnp.float32),
            pltpu.VMEM((2, 2, 40, ROWS, tones), jnp.float32),
            pltpu.VMEM((2, FOLD * ROWS, 4 * tones), jnp.bfloat16),
            pltpu.VMEM((2, FOLD * ROWS, 2 * LANES), jnp.float32),
            pltpu.VMEM((2, 2, RANGE_ROWS, ROWS, LANES), jnp.float32),
        ],
        out_shape=[out] * blocks,
        compiler_params=pltpu.CompilerParams(vmem_limit_bytes=VMEM_LIMIT),
        cost_estimate=pl.CostEstimate(flops=10**9, bytes_accessed=4 * 10**6, transcendentals=0),
        name="profiles",
    )(cp_offset, pilot_offsets, places, spectrum, own, other, spot, high, low, twist)


def doppler_plain(own_profiles, symbols):
    turned = lax.all_to_all(own_profiles, "sub", split_axis=3, concat_axis=1, tiled=True)
    turned = lax.all_to_all(turned, "sym", split_axis=3, concat_axis=2, tiled=True)
    ids = np.arange(symbols)
    angle = TWO_PI / symbols * (ids[:, None] * ids[None, :] % symbols)
    c, s = np.cos(angle).astype(np.float32), np.sin(angle).astype(np.float32)
    product = lambda t, x: jnp.einsum("fm,cmq->cfq", t, x, precision=HIGHEST)
    re = product(c, turned[0]) + product(s, turned[1])
    im = product(c, turned[1]) - product(s, turned[0])
    return lax.all_to_all(jnp.stack([re, im]), "sym", split_axis=2, concat_axis=3, tiled=True)


def doppler_paired(pieces, place, rank, syms, subs):
    share = syms // subs
    got = [pieces[0]] + [
        lax.ppermute(pieces[d], "sym", [(i, i ^ d) for i in range(syms)]) for d in range(1, syms)
    ]
    symbols, _, _, each = got[0].shape[:4]
    piece = jax.ShapeDtypeStruct((2, symbols, ROWS, each * LANES), jnp.float32)
    spread = pl.pallas_call(
        doppler_kernel,
        in_specs=[IN_SMEM] + [IN_VMEM] * syms,
        out_specs=[IN_VMEM] * syms,
        out_shape=[piece] * syms,
        scratch_shapes=[
            pltpu.VMEM((syms, symbols, 2, each, ROWS, LANES), jnp.float32),
            pltpu.VMEM((syms,) + piece.shape, jnp.float32),
        ],
        compiler_params=pltpu.CompilerParams(vmem_limit_bytes=VMEM_LIMIT),
        name="doppler",
    )(jnp.stack([place, rank]), *got)
    joined = []
    for d in range(syms):
        route = [
            (s * subs + u, (((s % share) * subs + u) ^ d) * subs + s // share)
            for s in range(syms)
            for u in range(subs)
        ]
        joined.append(lax.ppermute(spread[d], ("sym", "sub"), route))
    out = pl.pallas_call(
        join_kernel,
        in_specs=[IN_SMEM] + [IN_VMEM] * syms,
        out_specs=IN_VMEM,
        out_shape=jax.ShapeDtypeStruct((2, symbols, subs * ROWS, share * each * LANES), jnp.float32),
        compiler_params=pltpu.CompilerParams(vmem_limit_bytes=VMEM_LIMIT),
        name="join",
    )(place[None], *joined)
    return jnp.transpose(out, (0, 2, 1, 3))


def local(samples, constellation_index, pilot_offsets, cp_offset):
    syms, subs = lax.axis_size("sym"), lax.axis_size("sub")
    place, sub = lax.axis_index("sym"), lax.axis_index("sub")
    channels, symbols = samples.shape[1:3]
    paired = syms == 4 and subs == 2 and channels == ROWS and symbols == 6
    half = ACTIVE_TONES // 2
    if paired:
        own = constellation_index
        other = lax.ppermute(own, "sub", [(0, 1), (1, 0)])
        swapped = sub
    else:
        index = lax.all_gather(constellation_index, "sub", axis=1, tiled=True)
        own, other, swapped = index[:, :half], index[:, half:], jnp.zeros_like(sub)
    windows = jnp.transpose(samples, (0, 2, 1, 3))
    short = -channels % ROWS
    if short:
        windows = jnp.pad(windows, ((0, 0), (0, 0), (0, short), (0, 0)))
    spectrum = spectra(windows, cp_offset)
    scale = ROOT_FORTYTWO / math.sqrt(WHOLE * ACTIVE_TONES * symbols * syms)
    places = jnp.stack([place, swapped])
    blocks = syms if paired else 1
    got = profiles(spectrum, own, other, pilot_offsets, cp_offset, places, blocks, scale)
    if paired:
        rank = (place % (syms // subs)) * subs + sub
        return doppler_paired(got, place, rank, syms, subs)
    own = jnp.transpose(got[0], (2, 1, 4, 0, 3, 5))
    own = own.reshape(2, channels + short, symbols, GUARD_SAMPLES)[:, :channels]
    return doppler_plain(own, symbols * syms)


def solution(mesh):
    return jax.shard_map(
        local,
        mesh=mesh,
        in_specs=(
            P(None, ("chan", "sub"), "sym", None),
            P(("chan", "sym"), "sub"),
            P("sym"),
            P(("chan", "sym")),
        ),
        out_specs=P(None, "chan", "sym", "sub"),
        check_vma=False,
    )
```

time: 53 us -> 45.1 us (0.85)
  blocking collectives: 7.12 us -> 0 us
  local copies, waits for them, and re-layouts: 7.97 us -> 1.44 us
  starting transfers between devices: 14.7 us -> 17.7 us
  Pallas kernels: 10.4 us -> 12.8 us
  waiting for transfers between devices: 11.4 us -> 12.8 us
  other arithmetic: 0.92 us -> 0.15 us
    all_gather x1 -> x0, blocking collectives: 7.12 us -> none  [local(): index = lax.all_gather(index, 'sub', axis=2, tiled=True)]
    unnamed x18 -> x16, local copies, waits for them, and re-layouts: 5.42 us -> 1.44 us
    ppermute x0 -> x1, starting transfers between devices: none -> 2.97 us  [local(): other = lax.ppermute(own, 'sub', [(0, 1), (1, 0)])]
    convert_element_type x3 -> x0, local copies, waits for them, and re-layouts: 2.39 us -> none  [local(): index = index.reshape(symbols, FOLD, -1).astype(jnp.bfloat16)]
    pallas_call x4, Pallas kernels: 10.4 us -> 12.8 us  [the longest x1 7.59 us: spectra(): pl.pallas_call(spectrum_kernel, in_specs=[IN_SMEM] + [IN_HBM] * 4, out_sp...]
    ppermute x4, waiting for transfers between devices: 4.48 us -> 5.53 us  [doppler_paired(): joined.append(lax.ppermute(spread[d], ('sym', 'sub'), route))]
    convert_element_type x1 -> x0, other arithmetic: 0.84 us -> none  [local(): index = index.reshape(symbols, FOLD, -1).astype(jnp.bfloat16)]
  transfers between devices with their start and end apart: 7 -> 8, of which waited for: 4 -> 4; matrix products, arithmetic and copies ran while one was open for 0% -> 0% of each run, Pallas kernels for 0% -> 17%
where the time goes in v2:
time: 45.1 us; the launch traced here: 45 us
  starting transfers between devices  17.7 us (39%)
  Pallas kernels  12.8 us (28%)
  waiting for transfers between devices  12.8 us (28%)
  local copies, waits for them, and re-layouts  1.44 us (3%)
    ppermute x4, starting transfers between devices, doppler_paired(): joined.append(lax.ppermute(spread[d], ('sym', 'sub'), route))  10.3 us
    pallas_call x1, Pallas kernels, spectra(): pl.pallas_call(spectrum_kernel, in_specs=[IN_SMEM] + [IN_HBM] * 4, out_sp...  7.59 us
    ppermute x3, waiting for transfers between devices, doppler_paired(): lax.ppermute(pieces[d], 'sym', [(i, i ^ d) for i in range(syms)])  7.26 us
    ppermute x4, waiting for transfers between devices, doppler_paired(): joined.append(lax.ppermute(spread[d], ('sym', 'sub'), route))  5.53 us
    ppermute x3, starting transfers between devices, doppler_paired(): lax.ppermute(pieces[d], 'sym', [(i, i ^ d) for i in range(syms)])  4.45 us
    pallas_call x1, Pallas kernels, profiles(): pl.pallas_call(functools.partial(profile_kernel, blocks, scale), in_specs...  3.69 us
    ppermute x1, starting transfers between devices, local(): other = lax.ppermute(own, 'sub', [(0, 1), (1, 0)])  2.97 us
    unnamed x16, local copies, waits for them, and re-layouts  1.44 us
  transfers between devices with their start and end apart: 8, of which 4 were waited for; matrix products, arithmetic and copies ran while one was open for 0% of the time, Pallas kernels for 17%

profile of v2, /device:TPU:0, one launch (start us, length us, event | category | flops | bytes accessed | tf_op | source)
XLA Modules:
  0.0 45.0 jit_solution(701724610565961658)
XLA Ops:
  0.0 3.0 %collective-permute-start = (s32[6,2048]{1,0:T(8,128)}, s32[6,2048]{1,0:T(8,128)S(1)}, u32[]{:S(2)}, u32[]{:S(2)}) collective-permute-start(s32[6,2048]{1,0:T(8,128)} %own_ref.1), channel_id=1, source_target_pairs={{0,1},{1,0},{2,3},{3,2},{4,5},{5,4},{6,7},{7,6},{8,9},{9,8},{10,11... | collective-permute-start | bytes 147464 | tf_op jit(solution)/shard_map/ppermute | solution.py:482
  3.0 0.0 copy-start.4
  3.0 0.0 copy-start.5
  3.0 0.0 copy-start.6
  3.0 7.6 %spectra.1.s_ref = f32[6,1,256,256]{3,2,1,0:T(8,128)} custom-call(s32[6]{0:T(128)} %off_ref.3, f32[2,6,8,9216]{3,2,1,0:T(8,128)} %bitcast.5, bf16[512,256]{1,0:T(8,128)(2,1)} %constant.35.clone.high_hbm, bf16[512,256]{1,0:T(8,128)(2,1)} %constant.36.clone.low_hbm, f32[2,32,256]{2,1,0:T(8,128)} %constant.37.clone.twist_hbm), custom_call_target="tpu_custom_call" | custom-call | flops 2000000000 | bytes 8000000 | tf_op jit(solution)/shard_map/spectra/pallas_call | solution.py:375
  10.6 0.1 pad_add_fusion.1.place_ref
  10.7 0.0 collective-permute-done.other_ref
  10.8 1.4 %copy-done.7 = f32[6,1,256,256]{3,2,1,0:T(8,128)S(1)} copy-done((f32[6,1,256,256]{3,2,1,0:T(8,128)S(1)}, f32[6,1,256,256]{3,2,1,0:T(8,128)}, u32[]{:S(2)}) %copy-start.7) | copy-done | bytes 1572888
  12.2 3.7 %profiles.1 = (f32[6,1,2,2,8,128]{5,4,3,2,1,0:T(8,128)S(1)}, f32[6,1,2,2,8,128]{5,4,3,2,1,0:T(8,128)S(1)}, f32[6,1,2,2,8,128]{5,4,3,2,1,0:T(8,128)S(1)}, f32[6,1,2,2,8,128]{5,4,3,2,1,0:T(8,128)S(1)}) custom-call(s32[6]{0:T(128)S(1)} %copy-done.1, s32[6]{0:T(128)S(1)} %copy-done.2, s32[2]{0:T(128)S(1)} %pad_add_fusion.1.place_ref, ...), custom_call_target="tpu_custom_call" | custom-call | flops 1000000000 | bytes 4000000 | tf_op jit(solution)/shard_map/profiles/pallas_call | solution.py:403
  15.9 1.6 %collective-permute-start.1 = (f32[6,1,2,2,8,128]{5,4,3,2,1,0:T(8,128)S(1)}, f32[6,1,2,2,8,128]{5,4,3,2,1,0:T(8,128)S(1)}, u32[]{:S(2)}, u32[]{:S(2)}) collective-permute-start(f32[6,1,2,2,8,128]{5,4,3,2,1,0:T(8,128)S(1)} %get-tuple-element.14), channel_id=1, source_target_pairs={{0,2},{2,0},{4,6},{6,4},{1,3},{3,1},{5,7},{7,5},{8,10},{10,8},{12,... | collective-permute-start | bytes 294920 | tf_op jit(solution)/shard_map/ppermute | solution.py:439
  17.5 2.6 %collective-permute-start.2 = (f32[6,1,2,2,8,128]{5,4,3,2,1,0:T(8,128)S(1)}, f32[6,1,2,2,8,128]{5,4,3,2,1,0:T(8,128)S(1)}, u32[]{:S(2)}, u32[]{:S(2)}) collective-permute-start(f32[6,1,2,2,8,128]{5,4,3,2,1,0:T(8,128)S(1)} %get-tuple-element.15), channel_id=1, source_target_pairs={{0,4},{2,6},{4,0},{6,2},{1,5},{3,7},{5,1},{7,3},{8,12},{10,14},{12... | collective-permute-start | bytes 294920 | tf_op jit(solution)/shard_map/ppermute | solution.py:439
  20.1 0.2 collective-permute-start.3
  20.3 0.1 pad_add_fusion.place_ref
  20.4 1.1 %collective-permute-done.1.refs_1_ = f32[6,1,2,2,8,128]{5,4,3,2,1,0:T(8,128)S(1)} collective-permute-done((f32[6,1,2,2,8,128]{5,4,3,2,1,0:T(8,128)S(1)}, f32[6,1,2,2,8,128]{5,4,3,2,1,0:T(8,128)S(1)}, u32[]{:S(2)}, u32[]{:S(2)}) %collective-permute-start.1) | collective-permute-done | bytes 98336 | tf_op jit(solution)/shard_map/ppermute | solution.py:439
  21.5 6.1 %collective-permute-done.2.refs_2_ = f32[6,1,2,2,8,128]{5,4,3,2,1,0:T(8,128)S(1)} collective-permute-done((f32[6,1,2,2,8,128]{5,4,3,2,1,0:T(8,128)S(1)}, f32[6,1,2,2,8,128]{5,4,3,2,1,0:T(8,128)S(1)}, u32[]{:S(2)}, u32[]{:S(2)}) %collective-permute-start.2) | collective-permute-done | bytes 98336 | tf_op jit(solution)/shard_map/ppermute | solution.py:439
  27.6 0.7 %doppler.1 = (f32[2,6,8,256]{3,2,1,0:T(8,128)S(1)}, f32[2,6,8,256]{3,2,1,0:T(8,128)S(1)}, f32[2,6,8,256]{3,2,1,0:T(8,128)S(1)}, f32[2,6,8,256]{3,2,1,0:T(8,128)S(1)}) custom-call(s32[2]{0:T(128)S(1)} %pad_add_fusion.place_ref, f32[6,1,2,2,8,128]{5,4,3,2,1,0:T(8,128)S(1)} %get-tuple-element.13.refs_0_, ...), custom_call_target="tpu_custom_call" | custom-call | tf_op jit(solution)/shard_map/doppler/pallas_call | solution.py:443
  28.4 0.7 %collective-permute-start.4 = (f32[2,6,8,256]{3,2,1,0:T(8,128)S(1)}, f32[2,6,8,256]{3,2,1,0:T(8,128)S(1)}, u32[]{:S(2)}, u32[]{:S(2)}) collective-permute-start(f32[2,6,8,256]{3,2,1,0:T(8,128)S(1)} %get-tuple-element.17), channel_id=1, source_target_pairs={{0,0},{1,2},{2,4},{3,6},{4,1},{5,3},{6,5},{7,7},{8,8},{9,10},{10,1... | collective-permute-start | bytes 294920 | tf_op jit(solution)/shard_map/ppermute | solution.py:462
  29.0 4.5 %collective-permute-start.5 = (f32[2,6,8,256]{3,2,1,0:T(8,128)S(1)}, f32[2,6,8,256]{3,2,1,0:T(8,128)S(1)}, u32[]{:S(2)}, u32[]{:S(2)}) collective-permute-start(f32[2,6,8,256]{3,2,1,0:T(8,128)S(1)} %get-tuple-element.18), channel_id=1, source_target_pairs={{0,2},{1,0},{2,6},{3,4},{4,3},{5,1},{6,7},{7,5},{8,10},{9,8},{10,1... | collective-permute-start | bytes 294920 | tf_op jit(solution)/shard_map/ppermute | solution.py:462
  33.5 2.2 %collective-permute-start.6 = (f32[2,6,8,256]{3,2,1,0:T(8,128)S(1)}, f32[2,6,8,256]{3,2,1,0:T(8,128)S(1)}, u32[]{:S(2)}, u32[]{:S(2)}) collective-permute-start(f32[2,6,8,256]{3,2,1,0:T(8,128)S(1)} %get-tuple-element.19), channel_id=1, source_target_pairs={{0,4},{1,6},{2,0},{3,2},{4,5},{5,7},{6,1},{7,3},{8,12},{9,14},{10,... | collective-permute-start | bytes 294920 | tf_op jit(solution)/shard_map/ppermute | solution.py:462
  35.7 2.9 %collective-permute-start.7 = (f32[2,6,8,256]{3,2,1,0:T(8,128)S(1)}, f32[2,6,8,256]{3,2,1,0:T(8,128)S(1)}, u32[]{:S(2)}, u32[]{:S(2)}) collective-permute-start(f32[2,6,8,256]{3,2,1,0:T(8,128)S(1)} %get-tuple-element.20), channel_id=1, source_target_pairs={{0,6},{1,4},{2,2},{3,0},{4,7},{5,5},{6,3},{7,1},{8,14},{9,12},{10,... | collective-permute-start | bytes 294920 | tf_op jit(solution)/shard_map/ppermute | solution.py:462
  38.6 0.0 collective-permute-done.5.refs_1_
  38.7 0.2 collective-permute-done.6.refs_2_
  38.9 5.3 %collective-permute-done.7.refs_3_ = f32[2,6,8,256]{3,2,1,0:T(8,128)S(1)} collective-permute-done((f32[2,6,8,256]{3,2,1,0:T(8,128)S(1)}, f32[2,6,8,256]{3,2,1,0:T(8,128)S(1)}, u32[]{:S(2)}, u32[]{:S(2)}) %collective-permute-start.7) | collective-permute-done | bytes 98336 | tf_op jit(solution)/shard_map/ppermute | solution.py:462
  44.2 0.8 %join.1 = f32[2,6,16,512]{3,2,1,0:T(8,128)} custom-call(s32[1]{0:T(128)} %bitcast.place_ref, f32[2,6,8,256]{3,2,1,0:T(8,128)S(1)} %collective-permute-done.4.refs_0_, f32[2,6,8,256]{3,2,1,0:T(8,128)S(1)} %collective-permute-done.5.refs_1_, f32[2,6,8,256]{3,2,1,0:T(8,128)S(1)} %collective-permute-done.6.refs_2_, ...), custom_call_target="tpu_custom_call" | custom-call | tf_op jit(solution)/shard_map/join/pallas_call | solution.py:463
  (14 shorter events, 0.0 us)
Async XLA Ops:
  0.0 10.7 %collective-permute-start = (s32[6,2048]{1,0:T(8,128)}, s32[6,2048]{1,0:T(8,128)S(1)}, u32[]{:S(2)}, u32[]{:S(2)}) collective-permute-start(s32[6,2048]{1,0:T(8,128)} %own_ref.1), channel_id=1, source_target_pairs={{0,1},{1,0},{2,3},{3,2},{4,5},{5,4},{6,7},{7,6},{8,9},{9,8},{10,11... | collective-permute-start | bytes 147464 | tf_op jit(solution)/shard_map/ppermute | solution.py:482
  3.0 7.7 %copy-start = (s32[6,2048]{1,0:T(8,128)S(1)}, s32[6,2048]{1,0:T(8,128)}, u32[]{:S(2)}) copy-start(s32[6,2048]{1,0:T(8,128)} %own_ref.1) | copy-start | bytes 147460
  3.0 7.7 %copy-start.1 = (s32[6]{0:T(128)S(1)}, s32[6]{0:T(128)}, u32[]{:S(2)}) copy-start(s32[6]{0:T(128)} %off_ref.3) | copy-start | bytes 76
  3.0 7.7 %copy-start.2 = (s32[6]{0:T(128)S(1)}, s32[6]{0:T(128)}, u32[]{:S(2)}) copy-start(s32[6]{0:T(128)} %pilot_ref.1) | copy-start | bytes 76
  3.0 7.7 %copy-start.3 = (bf16[256,256]{1,0:T(8,128)(2,1)S(1)}, bf16[256,256]{1,0:T(8,128)(2,1)}, u32[]{:S(2)}) copy-start(bf16[256,256]{1,0:T(8,128)(2,1)} %constant.40.clone.low_ref) | copy-start | bytes 393220
  3.0 7.7 %copy-start.4 = (bf16[256,256]{1,0:T(8,128)(2,1)S(1)}, bf16[256,256]{1,0:T(8,128)(2,1)}, u32[]{:S(2)}) copy-start(bf16[256,256]{1,0:T(8,128)(2,1)} %constant.39.clone.high_ref) | copy-start | bytes 393220
  3.0 7.7 %copy-start.5 = (f32[2,32,128]{2,1,0:T(8,128)S(1)}, f32[2,32,128]{2,1,0:T(8,128)}, u32[]{:S(2)}) copy-start(f32[2,32,128]{2,1,0:T(8,128)} %constant.41.clone.twist_ref) | copy-start | bytes 98308
  3.0 7.7 %copy-start.6 = (bf16[32,512]{1,0:T(8,128)(2,1)S(1)}, bf16[32,512]{1,0:T(8,128)(2,1)}, u32[]{:S(2)}) copy-start(bf16[32,512]{1,0:T(8,128)(2,1)} %constant.38.clone.spot_ref) | copy-start | bytes 98308
  10.8 1.4 %copy-start.7 = (f32[6,1,256,256]{3,2,1,0:T(8,128)S(1)}, f32[6,1,256,256]{3,2,1,0:T(8,128)}, u32[]{:S(2)}) copy-start(f32[6,1,256,256]{3,2,1,0:T(8,128)} %spectra.1.s_ref) | copy-start | bytes 4718596
  15.9 5.7 %collective-permute-start.1 = (f32[6,1,2,2,8,128]{5,4,3,2,1,0:T(8,128)S(1)}, f32[6,1,2,2,8,128]{5,4,3,2,1,0:T(8,128)S(1)}, u32[]{:S(2)}, u32[]{:S(2)}) collective-permute-start(f32[6,1,2,2,8,128]{5,4,3,2,1,0:T(8,128)S(1)} %get-tuple-element.14), channel_id=1, source_target_pairs={{0,2},{2,0},{4,6},{6,4},{1,3},{3,1},{5,7},{7,5},{8,10},{10,8},{12,... | collective-permute-start | bytes 294920 | tf_op jit(solution)/shard_map/ppermute | solution.py:439
  17.5 10.1 %collective-permute-start.2 = (f32[6,1,2,2,8,128]{5,4,3,2,1,0:T(8,128)S(1)}, f32[6,1,2,2,8,128]{5,4,3,2,1,0:T(8,128)S(1)}, u32[]{:S(2)}, u32[]{:S(2)}) collective-permute-start(f32[6,1,2,2,8,128]{5,4,3,2,1,0:T(8,128)S(1)} %get-tuple-element.15), channel_id=1, source_target_pairs={{0,4},{2,6},{4,0},{6,2},{1,5},{3,7},{5,1},{7,3},{8,12},{10,14},{12... | collective-permute-start | bytes 294920 | tf_op jit(solution)/shard_map/ppermute | solution.py:439
  20.1 7.6 %collective-permute-start.3 = (f32[6,1,2,2,8,128]{5,4,3,2,1,0:T(8,128)S(1)}, f32[6,1,2,2,8,128]{5,4,3,2,1,0:T(8,128)S(1)}, u32[]{:S(2)}, u32[]{:S(2)}) collective-permute-start(f32[6,1,2,2,8,128]{5,4,3,2,1,0:T(8,128)S(1)} %get-tuple-element.16), channel_id=1, source_target_pairs={{0,6},{2,4},{4,2},{6,0},{1,7},{3,5},{5,3},{7,1},{8,14},{10,12},{12... | collective-permute-start | bytes 294920 | tf_op jit(solution)/shard_map/ppermute | solution.py:439
  28.4 10.3 %collective-permute-start.4 = (f32[2,6,8,256]{3,2,1,0:T(8,128)S(1)}, f32[2,6,8,256]{3,2,1,0:T(8,128)S(1)}, u32[]{:S(2)}, u32[]{:S(2)}) collective-permute-start(f32[2,6,8,256]{3,2,1,0:T(8,128)S(1)} %get-tuple-element.17), channel_id=1, source_target_pairs={{0,0},{1,2},{2,4},{3,6},{4,1},{5,3},{6,5},{7,7},{8,8},{9,10},{10,1... | collective-permute-start | bytes 294920 | tf_op jit(solution)/shard_map/ppermute | solution.py:462
  29.0 9.6 %collective-permute-start.5 = (f32[2,6,8,256]{3,2,1,0:T(8,128)S(1)}, f32[2,6,8,256]{3,2,1,0:T(8,128)S(1)}, u32[]{:S(2)}, u32[]{:S(2)}) collective-permute-start(f32[2,6,8,256]{3,2,1,0:T(8,128)S(1)} %get-tuple-element.18), channel_id=1, source_target_pairs={{0,2},{1,0},{2,6},{3,4},{4,3},{5,1},{6,7},{7,5},{8,10},{9,8},{10,1... | collective-permute-start | bytes 294920 | tf_op jit(solution)/shard_map/ppermute | solution.py:462
  33.5 5.4 %collective-permute-start.6 = (f32[2,6,8,256]{3,2,1,0:T(8,128)S(1)}, f32[2,6,8,256]{3,2,1,0:T(8,128)S(1)}, u32[]{:S(2)}, u32[]{:S(2)}) collective-permute-start(f32[2,6,8,256]{3,2,1,0:T(8,128)S(1)} %get-tuple-element.19), channel_id=1, source_target_pairs={{0,4},{1,6},{2,0},{3,2},{4,5},{5,7},{6,1},{7,3},{8,12},{9,14},{10,... | collective-permute-start | bytes 294920 | tf_op jit(solution)/shard_map/ppermute | solution.py:462
  35.7 8.5 %collective-permute-start.7 = (f32[2,6,8,256]{3,2,1,0:T(8,128)S(1)}, f32[2,6,8,256]{3,2,1,0:T(8,128)S(1)}, u32[]{:S(2)}, u32[]{:S(2)}) collective-permute-start(f32[2,6,8,256]{3,2,1,0:T(8,128)S(1)} %get-tuple-element.20), channel_id=1, source_target_pairs={{0,6},{1,4},{2,2},{3,0},{4,7},{5,5},{6,3},{7,1},{8,14},{9,12},{10,... | collective-permute-start | bytes 294920 | tf_op jit(solution)/shard_map/ppermute | solution.py:462

commit v3 on v2

--- a/solution.py
+++ b/solution.py
@@ -29,7 +29,7 @@
 LOWEST = (WHOLE - ACTIVE_TONES) // 2
 RANGE_ROWS = GUARD_SAMPLES // LANES
 VMEM_LIMIT = 48 * 1024 * 1024
-SPECTRA_VMEM_LIMIT = 62 * 1024 * 1024
+SPECTRA_VMEM_LIMIT = 52 * 1024 * 1024
 
 
 def split_table(table):
@@ -47,14 +47,6 @@
 def residue_order():
     row = np.arange(FOLD)
     return row // 8 + 4 * (row % 8)
-
-
-def spectrum_tables():
-    b = np.arange(WIDE)
-    j = LOWEST // FOLD + np.arange(ACTIVE_TONES // FOLD)
-    high, low = split_table(turning(-1, b[:, None] * j[None, :], WIDE))
-    angle = -TWO_PI / WHOLE * (residue_order()[:, None] * b[None, :])
-    return high, low, np.stack([np.cos(angle), np.sin(angle)]).astype(np.float32)
 
 
 def range_tables():
@@ -127,27 +119,73 @@
     return lax.dot_general(x, w, (((1,), (0,)), ((), ())), preferred_element_type=jnp.float32)
 
 
-def spectrum_kernel(off_ref, x_hbm, high_hbm, low_hbm, twist_hbm, out_ref, x_ref, high_ref, low_ref, twist_ref, mid_ref, rows_ref, sems):
+def split_product(rows_ref, high_ref, low_ref):
+    width = high_ref.shape[0]
+    high, low = rows_ref[:, :width], rows_ref[:, width:]
+    return dot(high, high_ref[...]) + dot(low, high_ref[...]) + dot(high, low_ref[...])
+
+
+def code_scale(peak):
+    return jnp.ceil(jnp.log2(jnp.maximum(peak, 1e-30)) * 64.0)
+
+
+def encode(x, code):
+    size = jnp.sqrt(jnp.abs(x)) * (32767.0 * jnp.exp2(code * (-1.0 / 128.0))) + 0.5
+    return jnp.where(x < 0.0, -size, size).astype(jnp.int32)
+
+
+def decode(n, code):
+    n = n.astype(jnp.int32).astype(jnp.float32)
+    return n * jnp.abs(n) * (jnp.exp2(code * (1.0 / 64.0)) * (1.0 / 32767.0**2))
+
+
+def peak_of(values):
+    top = functools.reduce(jnp.maximum, [jnp.abs(v) for v in values])
+    return jnp.max(top, axis=1, keepdims=True)
+
+
+def phase(product, period):
+    n = product & (period - 1)
+    quarter = (n + period // 8) // (period // 4)
+    x = (n - quarter * (period // 4)).astype(jnp.float32) * (TWO_PI / period)
+    y = x * x
+    sine = x * (1 + y * (-1 / 6 + y * (1 / 120 + y * (-1 / 5040 + y * (1 / 362880)))))
+    cosine = 1 + y * (-1 / 2 + y * (1 / 24 + y * (-1 / 720 + y * (1 / 40320 - y * (1 / 3628800)))))
+    odd, low, turned = (quarter & 1) == 1, (quarter & 2) == 2, ((quarter + 1) & 2) == 2
+    c, s = jnp.where(odd, sine, cosine), jnp.where(odd, cosine, sine)
+    return jnp.where(turned, -c, c), jnp.where(low, -s, s)
+
+
+def spectrum_kernel(off_ref, x_hbm, out_ref, x_ref, high_ref, low_ref, twist_ref, mid_ref, rows_ref, sems):
     symbols, groups = out_ref.shape[:2]
+    tones = ACTIVE_TONES // FOLD
     tasks = [(m, g) for m in range(symbols) for g in range(groups)]
     fetches = []
     for n, (m, g) in enumerate(tasks):
         source = x_hbm.at[:, m, g * ROWS : (g + 1) * ROWS, :]
-        fetches.append(pltpu.make_async_copy(source, x_ref.at[n], sems.at[3 + n]))
-    tables = [
-        pltpu.make_async_copy(source, target, sems.at[n])
-        for n, (source, target) in enumerate([(twist_hbm, twist_ref), (high_hbm, high_ref), (low_hbm, low_ref)])
-    ]
-    fetches[0].start()
-    for table in tables:
-        table.start()
-    for fetch in fetches[1:]:
-        fetch.start()
+        fetches.append(pltpu.make_async_copy(source, x_ref.at[n], sems.at[n]))
+        fetches[-1].start()
+    row = lax.broadcasted_iota(jnp.int32, (ROWS, WIDE), 0)
+    lane = lax.broadcasted_iota(jnp.int32, (ROWS, WIDE), 1)
+    for p in range(4):
+        c, s = phase((p + 4 * row) * lane, WHOLE)
+        twist_ref[0, p * 8 : p * 8 + 8], twist_ref[1, p * 8 : p * 8 + 8] = c, -s
+    row = lax.broadcasted_iota(jnp.int32, (2 * ROWS, tones), 0)
+    lane = lax.broadcasted_iota(jnp.int32, (2 * ROWS, tones), 1)
+    for b in range(0, WIDE, 2 * ROWS):
+        c, s = phase((b + row) * (LOWEST // FOLD + lane), WIDE)
+        upper, lower = slice(b, b + 2 * ROWS), slice(WIDE + b, WIDE + b + 2 * ROWS)
+        (c, c_low), (s, s_low) = split_rows(c), split_rows(s)
+        high_ref[upper, :tones], high_ref[upper, tones:] = c, -s
+        high_ref[lower, :tones], high_ref[lower, tones:] = s, c
+        low_ref[upper, :tones], low_ref[upper, tones:] = c_low, -s_low
+        low_ref[lower, :tones], low_ref[lower, tones:] = s_low, c_low
     lane = lax.broadcasted_iota(jnp.int32, (ROWS, LANES), 1)
     halves = WIDE // LANES
     for n, (m, g) in enumerate(tasks):
         fetches[n].wait()
         off, slot = off_ref[m], n % 2
+        base = n * FOLD * ROWS
 
         def sample(part, chunk):
             value = x_ref[n, part, :, chunk * LANES : (chunk + 1) * LANES]
@@ -163,8 +201,6 @@
                 for p in range(4):
                     at = (slot, h, p, v)
                     mid_ref[at + (0,)], mid_ref[at + (1,)] = times(y[p], -v * p / FOLD)
-        if n == 0:
-            tables[0].wait()
         for p in range(4):
             for h in range(halves):
                 at = (slot, h, p)
@@ -176,18 +212,13 @@
                         c = twist_ref[0, row : row + 1, h * LANES : (h + 1) * LANES]
                         s = twist_ref[1, row : row + 1, h * LANES : (h + 1) * LANES]
                         pair.append((re * c - im * s, re * s + im * c))
-                    at_rows = slice((p * 8 + q) * ROWS, (p * 8 + q + 2) * ROWS)
+                    at_rows = slice(base + (p * 8 + q) * ROWS, base + (p * 8 + q + 2) * ROWS)
                     for part in range(2):
                         high, low = split_rows(jnp.concatenate([pair[0][part], pair[1][part]], axis=0))
                         column = part * WIDE + h * LANES
-                        rows_ref[slot, at_rows, column : column + LANES] = high
-                        rows_ref[slot, at_rows, 2 * WIDE + column : 2 * WIDE + column + LANES] = low
-        if n == 0:
-            tables[1].wait()
-            tables[2].wait()
-        high = rows_ref[slot, :, : 2 * WIDE]
-        low = rows_ref[slot, :, 2 * WIDE :]
-        out_ref[m, g] = dot(high, high_ref[...]) + dot(low, high_ref[...]) + dot(high, low_ref[...])
+                        rows_ref[at_rows, column : column + LANES] = high
+                        rows_ref[at_rows, 2 * WIDE + column : 2 * WIDE + column + LANES] = low
+    out_ref[...] = split_product(rows_ref, high_ref, low_ref).reshape(out_ref.shape)
 
 
 def symbol_phases(off_ref, symbols):
@@ -199,18 +230,15 @@
         by_row = jnp.where(row == m, off_ref[m], by_row)
         by_lane = jnp.where(lane == m, off_ref[m], by_lane)
 
-    def phase(product):
-        angle = (product & (WHOLE - 1)).astype(jnp.float32) * (TWO_PI / WHOLE)
-        return jnp.cos(angle), jnp.sin(angle)
-
-    return phase(by_row * (LOWEST + FOLD * lane)), [phase(by_lane * (p + 4 * row)) for p in range(4)]
+    by_lanes = phase(by_row * (LOWEST + FOLD * lane), WHOLE)
+    return by_lanes, [phase(by_lane * (p + 4 * row), WHOLE) for p in range(4)]
 
 
 def profile_kernel(
-    blocks, scale, off_ref, pilot_ref, place_ref, s_ref, own_ref, other_ref, spot_ref, high_ref, low_ref, twist_ref, *refs
+    syms, scale, off_ref, pilot_ref, place_ref, s_ref, own_ref, other_ref, spot_ref, high_ref, low_ref, twist_ref, *refs
 ):
-    outs = refs[:blocks]
-    flat_ref, turned_ref, gain_ref, ratio_ref, num_ref, rows_ref, range_ref, prof_ref = refs[blocks:]
+    outs = refs[: max(syms, 1)]
+    flat_ref, turned_ref, gain_ref, ratio_ref, num_ref, rows_ref, range_ref, prof_ref = refs[max(syms, 1) :]
     symbols, groups = s_ref.shape[:2]
     tones = ACTIVE_TONES // FOLD
     own_place, swapped = place_ref[0], place_ref[1] > 0
@@ -256,6 +284,7 @@
             gain_ref[slot, 3, at] = jnp.where(is_pilot, 1.0, 0.0)
 
         for g in range(groups):
+            base = (m * groups + g) * FOLD * ROWS
             for i in range(FOLD):
                 re = s_ref[m, g, i * ROWS : (i + 1) * ROWS, :tones]
                 im = s_ref[m, g, i * ROWS : (i + 1) * ROWS, tones:]
@@ -296,70 +325,96 @@
                         smooth = num_ref[slot, part, (n // 8) * 10 + n % 8 + 1] * gain_ref[slot, 2, n : n + 1, :]
                         pair.append(ratio_ref[slot, part, n] - smooth)
                     high, low = split_rows(jnp.concatenate(pair, axis=0))
-                    at = slice(i * ROWS, (i + 2) * ROWS)
-                    rows_ref[slot, at, part * tones : (part + 1) * tones] = high
-                    rows_ref[slot, at, (2 + part) * tones : (3 + part) * tones] = low
-            high = rows_ref[slot, :, : 2 * tones]
-            low = rows_ref[slot, :, 2 * tones :]
-            range_ref[slot] = dot(high, high_ref[...]) + dot(low, high_ref[...]) + dot(high, low_ref[...])
-
+                    at = slice(base + i * ROWS, base + (i + 2) * ROWS)
+                    rows_ref[at, part * tones : (part + 1) * tones] = high
+                    rows_ref[at, (2 + part) * tones : (3 + part) * tones] = low
+
+    range_ref[...] = split_product(rows_ref, high_ref, low_ref)
+    lane = lax.broadcasted_iota(jnp.int32, (ROWS, LANES), 1)
+    codes = jnp.zeros((ROWS, LANES), jnp.float32)
+    for m in range(symbols):
+        for g in range(groups):
+            base, slot = (m * groups + g) * FOLD * ROWS, m % 2
             sums = None
             for p in range(4):
                 x = []
                 for i in range(p * 8, p * 8 + 8):
-                    re = range_ref[slot, i * ROWS : (i + 1) * ROWS, :LANES]
-                    im = range_ref[slot, i * ROWS : (i + 1) * ROWS, LANES:]
-                    c = twist_ref[0, i : i + 1, :]
-                    s = twist_ref[1, i : i + 1, :]
+                    at = slice(base + i * ROWS, base + (i + 1) * ROWS)
+                    re, im = range_ref[at, :LANES], range_ref[at, LANES:]
+                    c, s = twist_ref[0, i : i + 1, :], twist_ref[1, i : i + 1, :]
                     x.append((re * c - im * s, re * s + im * c))
                 y = [times(v, p * h / FOLD) for h, v in enumerate(dft8(x, 1))]
                 sums = y if sums is None else [plus(a, b) for a, b in zip(sums, y)]
-            if blocks == 1:
+            if not syms:
                 for h in range(RANGE_ROWS):
                     outs[0][m, g, 0, h], outs[0][m, g, 1, h] = sums[h]
                 continue
+            code = code_scale(peak_of([v for pair in sums for v in pair]))
+            codes = jnp.where(lane == m, code, codes)
             for h in range(RANGE_ROWS):
-                prof_ref[slot, 0, h], prof_ref[slot, 1, h] = sums[h]
-            each = RANGE_ROWS // blocks
-            for d in range(blocks):
-                block = own_place ^ d
-                for part in range(2):
-                    for h in range(each):
-                        outs[d][m, g, part, h] = prof_ref[slot, part, block * each + h]
-
-
-def doppler_kernel(place_ref, *refs):
-    pieces, outs, (turned_ref, spread_ref) = refs[:4], refs[4:8], refs[8:]
-    own, rank = place_ref[0], place_ref[1]
-    local_symbols, _, _, each = pieces[0].shape[:4]
-    for d in range(4):
-        for m in range(local_symbols):
-            turned_ref[own ^ d, m] = pieces[d][m, 0]
-    for h in range(each):
-        grid = {}
-        for m in range(local_symbols):
-            x = [(turned_ref[s, m, 0, h], turned_ref[s, m, 1, h]) for s in range(4)]
+                prof_ref[slot, h, 0], prof_ref[slot, h, 1] = sums[h]
+            for h in range(RANGE_ROWS // syms):
+                for d in range(syms):
+                    row = syms * h + (own_place ^ d)
+                    if d == 0:
+                        outs[0][m, h] = prof_ref[slot, row]
+                        continue
+                    packed = [encode(prof_ref[slot, row, part], code) for part in range(2)]
+                    outs[d][m * (RANGE_ROWS // syms) + h] = jnp.concatenate(packed, axis=0).astype(jnp.int16)
+    if syms:
+        packed = jnp.concatenate([codes, codes], axis=0).astype(jnp.int32).astype(jnp.int16)
+        for d in range(1, syms):
+            outs[d][symbols * (RANGE_ROWS // syms)] = packed
+
+
+def doppler_kernel(place_ref, own_ref, *refs):
+    (first, second, third), out_ref, turned_ref, spread_ref = refs[:3], refs[3], refs[4], refs[5]
+    symbols, rows = own_ref.shape[:2]
+    syms = 4
+    own = place_ref[0]
+    turned_ref[own] = own_ref[...]
+    for d, piece in enumerate((first, second, third), 1):
+        codes = piece[symbols * rows].astype(jnp.int32).astype(jnp.float32)
+        for m in range(symbols):
+            code = codes[:, m : m + 1]
+            for h in range(rows):
+                value = decode(piece[m * rows + h], code)
+                turned_ref[own ^ d, m, h, 0], turned_ref[own ^ d, m, h, 1] = value[:ROWS], value[ROWS:]
+    for h in range(rows):
+        grid, bins = {}, {}
+        for m in range(symbols):
+            x = [(turned_ref[s, m, h, 0], turned_ref[s, m, h, 1]) for s in range(syms)]
             for p, y in enumerate(dft4(x, -1)):
-                grid[p, m] = times(y, -m * p / (4 * local_symbols))
-        for p in range(4):
-            for q, y in enumerate(dft6([grid[p, m] for m in range(local_symbols)], -1)):
-                f = p + 4 * q
-                at = slice(h * LANES, (h + 1) * LANES)
-                spread_ref[f // local_symbols, 0, f % local_symbols, :, at] = y[0]
-                spread_ref[f // local_symbols, 1, f % local_symbols, :, at] = y[1]
-    for d in range(4):
-        outs[d][...] = spread_ref[rank ^ d]
-
-
-def join_kernel(place_ref, *refs):
-    pieces, out_ref = refs[:4], refs[4]
-    own = place_ref[0]
-    wide = pieces[0].shape[-1]
-    for d in range(4):
-        h = own ^ d
-        rows = pl.ds(pl.multiple_of((h & 1) * ROWS, ROWS), ROWS)
-        columns = pl.ds(pl.multiple_of((h >> 1) * wide, LANES), wide)
-        out_ref[:, :, rows, columns] = pieces[d][...]
+                grid[p, m] = times(y, -m * p / (syms * symbols))
+        for p in range(syms):
+            for q, y in enumerate(dft6([grid[p, m] for m in range(symbols)], -1)):
+                f = p + syms * q
+                spread_ref[h, f, 0], spread_ref[h, f, 1] = y
+    for s in range(syms):
+        for h in range(rows):
+            values = [spread_ref[h, s * symbols + f] for f in range(symbols)]
+            code = code_scale(peak_of([v[part] for v in values for part in range(2)]))
+            to = s * rows + h
+            for f in range(symbols):
+                packed = [encode(values[f][part], code) for part in range(2)]
+                out_ref[to, f] = jnp.concatenate(packed, axis=0).astype(jnp.int16)
+            codes = jnp.broadcast_to(code, (ROWS, LANES)).astype(jnp.int32)
+            out_ref[to, symbols] = jnp.concatenate([codes, codes], axis=0).astype(jnp.int16)
+
+
+def join_kernel(piece_ref, out_ref):
+    _, symbols, channels, width = out_ref.shape
+    subs = channels // ROWS
+    for n in range(piece_ref.shape[0]):
+        s, u = n // subs, n % subs
+        code = piece_ref[n, symbols].astype(jnp.int32).astype(jnp.float32)
+        gain = jnp.exp2(code * (1.0 / 64.0)) * (1.0 / 32767.0**2)
+        for f in range(symbols):
+            value = piece_ref[n, f].astype(jnp.int32).astype(jnp.float32)
+            value = value * jnp.abs(value) * gain
+            for part in range(2):
+                at = slice(part * ROWS, (part + 1) * ROWS)
+                out_ref[part, f, u * ROWS : (u + 1) * ROWS, s * LANES : (s + 1) * LANES] = value[at]
 
 
 IN_VMEM = pl.BlockSpec(memory_space=pltpu.VMEM)
@@ -370,51 +425,54 @@
 def spectra(windows, cp_offset):
     _, symbols, channels, record = windows.shape
     groups = channels // ROWS
-    high, low, twist = spectrum_tables()
     tones = ACTIVE_TONES // FOLD
     return pl.pallas_call(
         spectrum_kernel,
-        in_specs=[IN_SMEM] + [IN_HBM] * 4,
+        in_specs=[IN_SMEM, IN_HBM],
         out_specs=IN_VMEM,
         scratch_shapes=[
             pltpu.VMEM((symbols * groups, 2, ROWS, record), jnp.float32),
-            pltpu.VMEM(high.shape, jnp.bfloat16),
-            pltpu.VMEM(low.shape, jnp.bfloat16),
-            pltpu.VMEM(twist.shape, jnp.float32),
+            pltpu.VMEM((2 * WIDE, 2 * tones), jnp.bfloat16),
+            pltpu.VMEM((2 * WIDE, 2 * tones), jnp.bfloat16),
+            pltpu.VMEM((2, FOLD, WIDE), jnp.float32),
             pltpu.VMEM((2, WIDE // LANES, 4, 8, 2, ROWS, LANES), jnp.float32),
-            pltpu.VMEM((2, FOLD * ROWS, 4 * WIDE), jnp.bfloat16),
-            pltpu.SemaphoreType.DMA((3 + symbols * groups,)),
+            pltpu.VMEM((symbols * groups * FOLD * ROWS, 4 * WIDE), jnp.bfloat16),
+            pltpu.SemaphoreType.DMA((symbols * groups,)),
         ],
         out_shape=jax.ShapeDtypeStruct((symbols, groups, FOLD * ROWS, 2 * tones), jnp.float32),
         compiler_params=pltpu.CompilerParams(vmem_limit_bytes=SPECTRA_VMEM_LIMIT),
         cost_estimate=pl.CostEstimate(flops=2 * 10**9, bytes_accessed=8 * 10**6, transcendentals=0),
         name="spectra",
-    )(cp_offset, windows, high, low, twist)
-
-
-def profiles(spectrum, own, other, pilot_offsets, cp_offset, places, blocks, scale):
+    )(cp_offset, windows)
+
+
+def profiles(spectrum, own, other, pilot_offsets, cp_offset, places, syms, scale):
     symbols, groups = spectrum.shape[:2]
     high, low, twist = range_tables()
     tones = ACTIVE_TONES // FOLD
-    each = RANGE_ROWS // blocks
     n, column = np.arange(FOLD)[:, None], np.arange(LANES // FOLD * tones)[None, :]
     spot = (column % tones == LANES // FOLD * n + column // tones).astype(ml_dtypes.bfloat16)
-    out = jax.ShapeDtypeStruct((symbols, groups, 2, each, ROWS, LANES), jnp.float32)
+    if syms:
+        rows = RANGE_ROWS // syms
+        piece = jax.ShapeDtypeStruct((symbols * rows + 1, 2 * ROWS, LANES), jnp.int16)
+        outs = [jax.ShapeDtypeStruct((symbols, rows, 2, ROWS, LANES), jnp.float32)] + [piece] * (syms - 1)
+    else:
+        outs = [jax.ShapeDtypeStruct((symbols, groups, 2, RANGE_ROWS, ROWS, LANES), jnp.float32)]
     return pl.pallas_call(
-        functools.partial(profile_kernel, blocks, scale),
+        functools.partial(profile_kernel, syms, scale),
         in_specs=[IN_SMEM] * 3 + [IN_VMEM] * 7,
-        out_specs=[IN_VMEM] * blocks,
+        out_specs=[IN_VMEM] * len(outs),
         scratch_shapes=[
             pltpu.VMEM((FOLD, ROWS, LANES), jnp.float32),
             pltpu.VMEM((2, FOLD, tones), jnp.float32),
             pltpu.VMEM((2, 4, FOLD, tones), jnp.float32),
             pltpu.VMEM((2, 2, FOLD, ROWS, tones), jnp.float32),
             pltpu.VMEM((2, 2, 40, ROWS, tones), jnp.float32),
-            pltpu.VMEM((2, FOLD * ROWS, 4 * tones), jnp.bfloat16),
-            pltpu.VMEM((2, FOLD * ROWS, 2 * LANES), jnp.float32),
-            pltpu.VMEM((2, 2, RANGE_ROWS, ROWS, LANES), jnp.float32),
+            pltpu.VMEM((symbols * groups * FOLD * ROWS, 4 * tones), jnp.bfloat16),
+            pltpu.VMEM((symbols * groups * FOLD * ROWS, 2 * LANES), jnp.float32),
+            pltpu.VMEM((2, RANGE_ROWS, 2, ROWS, LANES), jnp.float32),
         ],
-        out_shape=[out] * blocks,
+        out_shape=outs,
         compiler_params=pltpu.CompilerParams(vmem_limit_bytes=VMEM_LIMIT),
         cost_estimate=pl.CostEstimate(flops=10**9, bytes_accessed=4 * 10**6, transcendentals=0),
         name="profiles",
@@ -433,41 +491,32 @@
     return lax.all_to_all(jnp.stack([re, im]), "sym", split_axis=2, concat_axis=3, tiled=True)
 
 
-def doppler_paired(pieces, place, rank, syms, subs):
-    share = syms // subs
+def doppler_paired(pieces, places, syms, subs):
     got = [pieces[0]] + [
         lax.ppermute(pieces[d], "sym", [(i, i ^ d) for i in range(syms)]) for d in range(1, syms)
     ]
-    symbols, _, _, each = got[0].shape[:4]
-    piece = jax.ShapeDtypeStruct((2, symbols, ROWS, each * LANES), jnp.float32)
-    spread = pl.pallas_call(
+    symbols, rows = got[0].shape[:2]
+    coded = pl.pallas_call(
         doppler_kernel,
         in_specs=[IN_SMEM] + [IN_VMEM] * syms,
-        out_specs=[IN_VMEM] * syms,
-        out_shape=[piece] * syms,
+        out_specs=IN_VMEM,
+        out_shape=jax.ShapeDtypeStruct((syms * subs, symbols + 1, 2 * ROWS, LANES), jnp.int16),
         scratch_shapes=[
-            pltpu.VMEM((syms, symbols, 2, each, ROWS, LANES), jnp.float32),
-            pltpu.VMEM((syms,) + piece.shape, jnp.float32),
+            pltpu.VMEM((syms, symbols, rows, 2, ROWS, LANES), jnp.float32),
+            pltpu.VMEM((rows, syms * symbols, 2, ROWS, LANES), jnp.float32),
         ],
         compiler_params=pltpu.CompilerParams(vmem_limit_bytes=VMEM_LIMIT),
         name="doppler",
-    )(jnp.stack([place, rank]), *got)
-    joined = []
-    for d in range(syms):
-        route = [
-            (s * subs + u, (((s % share) * subs + u) ^ d) * subs + s // share)
-            for s in range(syms)
-            for u in range(subs)
-        ]
-        joined.append(lax.ppermute(spread[d], ("sym", "sub"), route))
+    )(places, *got)
+    coded = lax.all_to_all(coded, ("sym", "sub"), split_axis=0, concat_axis=0)
     out = pl.pallas_call(
         join_kernel,
-        in_specs=[IN_SMEM] + [IN_VMEM] * syms,
+        in_specs=[IN_VMEM],
         out_specs=IN_VMEM,
-        out_shape=jax.ShapeDtypeStruct((2, symbols, subs * ROWS, share * each * LANES), jnp.float32),
+        out_shape=jax.ShapeDtypeStruct((2, symbols, subs * ROWS, syms * LANES), jnp.float32),
         compiler_params=pltpu.CompilerParams(vmem_limit_bytes=VMEM_LIMIT),
         name="join",
-    )(place[None], *joined)
+    )(coded)
     return jnp.transpose(out, (0, 2, 1, 3))
 
 
@@ -475,7 +524,7 @@
     syms, subs = lax.axis_size("sym"), lax.axis_size("sub")
     place, sub = lax.axis_index("sym"), lax.axis_index("sub")
     channels, symbols = samples.shape[1:3]
-    paired = syms == 4 and subs == 2 and channels == ROWS and symbols == 6
+    paired = syms == 4 and syms * subs == RANGE_ROWS and channels == ROWS and symbols == 6
     half = ACTIVE_TONES // 2
     if paired:
         own = constellation_index
@@ -491,11 +540,11 @@
     spectrum = spectra(windows, cp_offset)
     scale = ROOT_FORTYTWO / math.sqrt(WHOLE * ACTIVE_TONES * symbols * syms)
     places = jnp.stack([place, swapped])
-    blocks = syms if paired else 1
-    got = profiles(spectrum, own, other, pilot_offsets, cp_offset, places, blocks, scale)
+    got = profiles(
+        spectrum, own, other, pilot_offsets, cp_offset, places, syms if paired else 0, scale
+    )
     if paired:
-        rank = (place % (syms // subs)) * subs + sub
-        return doppler_paired(got, place, rank, syms, subs)
+        return doppler_paired(got, places, syms, subs)
     own = jnp.transpose(got[0], (2, 1, 4, 0, 3, 5))
     own = own.reshape(2, channels + short, symbols, GUARD_SAMPLES)[:, :channels]
     return doppler_plain(own, symbols * syms)

time: 45.1 us -> 34.7 us (0.77)
  blocking collectives: 0 us -> 10.4 us
  starting transfers between devices: 17.7 us -> 7.42 us
  waiting for transfers between devices: 12.8 us -> 5.72 us
  Pallas kernels: 12.8 us -> 10.1 us
  local copies, waits for them, and re-layouts: 1.44 us -> 0.68 us
    all_to_all x0 -> x1, blocking collectives: none -> 10.4 us  [doppler_paired(): coded = lax.all_to_all(coded, ('sym', 'sub'), split_axis=0, concat_axis=0)]
    ppermute x4 -> x0, starting transfers between devices: 10.3 us -> none  [doppler_paired(): joined.append(lax.ppermute(spread[d], ('sym', 'sub'), route))]
    ppermute x4 -> x0, waiting for transfers between devices: 5.53 us -> none  [doppler_paired(): joined.append(lax.ppermute(spread[d], ('sym', 'sub'), route))]
    pallas_call x3, Pallas kernels: 12.1 us -> 9.04 us  [the longest x1 4.76 us: spectra(): pl.pallas_call(spectrum_kernel, in_specs=[IN_SMEM, IN_HBM], out_specs=IN_...]
    ppermute x3, waiting for transfers between devices: 7.26 us -> 5.72 us  [doppler_paired(): lax.ppermute(pieces[d], 'sym', [(i, i ^ d) for i in range(syms)])]
    unnamed x16 -> x14, local copies, waits for them, and re-layouts: 1.44 us -> 0.68 us
  transfers between devices with their start and end apart: 8 -> 4, of which waited for: 4 -> 2; matrix products, arithmetic and copies ran while one was open for 0% -> 0% of each run, Pallas kernels for 17% -> 14%
where the time goes in v3:
time: 34.7 us; the launch traced here: 34.5 us
  blocking collectives  10.4 us (30%)
  Pallas kernels  10.1 us (29%)
  starting transfers between devices  7.42 us (21%)
  waiting for transfers between devices  5.72 us (16%)
  local copies, waits for them, and re-layouts  0.68 us (2%)
    all_to_all x1, blocking collectives, doppler_paired(): coded = lax.all_to_all(coded, ('sym', 'sub'), split_axis=0, concat_axis=0)  10.4 us
    ppermute x3, waiting for transfers between devices, doppler_paired(): lax.ppermute(pieces[d], 'sym', [(i, i ^ d) for i in range(syms)])  5.72 us
    pallas_call x1, Pallas kernels, spectra(): pl.pallas_call(spectrum_kernel, in_specs=[IN_SMEM, IN_HBM], out_specs=IN_...  4.76 us
    ppermute x3, starting transfers between devices, doppler_paired(): lax.ppermute(pieces[d], 'sym', [(i, i ^ d) for i in range(syms)])  4.45 us
    pallas_call x1, Pallas kernels, profiles(): pl.pallas_call(functools.partial(profile_kernel, syms, scale), in_specs=[...  3.45 us
    ppermute x1, starting transfers between devices, local(): other = lax.ppermute(own, 'sub', [(0, 1), (1, 0)])  2.97 us
    pallas_call x1, Pallas kernels, doppler_paired(): pl.pallas_call(doppler_kernel, in_specs=[IN_SMEM] + [IN_VMEM] * syms, out...  1.03 us
    pallas_call x1, Pallas kernels, doppler_paired(): pl.pallas_call(join_kernel, in_specs=[IN_VMEM], out_specs=IN_VMEM, out_sh...  0.83 us
  transfers between devices with their start and end apart: 4, of which 2 were waited for; matrix products, arithmetic and copies ran while one was open for 0% of the time, Pallas kernels for 14%

profile of v3, /device:TPU:0, one launch (start us, length us, event | category | flops | bytes accessed | tf_op | source)
XLA Modules:
  0.0 34.5 jit_solution(10902470033441905626)
XLA Ops:
  0.0 3.0 %collective-permute-start = (s32[6,2048]{1,0:T(8,128)}, s32[6,2048]{1,0:T(8,128)S(1)}, u32[]{:S(2)}, u32[]{:S(2)}) collective-permute-start(s32[6,2048]{1,0:T(8,128)} %own_ref.1), channel_id=1, source_target_pairs={{0,1},{1,0},{2,3},{3,2},{4,5},{5,4},{6,7},{7,6},{8,9},{9,8},{10,11... | collective-permute-start | bytes 147464 | tf_op jit(solution)/shard_map/ppermute | solution.py:531
  3.0 0.0 copy-start.1
  3.0 0.7 %copy-done.1 = s32[6]{0:T(128)S(1)} copy-done((s32[6]{0:T(128)S(1)}, s32[6]{0:T(128)}, u32[]{:S(2)}) %copy-start.1) | copy-done | bytes 48
  3.6 0.0 copy-start.5
  3.6 0.0 copy-start.6
  3.7 4.8 %spectra.1.s_ref = f32[6,1,256,256]{3,2,1,0:T(8,128)S(1)} custom-call(s32[6]{0:T(128)S(1)} %copy-done.1, f32[2,6,8,9216]{3,2,1,0:T(8,128)} %bitcast.4), custom_call_target="tpu_custom_call" | custom-call | flops 2000000000 | bytes 8000000 | tf_op jit(solution)/shard_map/spectra/pallas_call | solution.py:429
  8.4 0.1 pad_add_fusion.place_ref
  8.5 0.0 collective-permute-done.other_ref
  8.5 0.0 copy-done
  8.5 0.0 copy-done.2
  8.5 0.0 copy-done.3
  8.5 0.0 copy-done.4
  8.5 0.0 copy-done.5
  8.5 0.0 copy-done.6
  8.6 3.5 %profiles.1 = (f32[6,2,2,8,128]{4,3,2,1,0:T(8,128)S(1)}, s16[13,16,128]{2,1,0:T(8,128)(2,1)S(1)}, s16[13,16,128]{2,1,0:T(8,128)(2,1)S(1)}, s16[13,16,128]{2,1,0:T(8,128)(2,1)S(1)}) custom-call(s32[6]{0:T(128)S(1)} %copy-done.1, s32[6]{0:T(128)S(1)} %copy-done.2, s32[2]{0:T(128)S(1)} %pad_add_fusion.place_ref, f32[6,1,256,256]{3,2,1,0:T(8,128)S(1)} %spectra.1.s_ref, ...), custom_call_target="tpu_custom_call" | custom-call | flops 1000000000 | bytes 4000000 | tf_op jit(solution)/shard_map/profiles/pallas_call | solution.py:461
  12.0 1.6 %collective-permute-start.1 = (s16[13,16,128]{2,1,0:T(8,128)(2,1)S(1)}, s16[13,16,128]{2,1,0:T(8,128)(2,1)S(1)}, u32[]{:S(2)}, u32[]{:S(2)}) collective-permute-start(s16[13,16,128]{2,1,0:T(8,128)(2,1)S(1)} %get-tuple-element.10), channel_id=1, source_target_pairs={{0,2},{2,0},{4,6},{6,4},{1,3},{3,1},{5,7},{7,5},{8,10},{10,8},{12,... | collective-permute-start | bytes 159752 | tf_op jit(solution)/shard_map/ppermute | solution.py:496
  13.7 2.6 %collective-permute-start.2 = (s16[13,16,128]{2,1,0:T(8,128)(2,1)S(1)}, s16[13,16,128]{2,1,0:T(8,128)(2,1)S(1)}, u32[]{:S(2)}, u32[]{:S(2)}) collective-permute-start(s16[13,16,128]{2,1,0:T(8,128)(2,1)S(1)} %get-tuple-element.11), channel_id=1, source_target_pairs={{0,4},{2,6},{4,0},{6,2},{1,5},{3,7},{5,1},{7,3},{8,12},{10,14},{12... | collective-permute-start | bytes 159752 | tf_op jit(solution)/shard_map/ppermute | solution.py:496
  16.3 0.2 collective-permute-start.3
  16.5 0.0 collective-permute-done.1.refs_0_
  16.5 3.0 %collective-permute-done.2.refs_1_ = s16[13,16,128]{2,1,0:T(8,128)(2,1)S(1)} collective-permute-done((s16[13,16,128]{2,1,0:T(8,128)(2,1)S(1)}, s16[13,16,128]{2,1,0:T(8,128)(2,1)S(1)}, u32[]{:S(2)}, u32[]{:S(2)}) %collective-permute-start.2) | collective-permute-done | bytes 53280 | tf_op jit(solution)/shard_map/ppermute | solution.py:496
  19.4 2.8 %collective-permute-done.3.refs_2_ = s16[13,16,128]{2,1,0:T(8,128)(2,1)S(1)} collective-permute-done((s16[13,16,128]{2,1,0:T(8,128)(2,1)S(1)}, s16[13,16,128]{2,1,0:T(8,128)(2,1)S(1)}, u32[]{:S(2)}, u32[]{:S(2)}) %collective-permute-start.3) | collective-permute-done | bytes 53280 | tf_op jit(solution)/shard_map/ppermute | solution.py:496
  22.2 1.0 %doppler.1 = s16[8,7,16,128]{3,2,1,0:T(8,128)(2,1)S(1)} custom-call(s32[2]{0:T(128)S(1)} %pad_add_fusion.place_ref, f32[6,2,2,8,128]{4,3,2,1,0:T(8,128)S(1)} %get-tuple-element.9.own_ref, s16[13,16,128]{2,1,0:T(8,128)(2,1)S(1)} %collective-permute-done.1.refs_0_, s16[13,16,128]{2,1,0:T(8,128)(2,1)S(1)} %collective-permute-done.2.refs_1_, ...), custom_call_target="tpu_custom_call" | custom-call | tf_op jit(solution)/shard_map/doppler/pallas_call | solution.py:499
  23.2 10.4 %all_to_all.5.piece_ref = s16[8,7,16,128]{3,2,1,0:T(8,128)(2,1)S(1)} all-to-all(s16[8,7,16,128]{3,2,1,0:T(8,128)(2,1)S(1)} %doppler.1), channel_id=1, replica_groups=mesh['chan'=4,'sym'=4,'sub'=2] {'sym','sub'}, dimensions={0} | all-to-all | bytes 458752 | tf_op jit(solution)/shard_map/all_to_all | solution.py:511
  33.6 0.8 %join.1 = f32[2,6,16,512]{3,2,1,0:T(8,128)} custom-call(s16[8,7,16,128]{3,2,1,0:T(8,128)(2,1)S(1)} %all_to_all.5.piece_ref), custom_call_target="tpu_custom_call" | custom-call | tf_op jit(solution)/shard_map/join/pallas_call | solution.py:512
  (4 shorter events, 0.0 us)
Async XLA Ops:
  0.0 8.5 %collective-permute-start = (s32[6,2048]{1,0:T(8,128)}, s32[6,2048]{1,0:T(8,128)S(1)}, u32[]{:S(2)}, u32[]{:S(2)}) collective-permute-start(s32[6,2048]{1,0:T(8,128)} %own_ref.1), channel_id=1, source_target_pairs={{0,1},{1,0},{2,3},{3,2},{4,5},{5,4},{6,7},{7,6},{8,9},{9,8},{10,11... | collective-permute-start | bytes 147464 | tf_op jit(solution)/shard_map/ppermute | solution.py:531
  3.0 0.7 %copy-start.1 = (s32[6]{0:T(128)S(1)}, s32[6]{0:T(128)}, u32[]{:S(2)}) copy-start(s32[6]{0:T(128)} %off_ref.3) | copy-start | bytes 76
  3.6 4.9 %copy-start = (s32[6,2048]{1,0:T(8,128)S(1)}, s32[6,2048]{1,0:T(8,128)}, u32[]{:S(2)}) copy-start(s32[6,2048]{1,0:T(8,128)} %own_ref.1) | copy-start | bytes 147460
  3.6 4.9 %copy-start.2 = (s32[6]{0:T(128)S(1)}, s32[6]{0:T(128)}, u32[]{:S(2)}) copy-start(s32[6]{0:T(128)} %pilot_ref.1) | copy-start | bytes 76
  3.6 4.9 %copy-start.3 = (bf16[256,256]{1,0:T(8,128)(2,1)S(1)}, bf16[256,256]{1,0:T(8,128)(2,1)}, u32[]{:S(2)}) copy-start(bf16[256,256]{1,0:T(8,128)(2,1)} %constant.18.clone.low_ref) | copy-start | bytes 393220
  3.6 4.9 %copy-start.4 = (bf16[256,256]{1,0:T(8,128)(2,1)S(1)}, bf16[256,256]{1,0:T(8,128)(2,1)}, u32[]{:S(2)}) copy-start(bf16[256,256]{1,0:T(8,128)(2,1)} %constant.17.clone.high_ref) | copy-start | bytes 393220
  3.6 4.9 %copy-start.5 = (f32[2,32,128]{2,1,0:T(8,128)S(1)}, f32[2,32,128]{2,1,0:T(8,128)}, u32[]{:S(2)}) copy-start(f32[2,32,128]{2,1,0:T(8,128)} %constant.19.clone.twist_ref) | copy-start | bytes 98308
  3.6 4.9 %copy-start.6 = (bf16[32,512]{1,0:T(8,128)(2,1)S(1)}, bf16[32,512]{1,0:T(8,128)(2,1)}, u32[]{:S(2)}) copy-start(bf16[32,512]{1,0:T(8,128)(2,1)} %constant.16.clone.spot_ref) | copy-start | bytes 98308
  12.0 4.5 %collective-permute-start.1 = (s16[13,16,128]{2,1,0:T(8,128)(2,1)S(1)}, s16[13,16,128]{2,1,0:T(8,128)(2,1)S(1)}, u32[]{:S(2)}, u32[]{:S(2)}) collective-permute-start(s16[13,16,128]{2,1,0:T(8,128)(2,1)S(1)} %get-tuple-element.10), channel_id=1, source_target_pairs={{0,2},{2,0},{4,6},{6,4},{1,3},{3,1},{5,7},{7,5},{8,10},{10,8},{12,... | collective-permute-start | bytes 159752 | tf_op jit(solution)/shard_map/ppermute | solution.py:496
  13.7 5.8 %collective-permute-start.2 = (s16[13,16,128]{2,1,0:T(8,128)(2,1)S(1)}, s16[13,16,128]{2,1,0:T(8,128)(2,1)S(1)}, u32[]{:S(2)}, u32[]{:S(2)}) collective-permute-start(s16[13,16,128]{2,1,0:T(8,128)(2,1)S(1)} %get-tuple-element.11), channel_id=1, source_target_pairs={{0,4},{2,6},{4,0},{6,2},{1,5},{3,7},{5,1},{7,3},{8,12},{10,14},{12... | collective-permute-start | bytes 159752 | tf_op jit(solution)/shard_map/ppermute | solution.py:496
  16.3 5.9 %collective-permute-start.3 = (s16[13,16,128]{2,1,0:T(8,128)(2,1)S(1)}, s16[13,16,128]{2,1,0:T(8,128)(2,1)S(1)}, u32[]{:S(2)}, u32[]{:S(2)}) collective-permute-start(s16[13,16,128]{2,1,0:T(8,128)(2,1)S(1)} %get-tuple-element.12), channel_id=1, source_target_pairs={{0,6},{2,4},{4,2},{6,0},{1,7},{3,5},{5,3},{7,1},{8,14},{10,12},{12... | collective-permute-start | bytes 159752 | tf_op jit(solution)/shard_map/ppermute | solution.py:496

commit v4 on v3

--- a/solution.py
+++ b/solution.py
@@ -156,7 +156,7 @@
     return jnp.where(turned, -c, c), jnp.where(low, -s, s)
 
 
-def spectrum_kernel(off_ref, x_hbm, out_ref, x_ref, high_ref, low_ref, twist_ref, mid_ref, rows_ref, sems):
+def spectrum_kernel(off_hbm, x_hbm, out_ref, off_ref, x_ref, high_ref, low_ref, twist_ref, mid_ref, rows_ref, sems):
     symbols, groups = out_ref.shape[:2]
     tones = ACTIVE_TONES // FOLD
     tasks = [(m, g) for m in range(symbols) for g in range(groups)]
@@ -165,6 +165,9 @@
         source = x_hbm.at[:, m, g * ROWS : (g + 1) * ROWS, :]
         fetches.append(pltpu.make_async_copy(source, x_ref.at[n], sems.at[n]))
         fetches[-1].start()
+        if n == 0:
+            starts = pltpu.make_async_copy(off_hbm, off_ref, sems.at[len(tasks)])
+            starts.start()
     row = lax.broadcasted_iota(jnp.int32, (ROWS, WIDE), 0)
     lane = lax.broadcasted_iota(jnp.int32, (ROWS, WIDE), 1)
     for p in range(4):
@@ -182,6 +185,7 @@
         low_ref[lower, :tones], low_ref[lower, tones:] = s_low, c_low
     lane = lax.broadcasted_iota(jnp.int32, (ROWS, LANES), 1)
     halves = WIDE // LANES
+    starts.wait()
     for n, (m, g) in enumerate(tasks):
         fetches[n].wait()
         off, slot = off_ref[m], n % 2
@@ -367,13 +371,16 @@
             outs[d][symbols * (RANGE_ROWS // syms)] = packed
 
 
+SEND_ORDER = (3, 1, 2)
+
+
 def doppler_kernel(place_ref, own_ref, *refs):
-    (first, second, third), out_ref, turned_ref, spread_ref = refs[:3], refs[3], refs[4], refs[5]
+    pieces, (out_ref, turned_ref, spread_ref) = refs[:3], refs[3:]
     symbols, rows = own_ref.shape[:2]
     syms = 4
     own = place_ref[0]
     turned_ref[own] = own_ref[...]
-    for d, piece in enumerate((first, second, third), 1):
+    for d, piece in zip(SEND_ORDER, pieces):
         codes = piece[symbols * rows].astype(jnp.int32).astype(jnp.float32)
         for m in range(symbols):
             code = codes[:, m : m + 1]
@@ -428,16 +435,17 @@
     tones = ACTIVE_TONES // FOLD
     return pl.pallas_call(
         spectrum_kernel,
-        in_specs=[IN_SMEM, IN_HBM],
+        in_specs=[IN_HBM, IN_HBM],
         out_specs=IN_VMEM,
         scratch_shapes=[
+            pltpu.SMEM((symbols,), jnp.int32),
             pltpu.VMEM((symbols * groups, 2, ROWS, record), jnp.float32),
             pltpu.VMEM((2 * WIDE, 2 * tones), jnp.bfloat16),
             pltpu.VMEM((2 * WIDE, 2 * tones), jnp.bfloat16),
             pltpu.VMEM((2, FOLD, WIDE), jnp.float32),
             pltpu.VMEM((2, WIDE // LANES, 4, 8, 2, ROWS, LANES), jnp.float32),
             pltpu.VMEM((symbols * groups * FOLD * ROWS, 4 * WIDE), jnp.bfloat16),
-            pltpu.SemaphoreType.DMA((symbols * groups,)),
+            pltpu.SemaphoreType.DMA((symbols * groups + 1,)),
         ],
         out_shape=jax.ShapeDtypeStruct((symbols, groups, FOLD * ROWS, 2 * tones), jnp.float32),
         compiler_params=pltpu.CompilerParams(vmem_limit_bytes=SPECTRA_VMEM_LIMIT),
@@ -493,7 +501,7 @@
 
 def doppler_paired(pieces, places, syms, subs):
     got = [pieces[0]] + [
-        lax.ppermute(pieces[d], "sym", [(i, i ^ d) for i in range(syms)]) for d in range(1, syms)
+        lax.ppermute(pieces[d], "sym", [(i, i ^ d) for i in range(syms)]) for d in SEND_ORDER
     ]
     symbols, rows = got[0].shape[:2]
     coded = pl.pallas_call(

time: 34.7 us -> 33.4 us (0.963)
  waiting for transfers between devices: 5.72 us -> 4.31 us
  blocking collectives: 10.4 us -> 11 us
  Pallas kernels: 10.1 us -> 9.59 us
    ppermute x3, waiting for transfers between devices: 5.72 us -> 4.31 us  [doppler_paired(): lax.ppermute(pieces[d], 'sym', [(i, i ^ d) for i in range(syms)])]
    all_to_all x1, blocking collectives: 10.4 us -> 11 us  [doppler_paired(): coded = lax.all_to_all(coded, ('sym', 'sub'), split_axis=0, concat_axis=0)]
    pallas_call x1, Pallas kernels: 4.76 us -> 4.28 us  [spectra(): pl.pallas_call(spectrum_kernel, in_specs=[IN_HBM, IN_HBM], out_specs=IN_V...]
  transfers between devices with their start and end apart: 4 -> 4, of which waited for: 2 -> 3; matrix products, arithmetic and copies ran while one was open for 0% -> 0% of each run, Pallas kernels for 14% -> 13%
where the time goes in v4:
time: 33.4 us; the launch traced here: 33.2 us
  blocking collectives  11 us (33%)
  Pallas kernels  9.59 us (29%)
  starting transfers between devices  7.42 us (22%)
  waiting for transfers between devices  4.31 us (13%)
  local copies, waits for them, and re-layouts  0.68 us (2%)
    all_to_all x1, blocking collectives, doppler_paired(): coded = lax.all_to_all(coded, ('sym', 'sub'), split_axis=0, concat_axis=0)  11 us
    ppermute x3, starting transfers between devices, doppler_paired(): lax.ppermute(pieces[d], 'sym', [(i, i ^ d) for i in range(syms)])  4.45 us
    ppermute x3, waiting for transfers between devices, doppler_paired(): lax.ppermute(pieces[d], 'sym', [(i, i ^ d) for i in range(syms)])  4.31 us
    pallas_call x1, Pallas kernels, spectra(): pl.pallas_call(spectrum_kernel, in_specs=[IN_HBM, IN_HBM], out_specs=IN_V...  4.28 us
    pallas_call x1, Pallas kernels, profiles(): pl.pallas_call(functools.partial(profile_kernel, syms, scale), in_specs=[...  3.45 us
    ppermute x1, starting transfers between devices, local(): other = lax.ppermute(own, 'sub', [(0, 1), (1, 0)])  2.97 us
    pallas_call x1, Pallas kernels, doppler_paired(): pl.pallas_call(doppler_kernel, in_specs=[IN_SMEM] + [IN_VMEM] * syms, out...  1.03 us
    pallas_call x1, Pallas kernels, doppler_paired(): pl.pallas_call(join_kernel, in_specs=[IN_VMEM], out_specs=IN_VMEM, out_sh...  0.83 us
  transfers between devices with their start and end apart: 4, of which 3 were waited for; matrix products, arithmetic and copies ran while one was open for 0% of the time, Pallas kernels for 13%

profile of v4, /device:TPU:0, one launch (start us, length us, event | category | flops | bytes accessed | tf_op | source)
XLA Modules:
  0.0 33.2 jit_solution(9763960746147188913)
XLA Ops:
  0.0 3.0 %collective-permute-start = (s32[6,2048]{1,0:T(8,128)}, s32[6,2048]{1,0:T(8,128)S(1)}, u32[]{:S(2)}, u32[]{:S(2)}) collective-permute-start(s32[6,2048]{1,0:T(8,128)} %own_ref.1), channel_id=1, source_target_pairs={{0,1},{1,0},{2,3},{3,2},{4,5},{5,4},{6,7},{7,6},{8,9},{9,8},{10,11... | collective-permute-start | bytes 147464 | tf_op jit(solution)/shard_map/ppermute | solution.py:539
  3.0 0.0 copy-start.1
  3.0 0.7 %copy-done.1 = s32[6]{0:T(128)S(1)} copy-done((s32[6]{0:T(128)S(1)}, s32[6]{0:T(128)}, u32[]{:S(2)}) %copy-start.1) | copy-done | bytes 48
  3.6 0.0 copy-start.5
  3.6 0.0 copy-start.6
  3.7 4.3 %spectra.1.s_ref = f32[6,1,256,256]{3,2,1,0:T(8,128)S(1)} custom-call(s32[6]{0:T(128)S(1)} %copy-done.1, f32[2,6,8,9216]{3,2,1,0:T(8,128)} %bitcast.4), custom_call_target="tpu_custom_call" | custom-call | flops 2000000000 | bytes 8000000 | tf_op jit(solution)/shard_map/spectra/pallas_call | solution.py:436
  7.9 0.1 pad_add_fusion.place_ref
  8.0 0.0 collective-permute-done.other_ref
  8.0 0.0 copy-done
  8.0 0.0 copy-done.2
  8.0 0.0 copy-done.3
  8.0 0.0 copy-done.4
  8.1 0.0 copy-done.5
  8.1 0.0 copy-done.6
  8.1 3.5 %profiles.1 = (f32[6,2,2,8,128]{4,3,2,1,0:T(8,128)S(1)}, s16[13,16,128]{2,1,0:T(8,128)(2,1)S(1)}, s16[13,16,128]{2,1,0:T(8,128)(2,1)S(1)}, s16[13,16,128]{2,1,0:T(8,128)(2,1)S(1)}) custom-call(s32[6]{0:T(128)S(1)} %copy-done.1, s32[6]{0:T(128)S(1)} %copy-done.2, s32[2]{0:T(128)S(1)} %pad_add_fusion.place_ref, f32[6,1,256,256]{3,2,1,0:T(8,128)S(1)} %spectra.1.s_ref, ...), custom_call_target="tpu_custom_call" | custom-call | flops 1000000000 | bytes 4000000 | tf_op jit(solution)/shard_map/profiles/pallas_call | solution.py:469
  11.5 3.7 %collective-permute-start.1 = (s16[13,16,128]{2,1,0:T(8,128)(2,1)S(1)}, s16[13,16,128]{2,1,0:T(8,128)(2,1)S(1)}, u32[]{:S(2)}, u32[]{:S(2)}) collective-permute-start(s16[13,16,128]{2,1,0:T(8,128)(2,1)S(1)} %get-tuple-element.10), channel_id=1, source_target_pairs={{0,6},{2,4},{4,2},{6,0},{1,7},{3,5},{5,3},{7,1},{8,14},{10,12},{12... | collective-permute-start | bytes 159752 | tf_op jit(solution)/shard_map/ppermute | solution.py:504
  15.2 0.0 collective-permute-start.2
  15.2 0.8 %collective-permute-start.3 = (s16[13,16,128]{2,1,0:T(8,128)(2,1)S(1)}, s16[13,16,128]{2,1,0:T(8,128)(2,1)S(1)}, u32[]{:S(2)}, u32[]{:S(2)}) collective-permute-start(s16[13,16,128]{2,1,0:T(8,128)(2,1)S(1)} %get-tuple-element.12), channel_id=1, source_target_pairs={{0,4},{2,6},{4,0},{6,2},{1,5},{3,7},{5,1},{7,3},{8,12},{10,14},{12... | collective-permute-start | bytes 159752 | tf_op jit(solution)/shard_map/ppermute | solution.py:504
  16.0 1.6 %collective-permute-done.1.refs_0_ = s16[13,16,128]{2,1,0:T(8,128)(2,1)S(1)} collective-permute-done((s16[13,16,128]{2,1,0:T(8,128)(2,1)S(1)}, s16[13,16,128]{2,1,0:T(8,128)(2,1)S(1)}, u32[]{:S(2)}, u32[]{:S(2)}) %collective-permute-start.1) | collective-permute-done | bytes 53280 | tf_op jit(solution)/shard_map/ppermute | solution.py:504
  17.6 1.8 %collective-permute-done.2.refs_1_ = s16[13,16,128]{2,1,0:T(8,128)(2,1)S(1)} collective-permute-done((s16[13,16,128]{2,1,0:T(8,128)(2,1)S(1)}, s16[13,16,128]{2,1,0:T(8,128)(2,1)S(1)}, u32[]{:S(2)}, u32[]{:S(2)}) %collective-permute-start.2) | collective-permute-done | bytes 53280 | tf_op jit(solution)/shard_map/ppermute | solution.py:504
  19.3 1.0 %collective-permute-done.3.refs_2_ = s16[13,16,128]{2,1,0:T(8,128)(2,1)S(1)} collective-permute-done((s16[13,16,128]{2,1,0:T(8,128)(2,1)S(1)}, s16[13,16,128]{2,1,0:T(8,128)(2,1)S(1)}, u32[]{:S(2)}, u32[]{:S(2)}) %collective-permute-start.3) | collective-permute-done | bytes 53280 | tf_op jit(solution)/shard_map/ppermute | solution.py:504
  20.3 1.0 %doppler.1 = s16[8,7,16,128]{3,2,1,0:T(8,128)(2,1)S(1)} custom-call(s32[2]{0:T(128)S(1)} %pad_add_fusion.place_ref, f32[6,2,2,8,128]{4,3,2,1,0:T(8,128)S(1)} %get-tuple-element.9.own_ref, s16[13,16,128]{2,1,0:T(8,128)(2,1)S(1)} %collective-permute-done.1.refs_0_, s16[13,16,128]{2,1,0:T(8,128)(2,1)S(1)} %collective-permute-done.2.refs_1_, ...), custom_call_target="tpu_custom_call" | custom-call | tf_op jit(solution)/shard_map/doppler/pallas_call | solution.py:507
  21.3 11.0 %all_to_all.5.piece_ref = s16[8,7,16,128]{3,2,1,0:T(8,128)(2,1)S(1)} all-to-all(s16[8,7,16,128]{3,2,1,0:T(8,128)(2,1)S(1)} %doppler.1), channel_id=1, replica_groups=mesh['chan'=4,'sym'=4,'sub'=2] {'sym','sub'}, dimensions={0} | all-to-all | bytes 458752 | tf_op jit(solution)/shard_map/all_to_all | solution.py:519
  32.4 0.8 %join.1 = f32[2,6,16,512]{3,2,1,0:T(8,128)} custom-call(s16[8,7,16,128]{3,2,1,0:T(8,128)(2,1)S(1)} %all_to_all.5.piece_ref), custom_call_target="tpu_custom_call" | custom-call | tf_op jit(solution)/shard_map/join/pallas_call | solution.py:520
  (4 shorter events, 0.0 us)
Async XLA Ops:
  0.0 8.0 %collective-permute-start = (s32[6,2048]{1,0:T(8,128)}, s32[6,2048]{1,0:T(8,128)S(1)}, u32[]{:S(2)}, u32[]{:S(2)}) collective-permute-start(s32[6,2048]{1,0:T(8,128)} %own_ref.1), channel_id=1, source_target_pairs={{0,1},{1,0},{2,3},{3,2},{4,5},{5,4},{6,7},{7,6},{8,9},{9,8},{10,11... | collective-permute-start | bytes 147464 | tf_op jit(solution)/shard_map/ppermute | solution.py:539
  3.0 0.7 %copy-start.1 = (s32[6]{0:T(128)S(1)}, s32[6]{0:T(128)}, u32[]{:S(2)}) copy-start(s32[6]{0:T(128)} %off_ref.1) | copy-start | bytes 76
  3.6 4.4 %copy-start = (s32[6,2048]{1,0:T(8,128)S(1)}, s32[6,2048]{1,0:T(8,128)}, u32[]{:S(2)}) copy-start(s32[6,2048]{1,0:T(8,128)} %own_ref.1) | copy-start | bytes 147460
  3.6 4.4 %copy-start.2 = (s32[6]{0:T(128)S(1)}, s32[6]{0:T(128)}, u32[]{:S(2)}) copy-start(s32[6]{0:T(128)} %pilot_ref.1) | copy-start | bytes 76
  3.6 4.4 %copy-start.3 = (bf16[256,256]{1,0:T(8,128)(2,1)S(1)}, bf16[256,256]{1,0:T(8,128)(2,1)}, u32[]{:S(2)}) copy-start(bf16[256,256]{1,0:T(8,128)(2,1)} %constant.18.clone.low_ref) | copy-start | bytes 393220
  3.6 4.4 %copy-start.4 = (bf16[256,256]{1,0:T(8,128)(2,1)S(1)}, bf16[256,256]{1,0:T(8,128)(2,1)}, u32[]{:S(2)}) copy-start(bf16[256,256]{1,0:T(8,128)(2,1)} %constant.17.clone.high_ref) | copy-start | bytes 393220
  3.6 4.4 %copy-start.5 = (f32[2,32,128]{2,1,0:T(8,128)S(1)}, f32[2,32,128]{2,1,0:T(8,128)}, u32[]{:S(2)}) copy-start(f32[2,32,128]{2,1,0:T(8,128)} %constant.19.clone.twist_ref) | copy-start | bytes 98308
  3.6 4.4 %copy-start.6 = (bf16[32,512]{1,0:T(8,128)(2,1)S(1)}, bf16[32,512]{1,0:T(8,128)(2,1)}, u32[]{:S(2)}) copy-start(bf16[32,512]{1,0:T(8,128)(2,1)} %constant.16.clone.spot_ref) | copy-start | bytes 98308
  11.5 6.0 %collective-permute-start.1 = (s16[13,16,128]{2,1,0:T(8,128)(2,1)S(1)}, s16[13,16,128]{2,1,0:T(8,128)(2,1)S(1)}, u32[]{:S(2)}, u32[]{:S(2)}) collective-permute-start(s16[13,16,128]{2,1,0:T(8,128)(2,1)S(1)} %get-tuple-element.10), channel_id=1, source_target_pairs={{0,6},{2,4},{4,2},{6,0},{1,7},{3,5},{5,3},{7,1},{8,14},{10,12},{12... | collective-permute-start | bytes 159752 | tf_op jit(solution)/shard_map/ppermute | solution.py:504
  15.2 4.1 %collective-permute-start.2 = (s16[13,16,128]{2,1,0:T(8,128)(2,1)S(1)}, s16[13,16,128]{2,1,0:T(8,128)(2,1)S(1)}, u32[]{:S(2)}, u32[]{:S(2)}) collective-permute-start(s16[13,16,128]{2,1,0:T(8,128)(2,1)S(1)} %get-tuple-element.11), channel_id=1, source_target_pairs={{0,2},{2,0},{4,6},{6,4},{1,3},{3,1},{5,7},{7,5},{8,10},{10,8},{12,... | collective-permute-start | bytes 159752 | tf_op jit(solution)/shard_map/ppermute | solution.py:504
  15.2 5.1 %collective-permute-start.3 = (s16[13,16,128]{2,1,0:T(8,128)(2,1)S(1)}, s16[13,16,128]{2,1,0:T(8,128)(2,1)S(1)}, u32[]{:S(2)}, u32[]{:S(2)}) collective-permute-start(s16[13,16,128]{2,1,0:T(8,128)(2,1)S(1)} %get-tuple-element.12), channel_id=1, source_target_pairs={{0,4},{2,6},{4,0},{6,2},{1,5},{3,7},{5,1},{7,3},{8,12},{10,14},{12... | collective-permute-start | bytes 159752 | tf_op jit(solution)/shard_map/ppermute | solution.py:504

commit v5 on v4

--- a/solution.py
+++ b/solution.py
@@ -156,7 +156,7 @@
     return jnp.where(turned, -c, c), jnp.where(low, -s, s)
 
 
-def spectrum_kernel(off_hbm, x_hbm, out_ref, off_ref, x_ref, high_ref, low_ref, twist_ref, mid_ref, rows_ref, sems):
+def spectrum_kernel(off_hbm, pilot_hbm, x_hbm, out_ref, table_ref, off_ref, pilot_ref, x_ref, high_ref, low_ref, twist_ref, mid_ref, rows_ref, sems):
     symbols, groups = out_ref.shape[:2]
     tones = ACTIVE_TONES // FOLD
     tasks = [(m, g) for m in range(symbols) for g in range(groups)]
@@ -166,8 +166,12 @@
         fetches.append(pltpu.make_async_copy(source, x_ref.at[n], sems.at[n]))
         fetches[-1].start()
         if n == 0:
-            starts = pltpu.make_async_copy(off_hbm, off_ref, sems.at[len(tasks)])
-            starts.start()
+            scalars = [
+                pltpu.make_async_copy(off_hbm, off_ref, sems.at[len(tasks)]),
+                pltpu.make_async_copy(pilot_hbm, pilot_ref, sems.at[len(tasks) + 1]),
+            ]
+            for scalar in scalars:
+                scalar.start()
     row = lax.broadcasted_iota(jnp.int32, (ROWS, WIDE), 0)
     lane = lax.broadcasted_iota(jnp.int32, (ROWS, WIDE), 1)
     for p in range(4):
@@ -185,7 +189,9 @@
         low_ref[lower, :tones], low_ref[lower, tones:] = s_low, c_low
     lane = lax.broadcasted_iota(jnp.int32, (ROWS, LANES), 1)
     halves = WIDE // LANES
-    starts.wait()
+    for scalar in scalars:
+        scalar.wait()
+    symbol_tables(off_ref, pilot_ref, table_ref)
     for n, (m, g) in enumerate(tasks):
         fetches[n].wait()
         off, slot = off_ref[m], n % 2
@@ -225,7 +231,8 @@
     out_ref[...] = split_product(rows_ref, high_ref, low_ref).reshape(out_ref.shape)
 
 
-def symbol_phases(off_ref, symbols):
+def symbol_tables(off_ref, pilot_ref, table_ref):
+    symbols = table_ref.shape[0]
     tones = ACTIVE_TONES // FOLD
     row = lax.broadcasted_iota(jnp.int32, (ROWS, tones), 0)
     lane = lax.broadcasted_iota(jnp.int32, (ROWS, tones), 1)
@@ -233,13 +240,30 @@
     for m in range(symbols):
         by_row = jnp.where(row == m, off_ref[m], by_row)
         by_lane = jnp.where(lane == m, off_ref[m], by_lane)
-
-    by_lanes = phase(by_row * (LOWEST + FOLD * lane), WHOLE)
-    return by_lanes, [phase(by_lane * (p + 4 * row), WHOLE) for p in range(4)]
+    lane_re, lane_im = phase(by_row * (LOWEST + FOLD * lane), WHOLE)
+    row_phases = [phase(by_lane * (p + 4 * row), WHOLE) for p in range(4)]
+    span = SMOOTH_HALFSPAN + 1
+    for m in range(symbols):
+        offset = pilot_ref[m]
+        first_after = ACTIVE_TONES + lax.rem(offset + PSP * ACTIVE_TONES - ACTIVE_TONES, PSP)
+        a, b = lane_re[m : m + 1, :], lane_im[m : m + 1, :]
+        for p in range(4):
+            at = slice(p * 8, p * 8 + 8)
+            c, s = row_phases[p][0][:, m : m + 1], row_phases[p][1][:, m : m + 1]
+            table_ref[m, 0, at], table_ref[m, 1, at] = a * c - b * s, a * s + b * c
+            k = p + 4 * row + FOLD * lane
+            is_pilot = lax.rem(k + (PSP - offset), PSP) == 0
+            total = jnp.where(is_pilot, 201.0, 200.0)
+            for i in range(4):
+                before = span - (k - offset + PSP * (i + 1))
+                after = span - (first_after + PSP * i - k)
+                total -= (jnp.maximum(before, 0) + jnp.maximum(after, 0)).astype(jnp.float32)
+            table_ref[m, 2, at] = 1.0 / total
+            table_ref[m, 3, at] = jnp.where(is_pilot, 1.0, 0.0)
 
 
 def profile_kernel(
-    syms, scale, off_ref, pilot_ref, place_ref, s_ref, own_ref, other_ref, spot_ref, high_ref, low_ref, twist_ref, *refs
+    syms, scale, pilot_ref, place_ref, s_ref, table_ref, own_ref, other_ref, spot_ref, high_ref, low_ref, twist_ref, *refs
 ):
     outs = refs[: max(syms, 1)]
     flat_ref, turned_ref, gain_ref, ratio_ref, num_ref, rows_ref, range_ref, prof_ref = refs[max(syms, 1) :]
@@ -251,7 +275,6 @@
         own, other = own_ref[:, at], other_ref[:, at]
         flat_ref[j, :symbols] = jnp.where(swapped, other, own).astype(jnp.float32)
         flat_ref[FOLD // 2 + j, :symbols] = jnp.where(swapped, own, other).astype(jnp.float32)
-    (lane_re, lane_im), row_phases = symbol_phases(off_ref, symbols)
 
     for m in range(symbols):
         slot = m % 2
@@ -261,10 +284,7 @@
         turned_ref[slot] = sum(
             spread[FOLD * l : FOLD * (l + 1), tones * l : tones * (l + 1)] for l in range(LANES // FOLD)
         )
-        row = lax.broadcasted_iota(jnp.int32, (ROWS, tones), 0)
         lane = lax.broadcasted_iota(jnp.int32, (ROWS, tones), 1)
-        first_after = ACTIVE_TONES + lax.rem(offset + PSP * ACTIVE_TONES - ACTIVE_TONES, PSP)
-        span = SMOOTH_HALFSPAN + 1
         for p in range(4):
             at = slice(p * 8, p * 8 + 8)
             index = turned_ref[slot, pl.ds(p, 8, stride=4), :]
@@ -272,20 +292,9 @@
             level_re = 2.0 * (index - 8.0 * high_bits) - 7.0
             level_im = 2.0 * high_bits - 7.0
             factor = scale / (level_re * level_re + level_im * level_im)
-            a, b = lane_re[m : m + 1, :], lane_im[m : m + 1, :]
-            c, s = row_phases[p][0][:, m : m + 1], row_phases[p][1][:, m : m + 1]
-            c, s = a * c - b * s, a * s + b * c
+            c, s = table_ref[m, 0, at], table_ref[m, 1, at]
             gain_ref[slot, 0, at] = (c * level_re + s * level_im) * factor
             gain_ref[slot, 1, at] = (s * level_re - c * level_im) * factor
-            k = p + 4 * row + FOLD * lane
-            is_pilot = lax.rem(k + (PSP - offset), PSP) == 0
-            total = jnp.where(is_pilot, 201.0, 200.0)
-            for i in range(4):
-                before = span - (k - offset + PSP * (i + 1))
-                after = span - (first_after + PSP * i - k)
-                total -= (jnp.maximum(before, 0) + jnp.maximum(after, 0)).astype(jnp.float32)
-            gain_ref[slot, 2, at] = 1.0 / total
-            gain_ref[slot, 3, at] = jnp.where(is_pilot, 1.0, 0.0)
 
         for g in range(groups):
             base = (m * groups + g) * FOLD * ROWS
@@ -300,7 +309,7 @@
             r = offset & 3
             for part in range(2):
                 picked = [
-                    ratio_ref[slot, part, r * 8 + a] * gain_ref[slot, 3, pl.ds(r * 8 + a, 1), :] for a in range(8)
+                    ratio_ref[slot, part, r * 8 + a] * table_ref[m, 3, pl.ds(r * 8 + a, 1), :] for a in range(8)
                 ]
 
                 def pilot(i):
@@ -326,7 +335,7 @@
                 for part in range(2):
                     pair = []
                     for n in (i, i + 1):
-                        smooth = num_ref[slot, part, (n // 8) * 10 + n % 8 + 1] * gain_ref[slot, 2, n : n + 1, :]
+                        smooth = num_ref[slot, part, (n // 8) * 10 + n % 8 + 1] * table_ref[m, 2, n : n + 1, :]
                         pair.append(ratio_ref[slot, part, n] - smooth)
                     high, low = split_rows(jnp.concatenate(pair, axis=0))
                     at = slice(base + i * ROWS, base + (i + 2) * ROWS)
@@ -429,15 +438,16 @@
 IN_HBM = pl.BlockSpec(memory_space=pltpu.HBM)
 
 
-def spectra(windows, cp_offset):
+def spectra(windows, cp_offset, pilot_offsets):
     _, symbols, channels, record = windows.shape
     groups = channels // ROWS
     tones = ACTIVE_TONES // FOLD
     return pl.pallas_call(
         spectrum_kernel,
-        in_specs=[IN_HBM, IN_HBM],
-        out_specs=IN_VMEM,
+        in_specs=[IN_HBM] * 3,
+        out_specs=[IN_VMEM] * 2,
         scratch_shapes=[
+            pltpu.SMEM((symbols,), jnp.int32),
             pltpu.SMEM((symbols,), jnp.int32),
             pltpu.VMEM((symbols * groups, 2, ROWS, record), jnp.float32),
             pltpu.VMEM((2 * WIDE, 2 * tones), jnp.bfloat16),
@@ -445,16 +455,19 @@
             pltpu.VMEM((2, FOLD, WIDE), jnp.float32),
             pltpu.VMEM((2, WIDE // LANES, 4, 8, 2, ROWS, LANES), jnp.float32),
             pltpu.VMEM((symbols * groups * FOLD * ROWS, 4 * WIDE), jnp.bfloat16),
-            pltpu.SemaphoreType.DMA((symbols * groups + 1,)),
+            pltpu.SemaphoreType.DMA((symbols * groups + 2,)),
         ],
-        out_shape=jax.ShapeDtypeStruct((symbols, groups, FOLD * ROWS, 2 * tones), jnp.float32),
+        out_shape=[
+            jax.ShapeDtypeStruct((symbols, groups, FOLD * ROWS, 2 * tones), jnp.float32),
+            jax.ShapeDtypeStruct((symbols, 4, FOLD, tones), jnp.float32),
+        ],
         compiler_params=pltpu.CompilerParams(vmem_limit_bytes=SPECTRA_VMEM_LIMIT),
         cost_estimate=pl.CostEstimate(flops=2 * 10**9, bytes_accessed=8 * 10**6, transcendentals=0),
         name="spectra",
-    )(cp_offset, windows)
-
-
-def profiles(spectrum, own, other, pilot_offsets, cp_offset, places, syms, scale):
+    )(*(pltpu.with_memory_space_constraint(a, pltpu.HBM) for a in (cp_offset, pilot_offsets, windows)))
+
+
+def profiles(spectrum, tables, own, other, pilot_offsets, places, syms, scale):
     symbols, groups = spectrum.shape[:2]
     high, low, twist = range_tables()
     tones = ACTIVE_TONES // FOLD
@@ -468,12 +481,12 @@
         outs = [jax.ShapeDtypeStruct((symbols, groups, 2, RANGE_ROWS, ROWS, LANES), jnp.float32)]
     return pl.pallas_call(
         functools.partial(profile_kernel, syms, scale),
-        in_specs=[IN_SMEM] * 3 + [IN_VMEM] * 7,
+        in_specs=[IN_SMEM] * 2 + [IN_VMEM] * 8,
         out_specs=[IN_VMEM] * len(outs),
         scratch_shapes=[
             pltpu.VMEM((FOLD, ROWS, LANES), jnp.float32),
             pltpu.VMEM((2, FOLD, tones), jnp.float32),
-            pltpu.VMEM((2, 4, FOLD, tones), jnp.float32),
+            pltpu.VMEM((2, 2, FOLD, tones), jnp.float32),
             pltpu.VMEM((2, 2, FOLD, ROWS, tones), jnp.float32),
             pltpu.VMEM((2, 2, 40, ROWS, tones), jnp.float32),
             pltpu.VMEM((symbols * groups * FOLD * ROWS, 4 * tones), jnp.bfloat16),
@@ -484,7 +497,7 @@
         compiler_params=pltpu.CompilerParams(vmem_limit_bytes=VMEM_LIMIT),
         cost_estimate=pl.CostEstimate(flops=10**9, bytes_accessed=4 * 10**6, transcendentals=0),
         name="profiles",
-    )(cp_offset, pilot_offsets, places, spectrum, own, other, spot, high, low, twist)
+    )(pilot_offsets, places, spectrum, tables, own, other, spot, high, low, twist)
 
 
 def doppler_plain(own_profiles, symbols):
@@ -545,11 +558,11 @@
     short = -channels % ROWS
     if short:
         windows = jnp.pad(windows, ((0, 0), (0, 0), (0, short), (0, 0)))
-    spectrum = spectra(windows, cp_offset)
+    spectrum, tables = spectra(windows, cp_offset, pilot_offsets)
     scale = ROOT_FORTYTWO / math.sqrt(WHOLE * ACTIVE_TONES * symbols * syms)
     places = jnp.stack([place, swapped])
     got = profiles(
-        spectrum, own, other, pilot_offsets, cp_offset, places, syms if paired else 0, scale
+        spectrum, tables, own, other, pilot_offsets, places, syms if paired else 0, scale
     )
     if paired:
         return doppler_paired(got, places, syms, subs)

time: 33.4 us -> 32.6 us (0.976)
  local copies, waits for them, and re-layouts: 0.68 us -> 0.03 us
    unnamed x14 -> x12, local copies, waits for them, and re-layouts: 0.68 us -> 0.03 us
where the time goes in v5:
time: 32.6 us; the launch traced here: 32.4 us
  blocking collectives  11 us (34%)
  Pallas kernels  9.47 us (29%)
  starting transfers between devices  7.42 us (23%)
  waiting for transfers between devices  4.3 us (13%)
    all_to_all x1, blocking collectives, doppler_paired(): coded = lax.all_to_all(coded, ('sym', 'sub'), split_axis=0, concat_axis=0)  11 us
    ppermute x3, starting transfers between devices, doppler_paired(): lax.ppermute(pieces[d], 'sym', [(i, i ^ d) for i in range(syms)])  4.45 us
    pallas_call x1, Pallas kernels, spectra(): pl.pallas_call(spectrum_kernel, in_specs=[IN_HBM] * 3, out_specs=[IN_VMEM...  4.32 us
    ppermute x3, waiting for transfers between devices, doppler_paired(): lax.ppermute(pieces[d], 'sym', [(i, i ^ d) for i in range(syms)])  4.3 us
    pallas_call x1, Pallas kernels, profiles(): pl.pallas_call(functools.partial(profile_kernel, syms, scale), in_specs=[...  3.29 us
    ppermute x1, starting transfers between devices, local(): other = lax.ppermute(own, 'sub', [(0, 1), (1, 0)])  2.97 us
    pallas_call x1, Pallas kernels, doppler_paired(): pl.pallas_call(doppler_kernel, in_specs=[IN_SMEM] + [IN_VMEM] * syms, out...  1.03 us
    pallas_call x1, Pallas kernels, doppler_paired(): pl.pallas_call(join_kernel, in_specs=[IN_VMEM], out_specs=IN_VMEM, out_sh...  0.83 us
  transfers between devices with their start and end apart: 4, of which 3 were waited for; matrix products, arithmetic and copies ran while one was open for 0% of the time, Pallas kernels for 13%

profile of v5, /device:TPU:0, one launch (start us, length us, event | category | flops | bytes accessed | tf_op | source)
XLA Modules:
  0.0 32.4 jit_solution(2013291608928331125)
XLA Ops:
  0.0 3.0 %collective-permute-start = (s32[6,2048]{1,0:T(8,128)}, s32[6,2048]{1,0:T(8,128)S(1)}, u32[]{:S(2)}, u32[]{:S(2)}) collective-permute-start(s32[6,2048]{1,0:T(8,128)} %own_ref.1), channel_id=1, source_target_pairs={{0,1},{1,0},{2,3},{3,2},{4,5},{5,4},{6,7},{7,6},{8,9},{9,8},{10,11... | collective-permute-start | bytes 147464 | tf_op jit(solution)/shard_map/ppermute | solution.py:552
  3.0 0.0 copy-start
  3.0 0.0 copy-start.1
  3.0 0.0 copy-start.4
  3.0 0.0 copy-start.5
  3.0 4.3 %spectra.1 = (f32[6,1,256,256]{3,2,1,0:T(8,128)S(1)}, f32[6,4,32,128]{3,2,1,0:T(8,128)S(1)}) custom-call(s32[6]{0:T(128)} %off_hbm.1, s32[6]{0:T(128)} %pilot_ref.1, f32[2,6,8,9216]{3,2,1,0:T(8,128)} %bitcast.4), custom_call_target="tpu_custom_call" | custom-call | flops 2000000000 | bytes 8000000 | tf_op jit(solution)/shard_map/spectra/pallas_call | solution.py:445
  7.3 0.1 pad_add_fusion.place_ref
  7.4 0.0 collective-permute-done.other_ref
  7.4 0.0 copy-done
  7.4 0.0 copy-done.1
  7.4 0.0 copy-done.2
  7.4 0.0 copy-done.3
  7.4 0.0 copy-done.4
  7.5 0.0 copy-done.5
  7.5 3.3 %profiles.1 = (f32[6,2,2,8,128]{4,3,2,1,0:T(8,128)S(1)}, s16[13,16,128]{2,1,0:T(8,128)(2,1)S(1)}, s16[13,16,128]{2,1,0:T(8,128)(2,1)S(1)}, s16[13,16,128]{2,1,0:T(8,128)(2,1)S(1)}) custom-call(s32[6]{0:T(128)S(1)} %copy-done.1, s32[2]{0:T(128)S(1)} %pad_add_fusion.place_ref, f32[6,1,256,256]{3,2,1,0:T(8,128)S(1)} %get-tuple-element.11.s_ref, ...), custom_call_target="tpu_custom_call" | custom-call | flops 1000000000 | bytes 4000000 | tf_op jit(solution)/shard_map/profiles/pallas_call | solution.py:482
  10.8 3.7 %collective-permute-start.1 = (s16[13,16,128]{2,1,0:T(8,128)(2,1)S(1)}, s16[13,16,128]{2,1,0:T(8,128)(2,1)S(1)}, u32[]{:S(2)}, u32[]{:S(2)}) collective-permute-start(s16[13,16,128]{2,1,0:T(8,128)(2,1)S(1)} %get-tuple-element.14), channel_id=1, source_target_pairs={{0,6},{2,4},{4,2},{6,0},{1,7},{3,5},{5,3},{7,1},{8,14},{10,12},{12... | collective-permute-start | bytes 159752 | tf_op jit(solution)/shard_map/ppermute | solution.py:517
  14.4 0.0 collective-permute-start.2
  14.4 0.8 %collective-permute-start.3 = (s16[13,16,128]{2,1,0:T(8,128)(2,1)S(1)}, s16[13,16,128]{2,1,0:T(8,128)(2,1)S(1)}, u32[]{:S(2)}, u32[]{:S(2)}) collective-permute-start(s16[13,16,128]{2,1,0:T(8,128)(2,1)S(1)} %get-tuple-element.16), channel_id=1, source_target_pairs={{0,4},{2,6},{4,0},{6,2},{1,5},{3,7},{5,1},{7,3},{8,12},{10,14},{12... | collective-permute-start | bytes 159752 | tf_op jit(solution)/shard_map/ppermute | solution.py:517
  15.2 1.6 %collective-permute-done.1.refs_0_ = s16[13,16,128]{2,1,0:T(8,128)(2,1)S(1)} collective-permute-done((s16[13,16,128]{2,1,0:T(8,128)(2,1)S(1)}, s16[13,16,128]{2,1,0:T(8,128)(2,1)S(1)}, u32[]{:S(2)}, u32[]{:S(2)}) %collective-permute-start.1) | collective-permute-done | bytes 53280 | tf_op jit(solution)/shard_map/ppermute | solution.py:517
  16.8 1.7 %collective-permute-done.2.refs_1_ = s16[13,16,128]{2,1,0:T(8,128)(2,1)S(1)} collective-permute-done((s16[13,16,128]{2,1,0:T(8,128)(2,1)S(1)}, s16[13,16,128]{2,1,0:T(8,128)(2,1)S(1)}, u32[]{:S(2)}, u32[]{:S(2)}) %collective-permute-start.2) | collective-permute-done | bytes 53280 | tf_op jit(solution)/shard_map/ppermute | solution.py:517
  18.6 1.0 %collective-permute-done.3.refs_2_ = s16[13,16,128]{2,1,0:T(8,128)(2,1)S(1)} collective-permute-done((s16[13,16,128]{2,1,0:T(8,128)(2,1)S(1)}, s16[13,16,128]{2,1,0:T(8,128)(2,1)S(1)}, u32[]{:S(2)}, u32[]{:S(2)}) %collective-permute-start.3) | collective-permute-done | bytes 53280 | tf_op jit(solution)/shard_map/ppermute | solution.py:517
  19.5 1.0 %doppler.1 = s16[8,7,16,128]{3,2,1,0:T(8,128)(2,1)S(1)} custom-call(s32[2]{0:T(128)S(1)} %pad_add_fusion.place_ref, f32[6,2,2,8,128]{4,3,2,1,0:T(8,128)S(1)} %get-tuple-element.13.own_ref, s16[13,16,128]{2,1,0:T(8,128)(2,1)S(1)} %collective-permute-done.1.refs_0_, s16[13,16,128]{2,1,0:T(8,128)(2,1)S(1)} %collective-permute-done.2.refs_1_, ...), custom_call_target="tpu_custom_call" | custom-call | tf_op jit(solution)/shard_map/doppler/pallas_call | solution.py:520
  20.5 11.0 %all_to_all.5.piece_ref = s16[8,7,16,128]{3,2,1,0:T(8,128)(2,1)S(1)} all-to-all(s16[8,7,16,128]{3,2,1,0:T(8,128)(2,1)S(1)} %doppler.1), channel_id=1, replica_groups=mesh['chan'=4,'sym'=4,'sub'=2] {'sym','sub'}, dimensions={0} | all-to-all | bytes 458752 | tf_op jit(solution)/shard_map/all_to_all | solution.py:532
  31.6 0.8 %join.1 = f32[2,6,16,512]{3,2,1,0:T(8,128)} custom-call(s16[8,7,16,128]{3,2,1,0:T(8,128)(2,1)S(1)} %all_to_all.5.piece_ref), custom_call_target="tpu_custom_call" | custom-call | tf_op jit(solution)/shard_map/join/pallas_call | solution.py:533
  (2 shorter events, 0.0 us)
Async XLA Ops:
  0.0 7.4 %collective-permute-start = (s32[6,2048]{1,0:T(8,128)}, s32[6,2048]{1,0:T(8,128)S(1)}, u32[]{:S(2)}, u32[]{:S(2)}) collective-permute-start(s32[6,2048]{1,0:T(8,128)} %own_ref.1), channel_id=1, source_target_pairs={{0,1},{1,0},{2,3},{3,2},{4,5},{5,4},{6,7},{7,6},{8,9},{9,8},{10,11... | collective-permute-start | bytes 147464 | tf_op jit(solution)/shard_map/ppermute | solution.py:552
  3.0 4.4 %copy-start = (s32[6,2048]{1,0:T(8,128)S(1)}, s32[6,2048]{1,0:T(8,128)}, u32[]{:S(2)}) copy-start(s32[6,2048]{1,0:T(8,128)} %own_ref.1) | copy-start | bytes 147460
  3.0 4.4 %copy-start.1 = (s32[6]{0:T(128)S(1)}, s32[6]{0:T(128)}, u32[]{:S(2)}) copy-start(s32[6]{0:T(128)} %pilot_ref.1) | copy-start | bytes 76
  3.0 4.5 %copy-start.2 = (bf16[256,256]{1,0:T(8,128)(2,1)S(1)}, bf16[256,256]{1,0:T(8,128)(2,1)}, u32[]{:S(2)}) copy-start(bf16[256,256]{1,0:T(8,128)(2,1)} %constant.18.clone.low_ref) | copy-start | bytes 393220
  3.0 4.5 %copy-start.3 = (bf16[256,256]{1,0:T(8,128)(2,1)S(1)}, bf16[256,256]{1,0:T(8,128)(2,1)}, u32[]{:S(2)}) copy-start(bf16[256,256]{1,0:T(8,128)(2,1)} %constant.17.clone.high_ref) | copy-start | bytes 393220
  3.0 4.5 %copy-start.4 = (f32[2,32,128]{2,1,0:T(8,128)S(1)}, f32[2,32,128]{2,1,0:T(8,128)}, u32[]{:S(2)}) copy-start(f32[2,32,128]{2,1,0:T(8,128)} %constant.19.clone.twist_ref) | copy-start | bytes 98308
  3.0 4.5 %copy-start.5 = (bf16[32,512]{1,0:T(8,128)(2,1)S(1)}, bf16[32,512]{1,0:T(8,128)(2,1)}, u32[]{:S(2)}) copy-start(bf16[32,512]{1,0:T(8,128)(2,1)} %constant.16.clone.spot_ref) | copy-start | bytes 98308
  10.8 6.0 %collective-permute-start.1 = (s16[13,16,128]{2,1,0:T(8,128)(2,1)S(1)}, s16[13,16,128]{2,1,0:T(8,128)(2,1)S(1)}, u32[]{:S(2)}, u32[]{:S(2)}) collective-permute-start(s16[13,16,128]{2,1,0:T(8,128)(2,1)S(1)} %get-tuple-element.14), channel_id=1, source_target_pairs={{0,6},{2,4},{4,2},{6,0},{1,7},{3,5},{5,3},{7,1},{8,14},{10,12},{12... | collective-permute-start | bytes 159752 | tf_op jit(solution)/shard_map/ppermute | solution.py:517
  14.4 4.1 %collective-permute-start.2 = (s16[13,16,128]{2,1,0:T(8,128)(2,1)S(1)}, s16[13,16,128]{2,1,0:T(8,128)(2,1)S(1)}, u32[]{:S(2)}, u32[]{:S(2)}) collective-permute-start(s16[13,16,128]{2,1,0:T(8,128)(2,1)S(1)} %get-tuple-element.15), channel_id=1, source_target_pairs={{0,2},{2,0},{4,6},{6,4},{1,3},{3,1},{5,7},{7,5},{8,10},{10,8},{12,... | collective-permute-start | bytes 159752 | tf_op jit(solution)/shard_map/ppermute | solution.py:517
  14.4 5.1 %collective-permute-start.3 = (s16[13,16,128]{2,1,0:T(8,128)(2,1)S(1)}, s16[13,16,128]{2,1,0:T(8,128)(2,1)S(1)}, u32[]{:S(2)}, u32[]{:S(2)}) collective-permute-start(s16[13,16,128]{2,1,0:T(8,128)(2,1)S(1)} %get-tuple-element.16), channel_id=1, source_target_pairs={{0,4},{2,6},{4,0},{6,2},{1,5},{3,7},{5,1},{7,3},{8,12},{10,14},{12... | collective-permute-start | bytes 159752 | tf_op jit(solution)/shard_map/ppermute | solution.py:517

commit v6 on v5

--- a/solution.py
+++ b/solution.py
@@ -372,12 +372,13 @@
                     if d == 0:
                         outs[0][m, h] = prof_ref[slot, row]
                         continue
+                    to = 2 * (m * (RANGE_ROWS // syms) + h)
                     packed = [encode(prof_ref[slot, row, part], code) for part in range(2)]
-                    outs[d][m * (RANGE_ROWS // syms) + h] = jnp.concatenate(packed, axis=0).astype(jnp.int16)
+                    outs[d][to : to + 2] = jnp.stack(packed).astype(jnp.int16)
     if syms:
-        packed = jnp.concatenate([codes, codes], axis=0).astype(jnp.int32).astype(jnp.int16)
+        packed = codes.astype(jnp.int32).astype(jnp.int16)
         for d in range(1, syms):
-            outs[d][symbols * (RANGE_ROWS // syms)] = packed
+            outs[d][2 * symbols * (RANGE_ROWS // syms)] = packed
 
 
 SEND_ORDER = (3, 1, 2)
@@ -390,12 +391,12 @@
     own = place_ref[0]
     turned_ref[own] = own_ref[...]
     for d, piece in zip(SEND_ORDER, pieces):
-        codes = piece[symbols * rows].astype(jnp.int32).astype(jnp.float32)
+        codes = piece[2 * symbols * rows].astype(jnp.int32).astype(jnp.float32)
         for m in range(symbols):
             code = codes[:, m : m + 1]
             for h in range(rows):
-                value = decode(piece[m * rows + h], code)
-                turned_ref[own ^ d, m, h, 0], turned_ref[own ^ d, m, h, 1] = value[:ROWS], value[ROWS:]
+                to = 2 * (m * rows + h)
+                turned_ref[own ^ d, m, h] = decode(piece[to : to + 2], code)
     for h in range(rows):
         grid, bins = {}, {}
         for m in range(symbols):
@@ -413,9 +414,9 @@
             to = s * rows + h
             for f in range(symbols):
                 packed = [encode(values[f][part], code) for part in range(2)]
-                out_ref[to, f] = jnp.concatenate(packed, axis=0).astype(jnp.int16)
+                out_ref[to, 2 * f : 2 * f + 2] = jnp.stack(packed).astype(jnp.int16)
             codes = jnp.broadcast_to(code, (ROWS, LANES)).astype(jnp.int32)
-            out_ref[to, symbols] = jnp.concatenate([codes, codes], axis=0).astype(jnp.int16)
+            out_ref[to, 2 * symbols] = codes.astype(jnp.int16)
 
 
 def join_kernel(piece_ref, out_ref):
@@ -423,14 +424,13 @@
     subs = channels // ROWS
     for n in range(piece_ref.shape[0]):
         s, u = n // subs, n % subs
-        code = piece_ref[n, symbols].astype(jnp.int32).astype(jnp.float32)
+        code = piece_ref[n, 2 * symbols].astype(jnp.int32).astype(jnp.float32)
         gain = jnp.exp2(code * (1.0 / 64.0)) * (1.0 / 32767.0**2)
         for f in range(symbols):
-            value = piece_ref[n, f].astype(jnp.int32).astype(jnp.float32)
+            value = piece_ref[n, 2 * f : 2 * f + 2].astype(jnp.int32).astype(jnp.float32)
             value = value * jnp.abs(value) * gain
             for part in range(2):
-                at = slice(part * ROWS, (part + 1) * ROWS)
-                out_ref[part, f, u * ROWS : (u + 1) * ROWS, s * LANES : (s + 1) * LANES] = value[at]
+                out_ref[part, f, u * ROWS : (u + 1) * ROWS, s * LANES : (s + 1) * LANES] = value[part]
 
 
 IN_VMEM = pl.BlockSpec(memory_space=pltpu.VMEM)
@@ -475,7 +475,7 @@
     spot = (column % tones == LANES // FOLD * n + column // tones).astype(ml_dtypes.bfloat16)
     if syms:
         rows = RANGE_ROWS // syms
-        piece = jax.ShapeDtypeStruct((symbols * rows + 1, 2 * ROWS, LANES), jnp.int16)
+        piece = jax.ShapeDtypeStruct((2 * symbols * rows + 1, ROWS, LANES), jnp.int16)
         outs = [jax.ShapeDtypeStruct((symbols, rows, 2, ROWS, LANES), jnp.float32)] + [piece] * (syms - 1)
     else:
         outs = [jax.ShapeDtypeStruct((symbols, groups, 2, RANGE_ROWS, ROWS, LANES), jnp.float32)]
@@ -521,7 +521,7 @@
         doppler_kernel,
         in_specs=[IN_SMEM] + [IN_VMEM] * syms,
         out_specs=IN_VMEM,
-        out_shape=jax.ShapeDtypeStruct((syms * subs, symbols + 1, 2 * ROWS, LANES), jnp.int16),
+        out_shape=jax.ShapeDtypeStruct((syms * subs, 2 * symbols + 1, ROWS, LANES), jnp.int16),
         scratch_shapes=[
             pltpu.VMEM((syms, symbols, rows, 2, ROWS, LANES), jnp.float32),
             pltpu.VMEM((rows, syms * symbols, 2, ROWS, LANES), jnp.float32),

time: 32.6 us -> 32.4 us (level)
  no operation moved by 1% of the time
where the time goes in v6:
time: 32.4 us; the launch traced here: 32.3 us
  blocking collectives  11 us (34%)
  Pallas kernels  9.44 us (29%)
  starting transfers between devices  7.42 us (23%)
  waiting for transfers between devices  4.25 us (13%)
    all_to_all x1, blocking collectives, doppler_paired(): coded = lax.all_to_all(coded, ('sym', 'sub'), split_axis=0, concat_axis=0)  11 us
    ppermute x3, starting transfers between devices, doppler_paired(): lax.ppermute(pieces[d], 'sym', [(i, i ^ d) for i in range(syms)])  4.45 us
    pallas_call x1, Pallas kernels, spectra(): pl.pallas_call(spectrum_kernel, in_specs=[IN_HBM] * 3, out_specs=[IN_VMEM...  4.32 us
    ppermute x3, waiting for transfers between devices, doppler_paired(): lax.ppermute(pieces[d], 'sym', [(i, i ^ d) for i in range(syms)])  4.25 us
    pallas_call x1, Pallas kernels, profiles(): pl.pallas_call(functools.partial(profile_kernel, syms, scale), in_specs=[...  3.3 us
    ppermute x1, starting transfers between devices, local(): other = lax.ppermute(own, 'sub', [(0, 1), (1, 0)])  2.97 us
    pallas_call x1, Pallas kernels, doppler_paired(): pl.pallas_call(doppler_kernel, in_specs=[IN_SMEM] + [IN_VMEM] * syms, out...  1 us
    pallas_call x1, Pallas kernels, doppler_paired(): pl.pallas_call(join_kernel, in_specs=[IN_VMEM], out_specs=IN_VMEM, out_sh...  0.83 us
  transfers between devices with their start and end apart: 4, of which 3 were waited for; matrix products, arithmetic and copies ran while one was open for 0% of the time, Pallas kernels for 13%

profile of v6, /device:TPU:0, one launch (start us, length us, event | category | flops | bytes accessed | tf_op | source)
XLA Modules:
  0.0 32.3 jit_solution(9990483530564371212)
XLA Ops:
  0.0 3.0 %collective-permute-start = (s32[6,2048]{1,0:T(8,128)}, s32[6,2048]{1,0:T(8,128)S(1)}, u32[]{:S(2)}, u32[]{:S(2)}) collective-permute-start(s32[6,2048]{1,0:T(8,128)} %own_ref.1), channel_id=1, source_target_pairs={{0,1},{1,0},{2,3},{3,2},{4,5},{5,4},{6,7},{7,6},{8,9},{9,8},{10,11... | collective-permute-start | bytes 147464 | tf_op jit(solution)/shard_map/ppermute | solution.py:552
  3.0 0.0 copy-start
  3.0 0.0 copy-start.1
  3.0 0.0 copy-start.4
  3.0 0.0 copy-start.5
  3.0 4.3 %spectra.1 = (f32[6,1,256,256]{3,2,1,0:T(8,128)S(1)}, f32[6,4,32,128]{3,2,1,0:T(8,128)S(1)}) custom-call(s32[6]{0:T(128)} %off_hbm.1, s32[6]{0:T(128)} %pilot_ref.1, f32[2,6,8,9216]{3,2,1,0:T(8,128)} %bitcast.4), custom_call_target="tpu_custom_call" | custom-call | flops 2000000000 | bytes 8000000 | tf_op jit(solution)/shard_map/spectra/pallas_call | solution.py:445
  7.3 0.1 pad_add_fusion.place_ref
  7.4 0.0 collective-permute-done.other_ref
  7.4 0.0 copy-done
  7.4 0.0 copy-done.1
  7.4 0.0 copy-done.2
  7.4 0.0 copy-done.3
  7.4 0.0 copy-done.4
  7.5 0.0 copy-done.5
  7.5 3.3 %profiles.1 = (f32[6,2,2,8,128]{4,3,2,1,0:T(8,128)S(1)}, s16[25,8,128]{2,1,0:T(8,128)(2,1)S(1)}, s16[25,8,128]{2,1,0:T(8,128)(2,1)S(1)}, s16[25,8,128]{2,1,0:T(8,128)(2,1)S(1)}) custom-call(s32[6]{0:T(128)S(1)} %copy-done.1, s32[2]{0:T(128)S(1)} %pad_add_fusion.place_ref, f32[6,1,256,256]{3,2,1,0:T(8,128)S(1)} %get-tuple-element.11.s_ref, ...), custom_call_target="tpu_custom_call" | custom-call | flops 1000000000 | bytes 4000000 | tf_op jit(solution)/shard_map/profiles/pallas_call | solution.py:482
  10.8 3.7 %collective-permute-start.1 = (s16[25,8,128]{2,1,0:T(8,128)(2,1)S(1)}, s16[25,8,128]{2,1,0:T(8,128)(2,1)S(1)}, u32[]{:S(2)}, u32[]{:S(2)}) collective-permute-start(s16[25,8,128]{2,1,0:T(8,128)(2,1)S(1)} %get-tuple-element.14), channel_id=1, source_target_pairs={{0,6},{2,4},{4,2},{6,0},{1,7},{3,5},{5,3},{7,1},{8,14},{10,12},{12... | collective-permute-start | bytes 153608 | tf_op jit(solution)/shard_map/ppermute | solution.py:517
  14.4 0.0 collective-permute-start.2
  14.4 0.8 %collective-permute-start.3 = (s16[25,8,128]{2,1,0:T(8,128)(2,1)S(1)}, s16[25,8,128]{2,1,0:T(8,128)(2,1)S(1)}, u32[]{:S(2)}, u32[]{:S(2)}) collective-permute-start(s16[25,8,128]{2,1,0:T(8,128)(2,1)S(1)} %get-tuple-element.16), channel_id=1, source_target_pairs={{0,4},{2,6},{4,0},{6,2},{1,5},{3,7},{5,1},{7,3},{8,12},{10,14},{12... | collective-permute-start | bytes 153608 | tf_op jit(solution)/shard_map/ppermute | solution.py:517
  15.2 1.6 %collective-permute-done.1.refs_0_ = s16[25,8,128]{2,1,0:T(8,128)(2,1)S(1)} collective-permute-done((s16[25,8,128]{2,1,0:T(8,128)(2,1)S(1)}, s16[25,8,128]{2,1,0:T(8,128)(2,1)S(1)}, u32[]{:S(2)}, u32[]{:S(2)}) %collective-permute-start.1) | collective-permute-done | bytes 51232 | tf_op jit(solution)/shard_map/ppermute | solution.py:517
  16.8 1.7 %collective-permute-done.2.refs_1_ = s16[25,8,128]{2,1,0:T(8,128)(2,1)S(1)} collective-permute-done((s16[25,8,128]{2,1,0:T(8,128)(2,1)S(1)}, s16[25,8,128]{2,1,0:T(8,128)(2,1)S(1)}, u32[]{:S(2)}, u32[]{:S(2)}) %collective-permute-start.2) | collective-permute-done | bytes 51232 | tf_op jit(solution)/shard_map/ppermute | solution.py:517
  18.5 0.9 %collective-permute-done.3.refs_2_ = s16[25,8,128]{2,1,0:T(8,128)(2,1)S(1)} collective-permute-done((s16[25,8,128]{2,1,0:T(8,128)(2,1)S(1)}, s16[25,8,128]{2,1,0:T(8,128)(2,1)S(1)}, u32[]{:S(2)}, u32[]{:S(2)}) %collective-permute-start.3) | collective-permute-done | bytes 51232 | tf_op jit(solution)/shard_map/ppermute | solution.py:517
  19.5 1.0 %doppler.1 = s16[8,13,8,128]{3,2,1,0:T(8,128)(2,1)S(1)} custom-call(s32[2]{0:T(128)S(1)} %pad_add_fusion.place_ref, f32[6,2,2,8,128]{4,3,2,1,0:T(8,128)S(1)} %get-tuple-element.13.own_ref, s16[25,8,128]{2,1,0:T(8,128)(2,1)S(1)} %collective-permute-done.1.refs_0_, s16[25,8,128]{2,1,0:T(8,128)(2,1)S(1)} %collective-permute-done.2.refs_1_, ...), custom_call_target="tpu_custom_call" | custom-call | tf_op jit(solution)/shard_map/doppler/pallas_call | solution.py:520
  20.5 11.0 %all_to_all.5.piece_ref = s16[8,13,8,128]{3,2,1,0:T(8,128)(2,1)S(1)} all-to-all(s16[8,13,8,128]{3,2,1,0:T(8,128)(2,1)S(1)} %doppler.1), channel_id=1, replica_groups=mesh['chan'=4,'sym'=4,'sub'=2] {'sym','sub'}, dimensions={0} | all-to-all | bytes 425984 | tf_op jit(solution)/shard_map/all_to_all | solution.py:532
  31.4 0.8 %join.1 = f32[2,6,16,512]{3,2,1,0:T(8,128)} custom-call(s16[8,13,8,128]{3,2,1,0:T(8,128)(2,1)S(1)} %all_to_all.5.piece_ref), custom_call_target="tpu_custom_call" | custom-call | tf_op jit(solution)/shard_map/join/pallas_call | solution.py:533
  (2 shorter events, 0.0 us)
Async XLA Ops:
  0.0 7.4 %collective-permute-start = (s32[6,2048]{1,0:T(8,128)}, s32[6,2048]{1,0:T(8,128)S(1)}, u32[]{:S(2)}, u32[]{:S(2)}) collective-permute-start(s32[6,2048]{1,0:T(8,128)} %own_ref.1), channel_id=1, source_target_pairs={{0,1},{1,0},{2,3},{3,2},{4,5},{5,4},{6,7},{7,6},{8,9},{9,8},{10,11... | collective-permute-start | bytes 147464 | tf_op jit(solution)/shard_map/ppermute | solution.py:552
  3.0 4.4 %copy-start = (s32[6,2048]{1,0:T(8,128)S(1)}, s32[6,2048]{1,0:T(8,128)}, u32[]{:S(2)}) copy-start(s32[6,2048]{1,0:T(8,128)} %own_ref.1) | copy-start | bytes 147460
  3.0 4.4 %copy-start.1 = (s32[6]{0:T(128)S(1)}, s32[6]{0:T(128)}, u32[]{:S(2)}) copy-start(s32[6]{0:T(128)} %pilot_ref.1) | copy-start | bytes 76
  3.0 4.5 %copy-start.2 = (bf16[256,256]{1,0:T(8,128)(2,1)S(1)}, bf16[256,256]{1,0:T(8,128)(2,1)}, u32[]{:S(2)}) copy-start(bf16[256,256]{1,0:T(8,128)(2,1)} %constant.18.clone.low_ref) | copy-start | bytes 393220
  3.0 4.5 %copy-start.3 = (bf16[256,256]{1,0:T(8,128)(2,1)S(1)}, bf16[256,256]{1,0:T(8,128)(2,1)}, u32[]{:S(2)}) copy-start(bf16[256,256]{1,0:T(8,128)(2,1)} %constant.17.clone.high_ref) | copy-start | bytes 393220
  3.0 4.5 %copy-start.4 = (f32[2,32,128]{2,1,0:T(8,128)S(1)}, f32[2,32,128]{2,1,0:T(8,128)}, u32[]{:S(2)}) copy-start(f32[2,32,128]{2,1,0:T(8,128)} %constant.19.clone.twist_ref) | copy-start | bytes 98308
  3.0 4.5 %copy-start.5 = (bf16[32,512]{1,0:T(8,128)(2,1)S(1)}, bf16[32,512]{1,0:T(8,128)(2,1)}, u32[]{:S(2)}) copy-start(bf16[32,512]{1,0:T(8,128)(2,1)} %constant.16.clone.spot_ref) | copy-start | bytes 98308
  10.8 6.0 %collective-permute-start.1 = (s16[25,8,128]{2,1,0:T(8,128)(2,1)S(1)}, s16[25,8,128]{2,1,0:T(8,128)(2,1)S(1)}, u32[]{:S(2)}, u32[]{:S(2)}) collective-permute-start(s16[25,8,128]{2,1,0:T(8,128)(2,1)S(1)} %get-tuple-element.14), channel_id=1, source_target_pairs={{0,6},{2,4},{4,2},{6,0},{1,7},{3,5},{5,3},{7,1},{8,14},{10,12},{12... | collective-permute-start | bytes 153608 | tf_op jit(solution)/shard_map/ppermute | solution.py:517
  14.4 4.1 %collective-permute-start.2 = (s16[25,8,128]{2,1,0:T(8,128)(2,1)S(1)}, s16[25,8,128]{2,1,0:T(8,128)(2,1)S(1)}, u32[]{:S(2)}, u32[]{:S(2)}) collective-permute-start(s16[25,8,128]{2,1,0:T(8,128)(2,1)S(1)} %get-tuple-element.15), channel_id=1, source_target_pairs={{0,2},{2,0},{4,6},{6,4},{1,3},{3,1},{5,7},{7,5},{8,10},{10,8},{12,... | collective-permute-start | bytes 153608 | tf_op jit(solution)/shard_map/ppermute | solution.py:517
  14.4 5.0 %collective-permute-start.3 = (s16[25,8,128]{2,1,0:T(8,128)(2,1)S(1)}, s16[25,8,128]{2,1,0:T(8,128)(2,1)S(1)}, u32[]{:S(2)}, u32[]{:S(2)}) collective-permute-start(s16[25,8,128]{2,1,0:T(8,128)(2,1)S(1)} %get-tuple-element.16), channel_id=1, source_target_pairs={{0,4},{2,6},{4,0},{6,2},{1,5},{3,7},{5,1},{7,3},{8,12},{10,14},{12... | collective-permute-start | bytes 153608 | tf_op jit(solution)/shard_map/ppermute | solution.py:517

commit v7 on v5

--- a/solution.py
+++ b/solution.py
@@ -263,13 +263,14 @@
 
 
 def profile_kernel(
-    syms, scale, pilot_ref, place_ref, s_ref, table_ref, own_ref, other_ref, spot_ref, high_ref, low_ref, twist_ref, *refs
+    syms, scale, pilot_ref, s_ref, table_ref, own_ref, other_ref, spot_ref, high_ref, low_ref, twist_ref, *refs
 ):
     outs = refs[: max(syms, 1)]
     flat_ref, turned_ref, gain_ref, ratio_ref, num_ref, rows_ref, range_ref, prof_ref = refs[max(syms, 1) :]
     symbols, groups = s_ref.shape[:2]
     tones = ACTIVE_TONES // FOLD
-    own_place, swapped = place_ref[0], place_ref[1] > 0
+    own_place = lax.axis_index("sym")
+    swapped = lax.axis_index("sub") > 0 if syms else False
     for j in range(FOLD // 2):
         at = slice(j * LANES, (j + 1) * LANES)
         own, other = own_ref[:, at], other_ref[:, at]
@@ -277,7 +278,7 @@
         flat_ref[FOLD // 2 + j, :symbols] = jnp.where(swapped, own, other).astype(jnp.float32)
 
     for m in range(symbols):
-        slot = m % 2
+        slot = m
         offset = pilot_ref[m]
         stood = flat_ref[:, m, :].T.astype(jnp.bfloat16)
         spread = dot(stood, spot_ref[...])
@@ -347,7 +348,7 @@
     codes = jnp.zeros((ROWS, LANES), jnp.float32)
     for m in range(symbols):
         for g in range(groups):
-            base, slot = (m * groups + g) * FOLD * ROWS, m % 2
+            base, slot = (m * groups + g) * FOLD * ROWS, m
             sums = None
             for p in range(4):
                 x = []
@@ -383,11 +384,11 @@
 SEND_ORDER = (3, 1, 2)
 
 
-def doppler_kernel(place_ref, own_ref, *refs):
+def doppler_kernel(own_ref, *refs):
     pieces, (out_ref, turned_ref, spread_ref) = refs[:3], refs[3:]
     symbols, rows = own_ref.shape[:2]
     syms = 4
-    own = place_ref[0]
+    own = lax.axis_index("sym")
     turned_ref[own] = own_ref[...]
     for d, piece in zip(SEND_ORDER, pieces):
         codes = piece[symbols * rows].astype(jnp.int32).astype(jnp.float32)
@@ -467,7 +468,7 @@
     )(*(pltpu.with_memory_space_constraint(a, pltpu.HBM) for a in (cp_offset, pilot_offsets, windows)))
 
 
-def profiles(spectrum, tables, own, other, pilot_offsets, places, syms, scale):
+def profiles(spectrum, tables, own, other, pilot_offsets, syms, scale):
     symbols, groups = spectrum.shape[:2]
     high, low, twist = range_tables()
     tones = ACTIVE_TONES // FOLD
@@ -481,23 +482,23 @@
         outs = [jax.ShapeDtypeStruct((symbols, groups, 2, RANGE_ROWS, ROWS, LANES), jnp.float32)]
     return pl.pallas_call(
         functools.partial(profile_kernel, syms, scale),
-        in_specs=[IN_SMEM] * 2 + [IN_VMEM] * 8,
+        in_specs=[IN_SMEM] + [IN_VMEM] * 8,
         out_specs=[IN_VMEM] * len(outs),
         scratch_shapes=[
             pltpu.VMEM((FOLD, ROWS, LANES), jnp.float32),
-            pltpu.VMEM((2, FOLD, tones), jnp.float32),
-            pltpu.VMEM((2, 2, FOLD, tones), jnp.float32),
-            pltpu.VMEM((2, 2, FOLD, ROWS, tones), jnp.float32),
-            pltpu.VMEM((2, 2, 40, ROWS, tones), jnp.float32),
+            pltpu.VMEM((symbols, FOLD, tones), jnp.float32),
+            pltpu.VMEM((symbols, 2, FOLD, tones), jnp.float32),
+            pltpu.VMEM((symbols, 2, FOLD, ROWS, tones), jnp.float32),
+            pltpu.VMEM((symbols, 2, 40, ROWS, tones), jnp.float32),
             pltpu.VMEM((symbols * groups * FOLD * ROWS, 4 * tones), jnp.bfloat16),
             pltpu.VMEM((symbols * groups * FOLD * ROWS, 2 * LANES), jnp.float32),
-            pltpu.VMEM((2, RANGE_ROWS, 2, ROWS, LANES), jnp.float32),
+            pltpu.VMEM((symbols, RANGE_ROWS, 2, ROWS, LANES), jnp.float32),
         ],
         out_shape=outs,
         compiler_params=pltpu.CompilerParams(vmem_limit_bytes=VMEM_LIMIT),
         cost_estimate=pl.CostEstimate(flops=10**9, bytes_accessed=4 * 10**6, transcendentals=0),
         name="profiles",
-    )(pilot_offsets, places, spectrum, tables, own, other, spot, high, low, twist)
+    )(pilot_offsets, spectrum, tables, own, other, spot, high, low, twist)
 
 
 def doppler_plain(own_profiles, symbols):
@@ -512,14 +513,14 @@
     return lax.all_to_all(jnp.stack([re, im]), "sym", split_axis=2, concat_axis=3, tiled=True)
 
 
-def doppler_paired(pieces, places, syms, subs):
+def doppler_paired(pieces, syms, subs):
     got = [pieces[0]] + [
         lax.ppermute(pieces[d], "sym", [(i, i ^ d) for i in range(syms)]) for d in SEND_ORDER
     ]
     symbols, rows = got[0].shape[:2]
     coded = pl.pallas_call(
         doppler_kernel,
-        in_specs=[IN_SMEM] + [IN_VMEM] * syms,
+        in_specs=[IN_VMEM] * syms,
         out_specs=IN_VMEM,
         out_shape=jax.ShapeDtypeStruct((syms * subs, symbols + 1, 2 * ROWS, LANES), jnp.int16),
         scratch_shapes=[
@@ -528,7 +529,7 @@
         ],
         compiler_params=pltpu.CompilerParams(vmem_limit_bytes=VMEM_LIMIT),
         name="doppler",
-    )(places, *got)
+    )(*got)
     coded = lax.all_to_all(coded, ("sym", "sub"), split_axis=0, concat_axis=0)
     out = pl.pallas_call(
         join_kernel,
@@ -543,29 +544,26 @@
 
 def local(samples, constellation_index, pilot_offsets, cp_offset):
     syms, subs = lax.axis_size("sym"), lax.axis_size("sub")
-    place, sub = lax.axis_index("sym"), lax.axis_index("sub")
     channels, symbols = samples.shape[1:3]
     paired = syms == 4 and syms * subs == RANGE_ROWS and channels == ROWS and symbols == 6
     half = ACTIVE_TONES // 2
     if paired:
         own = constellation_index
         other = lax.ppermute(own, "sub", [(0, 1), (1, 0)])
-        swapped = sub
     else:
         index = lax.all_gather(constellation_index, "sub", axis=1, tiled=True)
-        own, other, swapped = index[:, :half], index[:, half:], jnp.zeros_like(sub)
+        own, other = index[:, :half], index[:, half:]
     windows = jnp.transpose(samples, (0, 2, 1, 3))
     short = -channels % ROWS
     if short:
         windows = jnp.pad(windows, ((0, 0), (0, 0), (0, short), (0, 0)))
     spectrum, tables = spectra(windows, cp_offset, pilot_offsets)
     scale = ROOT_FORTYTWO / math.sqrt(WHOLE * ACTIVE_TONES * symbols * syms)
-    places = jnp.stack([place, swapped])
     got = profiles(
-        spectrum, tables, own, other, pilot_offsets, places, syms if paired else 0, scale
+        spectrum, tables, own, other, pilot_offsets, syms if paired else 0, scale
     )
     if paired:
-        return doppler_paired(got, places, syms, subs)
+        return doppler_paired(got, syms, subs)
     own = jnp.transpose(got[0], (2, 1, 4, 0, 3, 5))
     own = own.reshape(2, channels + short, symbols, GUARD_SAMPLES)[:, :channels]
     return doppler_plain(own, symbols * syms)

time: 32.6 us -> 32 us (0.982)
  Pallas kernels: 9.47 us -> 8.92 us
    pallas_call x1, Pallas kernels: 1.03 us -> 0.49 us  [doppler_paired(): pl.pallas_call(doppler_kernel, in_specs=[IN_VMEM] * syms, out_specs=IN_VM...]
  transfers between devices with their start and end apart: 4 -> 4, of which waited for: 3 -> 3; matrix products, arithmetic and copies ran while one was open for 0% -> 0% of each run, Pallas kernels for 13% -> 14%
where the time goes in v7:
time: 32 us; the launch traced here: 31.8 us
  blocking collectives  11 us (34%)
  Pallas kernels  8.92 us (28%)
  starting transfers between devices  7.42 us (23%)
  waiting for transfers between devices  4.3 us (13%)
    all_to_all x1, blocking collectives, doppler_paired(): coded = lax.all_to_all(coded, ('sym', 'sub'), split_axis=0, concat_axis=0)  11 us
    ppermute x3, starting transfers between devices, doppler_paired(): lax.ppermute(pieces[d], 'sym', [(i, i ^ d) for i in range(syms)])  4.45 us
    pallas_call x1, Pallas kernels, spectra(): pl.pallas_call(spectrum_kernel, in_specs=[IN_HBM] * 3, out_specs=[IN_VMEM...  4.32 us
    ppermute x3, waiting for transfers between devices, doppler_paired(): lax.ppermute(pieces[d], 'sym', [(i, i ^ d) for i in range(syms)])  4.3 us
    pallas_call x1, Pallas kernels, profiles(): pl.pallas_call(functools.partial(profile_kernel, syms, scale), in_specs=[...  3.28 us
    ppermute x1, starting transfers between devices, local(): other = lax.ppermute(own, 'sub', [(0, 1), (1, 0)])  2.97 us
    pallas_call x1, Pallas kernels, doppler_paired(): pl.pallas_call(join_kernel, in_specs=[IN_VMEM], out_specs=IN_VMEM, out_sh...  0.83 us
  transfers between devices with their start and end apart: 4, of which 3 were waited for; matrix products, arithmetic and copies ran while one was open for 0% of the time, Pallas kernels for 14%

profile of v7, /device:TPU:0, one launch (start us, length us, event | category | flops | bytes accessed | tf_op | source)
XLA Modules:
  0.0 31.8 jit_solution(3094533175857886719)
XLA Ops:
  0.0 3.0 %collective-permute-start = (s32[6,2048]{1,0:T(8,128)}, s32[6,2048]{1,0:T(8,128)S(1)}, u32[]{:S(2)}, u32[]{:S(2)}) collective-permute-start(s32[6,2048]{1,0:T(8,128)} %own_ref.1), channel_id=1, source_target_pairs={{0,1},{1,0},{2,3},{3,2},{4,5},{5,4},{6,7},{7,6},{8,9},{9,8},{10,11... | collective-permute-start | bytes 147464 | tf_op jit(solution)/shard_map/ppermute | solution.py:552
  3.0 0.0 copy-start
  3.0 0.0 copy-start.1
  3.0 0.0 copy-start.2
  3.0 0.0 copy-start.4
  3.0 0.0 copy-start.5
  3.0 4.3 %spectra.1 = (f32[6,1,256,256]{3,2,1,0:T(8,128)S(1)}, f32[6,4,32,128]{3,2,1,0:T(8,128)S(1)}) custom-call(s32[6]{0:T(128)} %off_hbm.1, s32[6]{0:T(128)} %pilot_ref.1, f32[2,6,8,9216]{3,2,1,0:T(8,128)} %bitcast.2), custom_call_target="tpu_custom_call" | custom-call | flops 2000000000 | bytes 8000000 | tf_op jit(solution)/shard_map/spectra/pallas_call | solution.py:446
  7.3 0.0 collective-permute-done.other_ref
  7.3 0.0 copy-done
  7.4 0.0 copy-done.1
  7.4 0.0 copy-done.2
  7.4 0.0 copy-done.3
  7.4 0.0 copy-done.4
  7.4 0.0 copy-done.5
  7.4 3.3 %profiles.1 = (f32[6,2,2,8,128]{4,3,2,1,0:T(8,128)S(1)}, s16[13,16,128]{2,1,0:T(8,128)(2,1)S(1)}, s16[13,16,128]{2,1,0:T(8,128)(2,1)S(1)}, s16[13,16,128]{2,1,0:T(8,128)(2,1)S(1)}) custom-call(s32[6]{0:T(128)S(1)} %copy-done.1, f32[6,1,256,256]{3,2,1,0:T(8,128)S(1)} %get-tuple-element.11.s_ref, f32[6,4,32,128]{3,2,1,0:T(8,128)S(1)} %get-tuple-element.12.table_ref, ...), custom_call_target="tpu_custom_call" | custom-call | flops 1000000000 | bytes 4000000 | tf_op jit(solution)/shard_map/profiles/pallas_call | solution.py:483
  10.7 3.7 %collective-permute-start.1 = (s16[13,16,128]{2,1,0:T(8,128)(2,1)S(1)}, s16[13,16,128]{2,1,0:T(8,128)(2,1)S(1)}, u32[]{:S(2)}, u32[]{:S(2)}) collective-permute-start(s16[13,16,128]{2,1,0:T(8,128)(2,1)S(1)} %get-tuple-element.14), channel_id=1, source_target_pairs={{0,6},{2,4},{4,2},{6,0},{1,7},{3,5},{5,3},{7,1},{8,14},{10,12},{12... | collective-permute-start | bytes 159752 | tf_op jit(solution)/shard_map/ppermute | solution.py:518
  14.4 0.0 collective-permute-start.2
  14.4 0.8 %collective-permute-start.3 = (s16[13,16,128]{2,1,0:T(8,128)(2,1)S(1)}, s16[13,16,128]{2,1,0:T(8,128)(2,1)S(1)}, u32[]{:S(2)}, u32[]{:S(2)}) collective-permute-start(s16[13,16,128]{2,1,0:T(8,128)(2,1)S(1)} %get-tuple-element.16), channel_id=1, source_target_pairs={{0,4},{2,6},{4,0},{6,2},{1,5},{3,7},{5,1},{7,3},{8,12},{10,14},{12... | collective-permute-start | bytes 159752 | tf_op jit(solution)/shard_map/ppermute | solution.py:518
  15.1 1.6 %collective-permute-done.1.refs_0_ = s16[13,16,128]{2,1,0:T(8,128)(2,1)S(1)} collective-permute-done((s16[13,16,128]{2,1,0:T(8,128)(2,1)S(1)}, s16[13,16,128]{2,1,0:T(8,128)(2,1)S(1)}, u32[]{:S(2)}, u32[]{:S(2)}) %collective-permute-start.1) | collective-permute-done | bytes 53280 | tf_op jit(solution)/shard_map/ppermute | solution.py:518
  16.7 1.7 %collective-permute-done.2.refs_1_ = s16[13,16,128]{2,1,0:T(8,128)(2,1)S(1)} collective-permute-done((s16[13,16,128]{2,1,0:T(8,128)(2,1)S(1)}, s16[13,16,128]{2,1,0:T(8,128)(2,1)S(1)}, u32[]{:S(2)}, u32[]{:S(2)}) %collective-permute-start.2) | collective-permute-done | bytes 53280 | tf_op jit(solution)/shard_map/ppermute | solution.py:518
  18.5 1.0 %collective-permute-done.3.refs_2_ = s16[13,16,128]{2,1,0:T(8,128)(2,1)S(1)} collective-permute-done((s16[13,16,128]{2,1,0:T(8,128)(2,1)S(1)}, s16[13,16,128]{2,1,0:T(8,128)(2,1)S(1)}, u32[]{:S(2)}, u32[]{:S(2)}) %collective-permute-start.3) | collective-permute-done | bytes 53280 | tf_op jit(solution)/shard_map/ppermute | solution.py:518
  19.4 0.5 %doppler.1 = s16[8,7,16,128]{3,2,1,0:T(8,128)(2,1)S(1)} custom-call(f32[6,2,2,8,128]{4,3,2,1,0:T(8,128)S(1)} %get-tuple-element.13.own_ref, s16[13,16,128]{2,1,0:T(8,128)(2,1)S(1)} %collective-permute-done.1.refs_0_, s16[13,16,128]{2,1,0:T(8,128)(2,1)S(1)} %collective-permute-done.2.refs_1_, s16[13,16,128]{2,1,0:T(8,128)(2,1)S(1)} %collective-permute-done.3.refs_2_), custom_call_target="tpu_custom_call" | custom-call | tf_op jit(solution)/shard_map/doppler/pallas_call | solution.py:521
  19.9 11.0 %all_to_all.5.piece_ref = s16[8,7,16,128]{3,2,1,0:T(8,128)(2,1)S(1)} all-to-all(s16[8,7,16,128]{3,2,1,0:T(8,128)(2,1)S(1)} %doppler.1), channel_id=1, replica_groups=mesh['chan'=4,'sym'=4,'sub'=2] {'sym','sub'}, dimensions={0} | all-to-all | bytes 458752 | tf_op jit(solution)/shard_map/all_to_all | solution.py:533
  31.0 0.8 %join.1 = f32[2,6,16,512]{3,2,1,0:T(8,128)} custom-call(s16[8,7,16,128]{3,2,1,0:T(8,128)(2,1)S(1)} %all_to_all.5.piece_ref), custom_call_target="tpu_custom_call" | custom-call | tf_op jit(solution)/shard_map/join/pallas_call | solution.py:534
  (1 shorter events, 0.0 us)
Async XLA Ops:
  0.0 7.3 %collective-permute-start = (s32[6,2048]{1,0:T(8,128)}, s32[6,2048]{1,0:T(8,128)S(1)}, u32[]{:S(2)}, u32[]{:S(2)}) collective-permute-start(s32[6,2048]{1,0:T(8,128)} %own_ref.1), channel_id=1, source_target_pairs={{0,1},{1,0},{2,3},{3,2},{4,5},{5,4},{6,7},{7,6},{8,9},{9,8},{10,11... | collective-permute-start | bytes 147464 | tf_op jit(solution)/shard_map/ppermute | solution.py:552
  3.0 4.4 %copy-start = (s32[6,2048]{1,0:T(8,128)S(1)}, s32[6,2048]{1,0:T(8,128)}, u32[]{:S(2)}) copy-start(s32[6,2048]{1,0:T(8,128)} %own_ref.1) | copy-start | bytes 147460
  3.0 4.4 %copy-start.1 = (s32[6]{0:T(128)S(1)}, s32[6]{0:T(128)}, u32[]{:S(2)}) copy-start(s32[6]{0:T(128)} %pilot_ref.1) | copy-start | bytes 76
  3.0 4.4 %copy-start.2 = (bf16[256,256]{1,0:T(8,128)(2,1)S(1)}, bf16[256,256]{1,0:T(8,128)(2,1)}, u32[]{:S(2)}) copy-start(bf16[256,256]{1,0:T(8,128)(2,1)} %constant.10.clone.low_ref) | copy-start | bytes 393220
  3.0 4.4 %copy-start.3 = (bf16[256,256]{1,0:T(8,128)(2,1)S(1)}, bf16[256,256]{1,0:T(8,128)(2,1)}, u32[]{:S(2)}) copy-start(bf16[256,256]{1,0:T(8,128)(2,1)} %constant.9.clone.high_ref) | copy-start | bytes 393220
  3.0 4.4 %copy-start.4 = (f32[2,32,128]{2,1,0:T(8,128)S(1)}, f32[2,32,128]{2,1,0:T(8,128)}, u32[]{:S(2)}) copy-start(f32[2,32,128]{2,1,0:T(8,128)} %constant.11.clone.twist_ref) | copy-start | bytes 98308
  3.0 4.4 %copy-start.5 = (bf16[32,512]{1,0:T(8,128)(2,1)S(1)}, bf16[32,512]{1,0:T(8,128)(2,1)}, u32[]{:S(2)}) copy-start(bf16[32,512]{1,0:T(8,128)(2,1)} %constant.8.clone.spot_ref) | copy-start | bytes 98308
  10.7 6.0 %collective-permute-start.1 = (s16[13,16,128]{2,1,0:T(8,128)(2,1)S(1)}, s16[13,16,128]{2,1,0:T(8,128)(2,1)S(1)}, u32[]{:S(2)}, u32[]{:S(2)}) collective-permute-start(s16[13,16,128]{2,1,0:T(8,128)(2,1)S(1)} %get-tuple-element.14), channel_id=1, source_target_pairs={{0,6},{2,4},{4,2},{6,0},{1,7},{3,5},{5,3},{7,1},{8,14},{10,12},{12... | collective-permute-start | bytes 159752 | tf_op jit(solution)/shard_map/ppermute | solution.py:518
  14.4 4.1 %collective-permute-start.2 = (s16[13,16,128]{2,1,0:T(8,128)(2,1)S(1)}, s16[13,16,128]{2,1,0:T(8,128)(2,1)S(1)}, u32[]{:S(2)}, u32[]{:S(2)}) collective-permute-start(s16[13,16,128]{2,1,0:T(8,128)(2,1)S(1)} %get-tuple-element.15), channel_id=1, source_target_pairs={{0,2},{2,0},{4,6},{6,4},{1,3},{3,1},{5,7},{7,5},{8,10},{10,8},{12,... | collective-permute-start | bytes 159752 | tf_op jit(solution)/shard_map/ppermute | solution.py:518
  14.4 5.1 %collective-permute-start.3 = (s16[13,16,128]{2,1,0:T(8,128)(2,1)S(1)}, s16[13,16,128]{2,1,0:T(8,128)(2,1)S(1)}, u32[]{:S(2)}, u32[]{:S(2)}) collective-permute-start(s16[13,16,128]{2,1,0:T(8,128)(2,1)S(1)} %get-tuple-element.16), channel_id=1, source_target_pairs={{0,4},{2,6},{4,0},{6,2},{1,5},{3,7},{5,1},{7,3},{8,12},{10,14},{12... | collective-permute-start | bytes 159752 | tf_op jit(solution)/shard_map/ppermute | solution.py:518
